TPU v7x, 128 devices: a whole 4x4x4 slice. The times are simulated.
128 devices in a mesh: rcv: 32 (over x, y, z_lo), src: 4 (over z_hi, core).
Axes of the slice: x: 4, y: 4, z: 4 (z_hi: 2, z_lo: 2; z = z_hi * 2 + z_lo), core: 2. Of those that a mesh axis runs over, the one named last changes fastest.
Arguments:
- record: bfloat16 [12800, 8192], P(('rcv', 'src')), may hold values from -6 to 6
- quality: int32 [8192], replicated, may hold values 0 or 1
- keep_flags: int32 [32, 8192], replicated, may hold values 0 or 1
- old_stacks: bfloat16 [401, 128, 8192], P(None, 'src', 'rcv'), may hold values from -4 to 4
Outputs:
- stacks: float32 [401, 128, 8192], P(None, 'src', 'rcv')
All inputs are finite; a program needn't handle non-finite values.
Results may differ from a plain program's by a relative error of at most 0.0039.
Values may be sent and summed in bfloat16 or wider, within the bound.
No kernel may reach another device: no remote copies, remote signals or barrier semaphores. Data moves between devices by JAX's collectives and lax.ppermute only.
A program may use at most 192 MiB of HBM per device.

v0:
```python
import math

import jax
import jax.numpy as jnp
from jax import lax
from jax.sharding import PartitionSpec as P

WIN = 400
NFFT = 800
BINS = 401
LARGEST_LAG = 200
LAGS = 401
HALFBAND = 32
SUB = 32


EPSILON = 1e-06


def spread(value, axis, source):
    kept = jnp.where(lax.axis_index(axis) == source, value, 0).astype(value.dtype)
    return lax.psum(kept, axis)


def forward_table():
    sample_ids = jnp.arange(WIN, dtype=jnp.int32)[:, None]
    bin_ids = jnp.arange(BINS, dtype=jnp.int32)[None, :]
    phases = (sample_ids * bin_ids % NFFT).astype(jnp.float32) * (2.0 * math.pi / NFFT)
    return jnp.concatenate([jnp.cos(phases), -jnp.sin(phases)], axis=1)


def band_table():
    bin_rows = jnp.arange(BINS, dtype=jnp.int32)[:, None]
    bin_cols = jnp.arange(BINS, dtype=jnp.int32)[None, :]
    inside = (jnp.abs(bin_rows - bin_cols) <= HALFBAND).astype(jnp.float32)
    counts = jnp.sum(inside, axis=1, keepdims=True)
    return inside / (2.0 * counts)


def lag_table():
    lag_ids = jnp.arange(LAGS, dtype=jnp.int32)[:, None] - LARGEST_LAG
    bin_ids = jnp.arange(BINS, dtype=jnp.int32)[None, :]
    phases = (lag_ids * bin_ids % NFFT).astype(jnp.float32) * (2.0 * math.pi / NFFT)
    edges = jnp.logical_or(bin_ids == 0, bin_ids == NFFT // 2)
    weights = jnp.where(edges, 1.0, 2.0).astype(jnp.float32) / math.sqrt(NFFT)
    return jnp.concatenate([weights * jnp.cos(phases), -weights * jnp.sin(phases)], axis=1).astype(
        jnp.bfloat16
    )


def whiten(samples, channel_flags):
    channels = samples.shape[1]
    segment = samples.astype(jnp.float32).reshape(SUB, WIN, channels)
    segment = segment - jnp.mean(segment, axis=1, keepdims=True)
    spectrum = jnp.einsum("swc,wg->sgc", segment, forward_table(), precision=lax.Precision.HIGHEST)
    real_part = spectrum[:, :BINS]
    imag_part = spectrum[:, BINS:]
    power_sum = real_part * real_part + imag_part * imag_part
    smooth = jnp.einsum("fg,sgc->sfc", band_table(), power_sum, precision=lax.Precision.HIGHEST)
    inverse_amp = channel_flags[:, None, :] / jnp.sqrt(smooth + EPSILON)
    return jnp.concatenate([real_part * inverse_amp, imag_part * inverse_amp], axis=1).astype(
        jnp.bfloat16
    )


def stack_update(sources, receivers, keep_src, keep_rcv, old_block):
    src_real = sources[:, :BINS]
    src_imag = sources[:, BINS:]
    rcv_real = receivers[:, :BINS]
    rcv_imag = receivers[:, BINS:]

    def product(left_operand, right_operand):
        return jnp.einsum(
            "gxy,gxa->xya", left_operand, right_operand, preferred_element_type=jnp.float32
        )

    cross_real = product(src_real, rcv_real) + product(src_imag, rcv_imag)
    cross_imag = product(src_real, rcv_imag) - product(src_imag, rcv_real)
    cross_spec = jnp.concatenate([cross_real, cross_imag], axis=0).astype(jnp.bfloat16)
    src_width = cross_spec.shape[1]
    rcv_width = cross_spec.shape[2]
    lagged = jnp.dot(
        lag_table(),
        cross_spec.reshape(2 * BINS, src_width * rcv_width),
        preferred_element_type=jnp.float32,
    )
    lagged = lagged.reshape(LAGS, src_width, rcv_width)
    station_pair_count = jnp.dot(keep_src.T, keep_rcv, preferred_element_type=jnp.float32)
    return old_block.astype(jnp.float32) + lagged / jnp.maximum(station_pair_count, 1.0)[None]


def on_device(record, quality, keep_flags, old_stacks):
    src_count = lax.axis_size("src")
    row_index = lax.axis_index("rcv")
    col_index = lax.axis_index("src")
    keep_all = keep_flags.astype(jnp.float32)
    channel_flags = keep_all * quality.astype(jnp.float32)[None, :]
    src_width = old_stacks.shape[1]
    rcv_width = old_stacks.shape[2]
    local_width = rcv_width // src_count
    owned_rows = lax.all_to_all(record, ("rcv", "src"), split_axis=1, concat_axis=0, tiled=True)
    offset = (row_index * src_count + col_index) * local_width
    own_spec = whiten(owned_rows, lax.dynamic_slice_in_dim(channel_flags, offset, local_width, 1))
    receivers = lax.all_gather(own_spec, "src", axis=2, tiled=True)
    source_piece = lax.dynamic_slice_in_dim(receivers, col_index * src_width, src_width, 2)
    sources = spread(source_piece, "rcv", 0)
    keep_src = lax.dynamic_slice_in_dim(keep_all, col_index * src_width, src_width, 1)
    keep_rcv = lax.dynamic_slice_in_dim(keep_all, row_index * rcv_width, rcv_width, 1)
    return stack_update(sources, receivers, keep_src, keep_rcv, old_stacks)


def solution(mesh):
    return jax.shard_map(
        on_device,
        mesh=mesh,
        in_specs=(P(("rcv", "src"), None), P(), P(), P(None, "src", "rcv")),
        out_specs=P(None, "src", "rcv"),
        check_vma=False,
    )
```

profile of v0, /device:TPU:0, one launch (start us, length us, event | category | flops | bytes accessed | tf_op | source)
XLA Modules:
  0.0 630.1 jit_solution(8645508476912494209)
XLA Ops:
  6.5 4.0 copy.45
  10.6 11.1 %all-to-all-start = ((bf16[100,128,64]{0,2,1:T(8,128)(2,1)}), bf16[100,128,64]{0,2,1:T(8,128)(2,1)S(1)}, u32[]{:S(2)}, u32[]{:S(2)}) async-start(bf16[100,128,64]{0,2,1:T(8,128)(2,1)} %bitcast.63), calls=%async_computation | async-start | bytes 4194304 | tf_op jit(solution)/shard_map/all_to_all | solution.py:101
  21.7 0.0 all-gather.2.cloned.1.call-start
  21.8 1.1 convert_element_type.51
  22.9 0.1 dynamic-slice
  23.0 0.2 convert_reduce_fusion.1
  23.1 4.1 sine_negate_fusion
  27.2 0.8 dynamic-slice_multiply_fusion
  28.0 24.3 %all-to-all-done = bf16[100,128,64]{0,2,1:T(8,128)(2,1)S(1)} async-done(((bf16[100,128,64]{0,2,1:T(8,128)(2,1)}), bf16[100,128,64]{0,2,1:T(8,128)(2,1)S(1)}, u32[]{:S(2)}, u32[]{:S(2)}) %all-to-all-start) | async-done | bytes 1638432 | tf_op jit(solution)/shard_map/all_to_all | solution.py:101
  52.3 1.2 convert_reduce_fusion
  53.6 0.1 copy.48
  53.6 0.5 convert_bitcast_fusion
  54.1 4.5 copy.46
  58.5 5.3 reshape.49
  63.8 2.6 broadcast_subtract_fusion
  66.5 2.4 copy.49
  68.9 15.2 %fusion.12 = f32[802,2048]{0,1:S(1)} fusion(f32[400,2048]{0,1:T(8,128)S(1)} %bitcast.61, f32[400,401]{1,0:T(8,128)S(1)} %get-tuple-element.13, f32[400,401]{1,0:T(8,128)S(1)} %copy-done.1), kind=kOutput, calls=%fused_computation.23 | convolution fusion | flops 7884301312 | bytes 11129984
  84.1 8.4 %fusion.4 = (bf16[32,401,64]{1,2,0:T(8,128)(2,1)S(1)}, bf16[32,401,64]{1,2,0:T(8,128)(2,1)S(1)}) fusion(f32[32,802,64]{1,2,0:T(8,128)S(1)} %bitcast.62, f32[32,64]{1,0:T(8,128)S(1)} %dynamic-slice_multiply_fusion, f32[401]{0:T(512)S(1)} %broadcast_multiply_fusion.1), kind=kOutput, calls=%fused_computation.11 | convolution fusion | flops 3960040704 | bytes 20080640 | tf_op jit(solution)/shard_map/fg,sgc->sfc/dot_general | solution.py:59
  92.5 3.2 pad_maximum_fusion.1
  95.7 0.0 all-gather.2.cloned.1.call-update
  95.7 0.0 all-reduce.2.cloned.1.call-start
  95.8 1.1 convolution_maximum_fusion
  96.9 92.2 %all-gather.2.cloned.1.call-done = bf16[32,802,256]{1,2,0:T(8,128)(2,1)} async-done(((bf16[32,802,64]{1,2,0:T(8,128)(2,1)}), bf16[32,802,256]{1,2,0:T(8,128)(2,1)}) %all-gather.2.cloned.1.call-update) | async-done | bytes 13139984 | tf_op jit(solution)/shard_map/all_gather | solution.py:104
  189.0 3.1 dynamic-slice_select_fusion
  192.1 0.0 all-reduce.2.cloned.1.call-update
  192.1 4.5 multiply_convert_fusion.1
  196.7 13.0 %fusion.41 = (bf16[32,401,256]{1,2,0:T(8,128)(2,1)}, bf16[32,401,256]{1,2,0:T(8,128)(2,1)}) fusion(bf16[32,802,256]{1,2,0:T(8,128)(2,1)} %all-gather.2.cloned.1.call-done), kind=kLoop, calls=%fused_computation.70 | loop fusion | bytes 26279936 | tf_op jit(solution)/shard_map/slice | solution.py:69
  209.7 14.3 %copy.51 = bf16[32,401,256]{2,0,1:T(8,128)(2,1)} copy(bf16[32,401,256]{1,2,0:T(8,128)(2,1)} %get-tuple-element.5) | data formatting | bytes 13139968 | tf_op jit(solution)/shard_map/slice | solution.py:69
  224.0 14.3 %copy.53 = bf16[32,401,256]{2,0,1:T(8,128)(2,1)} copy(bf16[32,401,256]{1,2,0:T(8,128)(2,1)} %get-tuple-element.6) | data formatting | bytes 13139968 | tf_op jit(solution)/shard_map/slice | solution.py:70
  238.3 265.1 %all-reduce.2.cloned.1.call-done = bf16[32,802,32]{1,2,0:T(8,128)(2,1)} async-done(((bf16[32,802,32]{1,2,0:T(8,128)(2,1)}), bf16[32,802,32]{1,2,0:T(8,128)(2,1)}) %all-reduce.2.cloned.1.call-update) | async-done | bytes 1642512 | tf_op jit(solution)/shard_map/psum | solution.py:22
  503.3 2.1 fusion.42
  505.5 3.9 copy.52
  509.4 4.1 copy.50
  513.5 0.0 slice-start.3
  513.6 10.8 %fusion.44 = f32[401,32,256]{2,1,0:T(8,128)} fusion(bf16[32,401,32]{0,2,1:T(8,128)(2,1)} %copy.50, bf16[32,401,256]{2,0,1:T(8,128)(2,1)} %copy.53), kind=kOutput, calls=%fused_computation.73 | convolution fusion | flops 210239488 | bytes 20531200 | tf_op jit(solution)/shard_map/gxy,gxa->xya/dot_general | solution.py:73
  524.4 6.6 %fusion.43 = f32[401,32,256]{2,1,0:T(8,128)} fusion(bf16[32,401,32]{0,2,1:T(8,128)(2,1)S(1)} %copy-done, bf16[32,401,256]{2,0,1:T(8,128)(2,1)S(1)} %bitcast.52), kind=kOutput, calls=%fused_computation.72 | convolution fusion | flops 210239488 | bytes 20531200 | tf_op jit(solution)/shard_map/gxy,gxa->xya/dot_general | solution.py:73
  531.0 10.3 %subtract_convert_fusion = bf16[401,32,256]{2,1,0:T(8,128)(2,1)} fusion(f32[401,32,256]{2,1,0:T(8,128)} %fusion.44, bf16[32,401,32]{0,2,1:T(8,128)(2,1)} %copy.52, bf16[32,401,256]{2,0,1:T(8,128)(2,1)S(1)} %bitcast.52), kind=kOutput, calls=%fused_computation.5 | convolution fusion | flops 216809472 | bytes 27101184 | tf_op jit(solution)/shard_map/gxy,gxa->xya/dot_general | solution.py:73
  541.3 3.8 pad.9
  545.1 11.0 %copy.62 = bf16[51,8,32,256]{3,1,2,0:T(8,128)(2,1)} copy(bf16[51,8,32,256]{3,2,1,0:T(8,128)(2,1)S(1)} %bitcast.60) | data formatting | bytes 13369344
  556.1 10.5 %add_convert_fusion = bf16[401,32,256]{2,1,0:T(8,128)(2,1)} fusion(f32[401,32,256]{2,1,0:T(8,128)} %fusion.43, bf16[32,401,32]{0,2,1:T(8,128)(2,1)} %copy.52, bf16[32,401,256]{2,0,1:T(8,128)(2,1)S(1)} %bitcast.50), kind=kOutput, calls=%fused_computation.6 | convolution fusion | flops 216809472 | bytes 27101184 | tf_op jit(solution)/shard_map/gxy,gxa->xya/dot_general | solution.py:73
  566.6 3.8 pad.8
  570.4 0.0 slice-start.5
  570.4 11.1 %copy.61 = bf16[51,8,32,256]{3,1,2,0:T(8,128)(2,1)} copy(bf16[51,8,32,256]{3,2,1,0:T(8,128)(2,1)S(1)} %bitcast.58) | data formatting | bytes 13369344
  581.5 6.6 %pad_maximum_fusion = bf16[802,8192]{1,0:T(8,128)(2,1)S(1)} fusion(bf16[401,8192]{1,0:T(8,128)(2,1)S(1)} %bitcast.57, bf16[401,8192]{1,0:T(8,128)(2,1)} %bitcast.59), kind=kLoop, calls=%fused_computation.1 | loop fusion | flops 26279936 | bytes 26279936 | tf_op jit(solution)/shard_map/concatenate | solution.py:79
  588.2 3.4 copy.63
  591.6 1.2 slice_bitcast_fusion
  592.8 16.2 %divide_add_fusion = f32[401,32,256]{2,0,1:T(8,128)} fusion(bf16[32,256,802]{1,0,2:T(8,128)(2,1)S(1)} %slice_bitcast_fusion, bf16[401,32,256]{2,1,0:T(8,128)(2,1)} %param.7, f32[32,256]{1,0:T(8,128)S(1)} %convolution_maximum_fusion, bf16[401,401]{1,0:T(8,128)(2,1)S(1)} %copy-done.4, bf16[401,401]{1,0:T(8,128)(2,1)S(1)} %copy-done.3), kind=kOutput, calls=%fused_computation | convolution fusion | flops 5280268800 | bytes 33525892 | tf_op jit(solution)/shard_map/dot_general | solution.py:82
  609.1 14.0 %copy.59 = f32[401,32,256]{2,1,0:T(8,128)} copy(f32[401,32,256]{2,0,1:T(8,128)} %divide_add_fusion) | data formatting | bytes 26279936 | tf_op jit(solution)/shard_map/add | solution.py:89
  (31 shorter events, 0.1 us)
Async XLA Ops:
  6.5 15.2 %copy-start.5 = (s32[8192]{0:T(1024)S(1)}, s32[8192]{0:T(1024)}, u32[]{:S(2)}) copy-start(s32[8192]{0:T(1024)} %param.5) | copy-start | bytes 98308
  6.5 15.3 %copy-start.2 = (s32[32,8192]{1,0:T(8,128)S(1)}, s32[32,8192]{1,0:T(8,128)}, u32[]{:S(2)}) copy-start(s32[32,8192]{1,0:T(8,128)} %param.6) | copy-start | bytes 3145732
  10.6 41.8 %all-to-all-start = ((bf16[100,128,64]{0,2,1:T(8,128)(2,1)}), bf16[100,128,64]{0,2,1:T(8,128)(2,1)S(1)}, u32[]{:S(2)}, u32[]{:S(2)}) async-start(bf16[100,128,64]{0,2,1:T(8,128)(2,1)} %bitcast.63), calls=%async_computation | async-start | bytes 4194304 | tf_op jit(solution)/shard_map/all_to_all | solution.py:101
  21.7 167.3 %all-gather.2.cloned.1.call-start = ((), (), s32[]{:S(2)}) async-start(), calls=%async_computation.1 | async-start | bytes 18350080 | tf_op jit(solution)/shard_map/all_gather | solution.py:104
  63.8 5.1 copy-start.1
  95.7 407.6 %all-reduce.2.cloned.1.call-start = ((), (), s32[]{:S(2)}) async-start(), calls=%async_computation.2 | async-start | bytes 3670016 | tf_op jit(solution)/shard_map/psum | solution.py:22
  509.4 15.0 %slice-start.2 = ((s8[6569984]{0:T(1024)(128)(4,1)}), s8[2375680]{0:T(1024)(128)(4,1)S(1)}, s32[]{:S(2)}) async-start(s8[6569984]{0:T(1024)(128)(4,1)} %bitcast.51), calls=%async_computation.5 | async-start | bytes 4751360
  513.5 10.8 %slice-start.3 = ((s8[6569984]{0:T(1024)(128)(4,1)}), s8[4194304]{0:T(1024)(128)(4,1)S(1)}, s32[]{:S(2)}) async-start(s8[6569984]{0:T(1024)(128)(4,1)} %bitcast.51), calls=%async_computation.6 | async-start | bytes 8388608
  513.6 10.8 %copy-start = (bf16[32,401,32]{0,2,1:T(8,128)(2,1)S(1)}, bf16[32,401,32]{0,2,1:T(8,128)(2,1)}, u32[]{:S(2)}) copy-start(bf16[32,401,32]{0,2,1:T(8,128)(2,1)} %copy.50) | copy-start | bytes 2463748
  541.3 14.8 %slice-start = ((s8[6569984]{0:T(1024)(128)(4,1)}), s8[4194304]{0:T(1024)(128)(4,1)S(1)}, s32[]{:S(2)}) async-start(s8[6569984]{0:T(1024)(128)(4,1)} %bitcast.49), calls=%async_computation.3 | async-start | bytes 8388608
  545.0 11.0 %slice-start.1 = ((s8[6569984]{0:T(1024)(128)(4,1)}), s8[2375680]{0:T(1024)(128)(4,1)S(1)}, s32[]{:S(2)}) async-start(s8[6569984]{0:T(1024)(128)(4,1)} %bitcast.49), calls=%async_computation.4 | async-start | bytes 4751360
  566.6 15.0 %slice-start.4 = ((s8[6684672]{0:T(1024)(128)(4,1)}), s8[4194304]{0:T(1024)(128)(4,1)S(1)}, s32[]{:S(2)}) async-start(s8[6684672]{0:T(1024)(128)(4,1)} %bitcast.55), calls=%async_computation.7 | async-start | bytes 8388608
  570.4 11.2 %slice-start.5 = ((s8[6684672]{0:T(1024)(128)(4,1)}), s8[2490368]{0:T(1024)(128)(4,1)S(1)}, s32[]{:S(2)}) async-start(s8[6684672]{0:T(1024)(128)(4,1)} %bitcast.55), calls=%async_computation.8 | async-start | bytes 4980736
  591.5 1.3 copy-start.3
  591.5 1.3 copy-start.4
Sparse Core Ops, SparseCore 0:
  95.8 93.1 all-gather.1
  192.2 311.0 all-reduce.1
where the time goes:
time: 642 us; the launch traced here: 630 us
  waiting for transfers between devices  382 us (60%)
  local copies, waits for them, and re-layouts  116 us (18%)
  matrix products  79.1 us (12%)
  other arithmetic  27.8 us (4%)
  between operations  13.9 us (2%)
  starting transfers between devices  11.2 us (2%)
    psum x1, waiting for transfers between devices, spread(): return lax.psum(kept, axis)  265 us
    all_gather x1, waiting for transfers between devices, on_device(): receivers = lax.all_gather(own_spec, 'src', axis=2, tiled=True)  92.2 us
    dot_general x4, matrix products, product(): jnp.einsum('gxy,gxa->xya', left_operand, right_operand, preferred_element...  38.2 us
    unnamed x30, local copies, waits for them, and re-layouts  37.1 us
    slice x2, local copies, waits for them, and re-layouts, stack_update(): rcv_real = receivers[:, :BINS]  27.3 us
    all_to_all x1, waiting for transfers between devices, on_device(): lax.all_to_all(record, ('rcv', 'src'), split_axis=1, concat_axis=0, tiled...  24.3 us
    dot_general x1, matrix products, stack_update(): jnp.dot(lag_table(), cross_spec.reshape(2 * BINS, src_width * rcv_width),...  16.2 us
    unnamed x1, matrix products  15.2 us
  transfers between devices with their start and end apart: 3, of which 3 were waited for; matrix products, arithmetic and copies ran while one was open for 8% of the time, Pallas kernels for 0%

commit v1 on v0

v1 whole, which is shorter than its diff:
```python
import functools
import math

import jax
import jax.numpy as jnp
import numpy as np
from jax import lax
from jax.experimental import pallas as pl
from jax.experimental.pallas import tpu as pltpu
from jax.sharding import PartitionSpec as P

WIN = 400
NFFT = 800
BINS = 401
LARGEST_LAG = 200
LAGS = 401
HALFBAND = 32
SUB = 32
EPSILON = 1e-06

PIECE = WIN // 4
PADDED = 112
DEPTH = 4 * PADDED
FREQ = 416
HALF = 128
SRC = 64
OWN = 32
SHIFTS = 208
PITCH = 72
ROWS = 2 * SRC
XPITCH = ROWS + 8
BLOCK = 16
VMEM = 56 * 1024 * 1024


def split(table):
    high = table.astype(jnp.bfloat16)
    low = (table - high.astype(np.float32)).astype(jnp.bfloat16)
    return high, low


def forward_table():
    samples = np.arange(WIN)[None, :]
    bins = np.arange(BINS)[:, None]
    phases = (samples * bins % NFFT) * (2.0 * math.pi / NFFT)
    table = np.zeros((2, FREQ, 4, PADDED), np.float32)
    table[0, :BINS, :, :PIECE] = np.cos(phases).reshape(BINS, 4, PIECE)
    table[1, :BINS, :, :PIECE] = -np.sin(phases).reshape(BINS, 4, PIECE)
    high, low = split(table.reshape(2 * FREQ, DEPTH))
    sums = (high.astype(np.float64) + low.astype(np.float64)).sum(axis=1, keepdims=True)
    return high, low, np.broadcast_to((sums / WIN).astype(np.float32), (2 * FREQ, HALF)).copy()


def band_table():
    bins = np.arange(FREQ)
    inside = np.abs(bins[:, None] - bins[None, :]) <= HALFBAND
    inside &= (bins[:, None] < BINS) & (bins[None, :] < BINS)
    counts = np.maximum(inside.sum(axis=1, keepdims=True), 1)
    inverse = np.broadcast_to((1.0 / (2.0 * counts)).astype(np.float32), (FREQ, HALF)).copy()
    return inside.astype(jnp.bfloat16), inverse


def lag_tables():
    shifts = np.arange(LARGEST_LAG + 1)[:, None]
    bins = np.arange(BINS)[None, :]
    phases = (shifts * bins % NFFT) * (2.0 * math.pi / NFFT)
    weights = np.where((bins == 0) | (bins == NFFT // 2), 1.0, 2.0) / math.sqrt(NFFT)
    tables = np.zeros((2, SHIFTS, FREQ), np.float32)
    tables[0, : LARGEST_LAG + 1, :BINS] = weights * np.cos(phases)
    tables[1, : LARGEST_LAG + 1, :BINS] = -weights * np.sin(phases)
    return tables.astype(jnp.bfloat16)


def dot(a, b):
    return jnp.dot(a, b, preferred_element_type=jnp.float32)


def whiten_pair(x_ref, flag_ref, high_ref, low_ref, sums_ref, band_ref, inverse_ref, spec):
    x = jnp.concatenate([x_ref[0], x_ref[1]], axis=1)
    spec[...] = dot(high_ref[...], x) + dot(low_ref[...], x)
    total = spec[0:1, :]
    sums = sums_ref[...]
    sums = jnp.concatenate([sums, sums], axis=1)
    real = spec[:FREQ] - sums[:FREQ] * total
    imag = spec[FREQ:] - sums[FREQ:] * total
    power = real * real + imag * imag
    power_high = power.astype(jnp.bfloat16)
    power_low = (power - power_high.astype(jnp.float32)).astype(jnp.bfloat16)
    band = band_ref[...]
    smooth = dot(band, power_high) + dot(band, power_low)
    inverse = inverse_ref[...]
    inverse = jnp.concatenate([inverse, inverse], axis=1)
    flags = jnp.concatenate([flag_ref[0], flag_ref[1]], axis=1)
    scale = flags * lax.rsqrt(smooth * inverse + EPSILON)
    return real * scale, imag * scale


def whiten_sources_kernel(x_ref, flag_ref, high_ref, low_ref, sums_ref, band_ref, inverse_ref, out_ref, spec):
    real, imag = whiten_pair(x_ref, flag_ref, high_ref, low_ref, sums_ref, band_ref, inverse_ref, spec)
    for g in range(2):
        out_ref[g, 0] = real[:, g * HALF : (g + 1) * HALF].astype(jnp.bfloat16)
        out_ref[g, 1] = imag[:, g * HALF : (g + 1) * HALF].astype(jnp.bfloat16)


def whiten_receivers_kernel(x_ref, flag_ref, high_ref, low_ref, sums_ref, band_ref, inverse_ref, out_ref, spec, held):
    step = pl.program_id(0)
    real, imag = whiten_pair(x_ref, flag_ref, high_ref, low_ref, sums_ref, band_ref, inverse_ref, spec)
    for g in range(2):
        window = 2 * step + g
        held[pl.ds(window, FREQ, stride=PITCH), :] = real[:, g * HALF : (g + 1) * HALF]
        held[pl.ds(SUB + window, FREQ, stride=PITCH), :] = imag[:, g * HALF : (g + 1) * HALF]

    @pl.when(step == pl.num_programs(0) - 1)
    def _():
        @pl.loop(0, FREQ // 8)
        def _(block):
            for i in range(8):
                f = block * 8 + i
                out_ref[f] = held[pl.ds(pl.multiple_of(f * PITCH, 8), 2 * SUB), :].astype(jnp.bfloat16)


def whole(shape):
    return pl.BlockSpec(shape, lambda *_: (0,) * len(shape))


def whiten_call(kernel, x, flags, out_shape, out_spec, scratch):
    groups = x.shape[0]
    high, low, sums = forward_table()
    band, inverse = band_table()
    return pl.pallas_call(
        kernel,
        grid=(groups // 2,),
        in_specs=[
            pl.BlockSpec((2, DEPTH, HALF), lambda g: (g, 0, 0)),
            pl.BlockSpec((2, 1, HALF), lambda g: (g, 0, 0)),
            whole(high.shape),
            whole(low.shape),
            whole(sums.shape),
            whole(band.shape),
            whole(inverse.shape),
        ],
        out_specs=out_spec,
        out_shape=out_shape,
        scratch_shapes=[pltpu.VMEM((2 * FREQ, 2 * HALF), jnp.float32)] + scratch,
        compiler_params=pltpu.CompilerParams(vmem_limit_bytes=VMEM),
        cost_estimate=pl.CostEstimate(
            flops=groups * 2 * 2 * 2 * FREQ * DEPTH * HALF, bytes_accessed=groups * DEPTH * HALF * 6, transcendentals=0
        ),
    )(x, flags, jnp.asarray(high), jnp.asarray(low), jnp.asarray(sums), jnp.asarray(band), jnp.asarray(inverse))


def whiten_receivers(x, flags):
    return whiten_call(
        whiten_receivers_kernel,
        x,
        flags,
        jax.ShapeDtypeStruct((FREQ, 2 * SUB, HALF), jnp.bfloat16),
        whole((FREQ, 2 * SUB, HALF)),
        [pltpu.VMEM((FREQ * PITCH, HALF), jnp.float32)],
    )


def whiten_sources(x, flags):
    groups = x.shape[0]
    return whiten_call(
        whiten_sources_kernel,
        x,
        flags,
        jax.ShapeDtypeStruct((groups, 2, FREQ, HALF), jnp.bfloat16),
        pl.BlockSpec((2, 2, FREQ, HALF), lambda g: (g, 0, 0, 0)),
        [],
    )


def cross_kernel(left_ref, right_ref, out_ref, held):
    zeros = jnp.zeros((2 * SUB, HALF), jnp.bfloat16)
    for pair in range(BLOCK // 2):
        first = right_ref[2 * pair]
        second = right_ref[2 * pair + 1]
        weights = jnp.concatenate(
            [jnp.concatenate([first, zeros], axis=1), jnp.concatenate([zeros, second], axis=1)], axis=0
        )
        product = dot(left_ref[pair], weights)
        held[pl.ds(2 * pair * XPITCH, ROWS), :] = product[:, :HALF]
        held[pl.ds((2 * pair + 1) * XPITCH, ROWS), :] = product[:, HALF:]
    for row in range(ROWS):
        out_ref[row] = held[pl.ds(row, BLOCK, stride=XPITCH), :].astype(jnp.bfloat16)


def cross(left, right):
    return pl.pallas_call(
        cross_kernel,
        grid=(FREQ // BLOCK,),
        in_specs=[
            pl.BlockSpec((BLOCK // 2, ROWS, 4 * SUB), lambda f: (f, 0, 0)),
            pl.BlockSpec((BLOCK, 2 * SUB, HALF), lambda f: (f, 0, 0)),
        ],
        out_specs=pl.BlockSpec((ROWS, BLOCK, HALF), lambda f: (0, f, 0)),
        out_shape=jax.ShapeDtypeStruct((ROWS, FREQ, HALF), jnp.bfloat16),
        scratch_shapes=[pltpu.VMEM((BLOCK * XPITCH, HALF), jnp.float32)],
        compiler_params=pltpu.CompilerParams(vmem_limit_bytes=VMEM),
        cost_estimate=pl.CostEstimate(flops=FREQ * ROWS * 4 * SUB * 2 * HALF, bytes_accessed=30 << 20, transcendentals=0),
    )(left, right)


def lag_sums(real_ref, imag_ref, tables_ref, even, odd):
    for pair in range(BLOCK // 2):
        real = jnp.concatenate([real_ref[2 * pair], real_ref[2 * pair + 1]], axis=1)
        imag = jnp.concatenate([imag_ref[2 * pair], imag_ref[2 * pair + 1]], axis=1)
        cosine = dot(tables_ref[0], real)
        sine = dot(tables_ref[1], imag)
        for i in range(2):
            rows = pl.ds(2 * pair + i, SHIFTS, stride=BLOCK)
            even[rows, :] = cosine[:, i * HALF : (i + 1) * HALF]
            odd[rows, :] = sine[:, i * HALF : (i + 1) * HALF]


def shift_rows(m):
    return pl.ds(pl.multiple_of(m * BLOCK, BLOCK), BLOCK)


def lag_partner_kernel(place_ref, real_ref, imag_ref, tables_ref, count_ref, out_ref, even, odd):
    lag_sums(real_ref, imag_ref, tables_ref, even, odd)

    @pl.loop(0, LARGEST_LAG + 1, unroll=3)
    def _(m):
        e, o = even[shift_rows(m), :], odd[shift_rows(m), :]
        out_ref[LARGEST_LAG + m] = ((e + o) * count_ref[...]).astype(jnp.bfloat16)
        out_ref[LARGEST_LAG - m] = ((e - o) * count_ref[...]).astype(jnp.bfloat16)


def lag_own_kernel(place_ref, real_ref, imag_ref, tables_ref, count_ref, old_ref, out_ref, even, odd):
    lag_sums(real_ref, imag_ref, tables_ref, even, odd)

    @pl.loop(0, LARGEST_LAG + 1, unroll=3)
    def _(m):
        e, o = even[shift_rows(m), :], odd[shift_rows(m), :]
        above, below = LARGEST_LAG + m, LARGEST_LAG - m
        out_ref[above] = old_ref[above].astype(jnp.float32) + (e + o) * count_ref[...]
        out_ref[below] = old_ref[below].astype(jnp.float32) + (e - o) * count_ref[...]


def lag_call(kernel, place, spectra, inverse_count, old, half):
    steps = OWN // BLOCK
    tables = lag_tables()
    in_specs = [
        pl.BlockSpec((BLOCK, FREQ, HALF), lambda g, place: (half(place) * steps + g, 0, 0)),
        pl.BlockSpec((BLOCK, FREQ, HALF), lambda g, place: (SRC // BLOCK + half(place) * steps + g, 0, 0)),
        pl.BlockSpec(tables.shape, lambda g, place: (0, 0, 0)),
        pl.BlockSpec((BLOCK, HALF), lambda g, place: (half(place) * steps + g, 0)),
    ]
    operands = [spectra, spectra, jnp.asarray(tables), inverse_count]
    if old is None:
        out_shape = jax.ShapeDtypeStruct((LAGS, OWN, HALF), jnp.bfloat16)
        out_spec = pl.BlockSpec((LAGS, BLOCK, HALF), lambda g, place: (0, g, 0))
    else:
        in_specs.append(pl.BlockSpec((LAGS, BLOCK, HALF), lambda g, place: (0, g, place[0])))
        operands.append(old)
        out_shape = jax.ShapeDtypeStruct((LAGS, OWN, 2 * HALF), jnp.float32)
        out_spec = pl.BlockSpec((LAGS, BLOCK, HALF), lambda g, place: (0, g, place[0]))
    return pl.pallas_call(
        kernel,
        grid_spec=pltpu.PrefetchScalarGridSpec(
            num_scalar_prefetch=1,
            grid=(steps,),
            in_specs=in_specs,
            out_specs=out_spec,
            scratch_shapes=[pltpu.VMEM((SHIFTS * BLOCK, HALF), jnp.float32)] * 2,
        ),
        out_shape=out_shape,
        compiler_params=pltpu.CompilerParams(vmem_limit_bytes=VMEM),
        cost_estimate=pl.CostEstimate(flops=OWN * SHIFTS * FREQ * HALF * 4, bytes_accessed=16 << 20, transcendentals=0),
    )(place, *operands)


def merge_kernel(place_ref, held_ref, got_ref, old_ref, out_ref):
    out_ref[...] = old_ref[...].astype(jnp.float32) + got_ref[...].astype(jnp.float32)


def merge(place, stacks, got, old):
    rows = 58
    spec = pl.BlockSpec((rows, OWN, HALF), lambda l, place: (l, 0, 1 - place[0]))
    return pl.pallas_call(
        merge_kernel,
        grid_spec=pltpu.PrefetchScalarGridSpec(
            num_scalar_prefetch=1,
            grid=(pl.cdiv(LAGS, rows),),
            in_specs=[
                pl.BlockSpec(memory_space=pl.ANY),
                pl.BlockSpec((rows, OWN, HALF), lambda l, place: (l, 0, 0)),
                spec,
            ],
            out_specs=spec,
        ),
        out_shape=jax.ShapeDtypeStruct(stacks.shape, stacks.dtype),
        input_output_aliases={1: 0},
        compiler_params=pltpu.CompilerParams(vmem_limit_bytes=VMEM),
        cost_estimate=pl.CostEstimate(flops=LAGS * OWN * HALF, bytes_accessed=13 << 20, transcendentals=0),
    )(place, stacks, got, old)


def source_operand(whitened):
    x = whitened.reshape(SUB // 2, 2, FREQ // 2, 2, 2, SRC)
    real = x.transpose(2, 5, 3, 1, 0, 4)
    imag = jnp.concatenate([-real[:, :, :, 1:], real[:, :, :, :1]], axis=3)
    return jnp.concatenate([real, imag], axis=1).reshape(FREQ // 2, ROWS, 4 * SUB)


def on_device(record, quality, keep_flags, old_stacks):
    row = lax.axis_index("rcv")
    col = lax.axis_index("src")
    core = lax.rem(col, 2)
    chip = lax.div(col, 2)
    place = jnp.reshape(core, (1,)).astype(jnp.int32)
    blocks = lax.axis_size("rcv")

    padded = jnp.pad(record, ((0, PADDED - PIECE), (0, 0)))
    pieces = padded.reshape(PADDED, blocks, 1, 2, HALF).transpose(1, 2, 3, 0, 4)
    pieces = jnp.broadcast_to(pieces, (blocks, 2, 2, PADDED, HALF)).reshape(4 * blocks, PADDED, HALF)
    source_pieces = padded[:, : 2 * SRC].reshape(PADDED, 1, 2, 1, SRC).transpose(1, 2, 3, 0, 4)
    source_pieces = jnp.broadcast_to(source_pieces, (blocks, 2, 2, PADDED, SRC)).reshape(4 * blocks, PADDED, SRC)

    sources = lax.all_to_all(source_pieces, ("rcv", "src"), split_axis=0, concat_axis=0, tiled=True)
    receivers = lax.all_to_all(pieces, ("rcv", "src"), split_axis=0, concat_axis=0, tiled=True)

    keep_all = keep_flags.astype(jnp.float32)
    flags = keep_all * quality.astype(jnp.float32)[None, :]
    first_receiver = row * 2 * HALF + core * HALF
    keep_src = lax.dynamic_slice_in_dim(keep_all, chip * SRC, SRC, 1)
    keep_rcv = lax.dynamic_slice_in_dim(keep_all, first_receiver, HALF, 1)
    inverse_count = 1.0 / jnp.maximum(dot(keep_src.T, keep_rcv), 1.0)
    flags_src = lax.dynamic_slice_in_dim(flags, chip * SRC, SRC, 1).reshape(SUB // 2, 1, 2 * SRC)
    flags_rcv = lax.dynamic_slice_in_dim(flags, first_receiver, HALF, 1).reshape(SUB, 1, HALF)

    sources = sources.reshape(SUB // 2, 2, DEPTH, SRC).transpose(0, 2, 1, 3).reshape(SUB // 2, DEPTH, 2 * SRC)
    left = source_operand(whiten_sources(sources, flags_src))
    right = whiten_receivers(receivers.reshape(SUB, DEPTH, HALF), flags_rcv)
    spectra = cross(left, right)
    away = lag_call(lag_partner_kernel, place, spectra, inverse_count, None, lambda place: 1 - place[0])
    got = lax.ppermute(away, "src", [(0, 1), (1, 0), (2, 3), (3, 2)])
    stacks = lag_call(lag_own_kernel, place, spectra, inverse_count, old_stacks, lambda place: place[0])
    return merge(place, stacks, got, old_stacks)


def solution(mesh):
    return jax.shard_map(
        on_device,
        mesh=mesh,
        in_specs=(P(("rcv", "src"), None), P(), P(), P(None, "src", "rcv")),
        out_specs=P(None, "src", "rcv"),
        check_vma=False,
    )
```

time: 642 us -> 220 us (0.34); the launches traced: 630 us -> 217 us
  waiting for transfers between devices: 382 us -> 20.7 us
  Pallas kernels: 0 us -> 91.7 us
  matrix products: 79.1 us -> 1.64 us
  local copies, waits for them, and re-layouts: 116 us -> 55.9 us
  between operations: 13.9 us -> 0.17 us
    psum x1 -> x0, waiting for transfers between devices: 265 us -> none  [spread(): return lax.psum(kept, axis)]
    all_gather x1 -> x0, waiting for transfers between devices: 92.2 us -> none  [on_device(): receivers = lax.all_gather(own_spec, 'src', axis=2, tiled=True)]
    pallas_call x0 -> x6, Pallas kernels: none -> 91.7 us  [the longest x2 42.6 us: whiten_call(): pl.pallas_call(kernel, grid=(groups // 2,), in_specs=[pl.BlockSpec((2, DE...]
    dot_general x7 -> x1, matrix products: 63.9 us -> 1.64 us  [dot(): return jnp.dot(a, b, preferred_element_type=jnp.float32)]
    slice x6 -> x1, local copies, waits for them, and re-layouts: 51.8 us -> 0.01 us  [on_device(): padded[:, :2 * SRC].reshape(PADDED, 1, 2, 1, SRC).transpose(1, 2, 3, 0, 4)]
    unnamed x30 -> x13, local copies, waits for them, and re-layouts: 37.1 us -> 5.85 us
    reshape x0 -> x5, local copies, waits for them, and re-layouts: none -> 29.5 us  [the longest x1 12.3 us: source_operand(): x = whitened.reshape(SUB // 2, 2, FREQ // 2, 2, 2, SRC)]
    unnamed x1 -> x0, matrix products: 15.2 us -> none
  transfers between devices with their start and end apart: 3 -> 3, of which waited for: 3 -> 1; matrix products, arithmetic and copies ran while one was open for 8% -> 35% of each run, Pallas kernels for 0% -> 11%
where the time goes in v1:
time: 220 us; the launch traced here: 217 us
  Pallas kernels  91.7 us (42%)
  local copies, waits for them, and re-layouts  55.9 us (25%)
  other arithmetic  29 us (13%)
  waiting for transfers between devices  20.7 us (9%)
  starting transfers between devices  17.6 us (8%)
    pallas_call x2, Pallas kernels, whiten_call(): pl.pallas_call(kernel, grid=(groups // 2,), in_specs=[pl.BlockSpec((2, DE...  42.6 us
    pallas_call x1, Pallas kernels, cross(): pl.pallas_call(cross_kernel, grid=(FREQ // BLOCK,), in_specs=[pl.BlockSpe...  23.2 us
    concatenate x1, other arithmetic, source_operand(): jnp.concatenate([real, imag], axis=1).reshape(FREQ // 2, ROWS, 4 * SUB)  21 us
    all_to_all x1, waiting for transfers between devices, on_device(): lax.all_to_all(source_pieces, ('rcv', 'src'), split_axis=0, concat_axis=0...  20.7 us
    pallas_call x2, Pallas kernels, lag_call(): pl.pallas_call(kernel, grid_spec=pltpu.PrefetchScalarGridSpec(num_scalar_...  17.8 us
    reshape x1, local copies, waits for them, and re-layouts, source_operand(): x = whitened.reshape(SUB // 2, 2, FREQ // 2, 2, 2, SRC)  12.3 us
    all_to_all x1, starting transfers between devices, on_device(): lax.all_to_all(source_pieces, ('rcv', 'src'), split_axis=0, concat_axis=0...  11.7 us
    reshape x1, local copies, waits for them, and re-layouts, source_operand(): jnp.concatenate([real, imag], axis=1).reshape(FREQ // 2, ROWS, 4 * SUB)  10.6 us
  transfers between devices with their start and end apart: 3, of which 1 were waited for; matrix products, arithmetic and copies ran while one was open for 35% of the time, Pallas kernels for 11%

profile of v1, /device:TPU:0, one launch (start us, length us, event | category | flops | bytes accessed | tf_op | source)
XLA Modules:
  0.0 216.8 jit_solution(12532910260429613578)
XLA Ops:
  0.0 3.2 %copy.28 = bf16[100,8192]{0,1:T(8,128)(2,1)S(1)} copy(bf16[100,8192]{1,0:T(8,128)(2,1)} %param.16) | data formatting | bytes 3276800 | tf_op args[0]
  3.2 0.0 copy-start.3
  3.2 0.0 copy-start
  3.2 1.8 broadcast_in_dim.16
  5.1 11.7 %all-to-all-start = ((bf16[128,112,64]{1,2,0:T(8,128)(2,1)}), bf16[128,112,64]{1,2,0:T(8,128)(2,1)}, u32[]{:S(2)}, u32[]{:S(2)}) async-start(bf16[128,112,64]{1,2,0:T(8,128)(2,1)} %bitcast.29), calls=%async_computation | async-start | bytes 4194304 | tf_op jit(solution)/shard_map/all_to_all | solution.py:323
  16.8 0.0 copy-done.3
  16.8 0.0 copy-done
  16.8 0.9 convert_element_type.8
  17.7 0.1 broadcast_multiply_fusion
  17.8 0.0 copy-start.2
  17.8 0.9 copy-done.2
  18.7 0.1 constant_dynamic-slice_fusion.1
  18.8 0.7 reshape.42.flag_ref
  19.5 1.7 pad.4
  21.2 3.4 %copy.33 = bf16[32,2,112,128]{3,2,1,0:T(8,128)(2,1)S(1)} copy(bf16[32,2,112,128]{2,3,1,0:T(8,128)(2,1)} %bitcast.30) | data formatting | bytes 3670016 | tf_op jit(solution)/shard_map/broadcast_in_dim | solution.py:319
  24.6 1.6 fusion.count_ref
  26.2 20.7 %all-to-all-done = bf16[128,112,64]{1,2,0:T(8,128)(2,1)} async-done(((bf16[128,112,64]{1,2,0:T(8,128)(2,1)}), bf16[128,112,64]{1,2,0:T(8,128)(2,1)}, u32[]{:S(2)}, u32[]{:S(2)}) %all-to-all-start) | async-done | bytes 1835040 | tf_op jit(solution)/shard_map/all_to_all | solution.py:323
  47.0 2.4 %broadcast_in_dim.18 = bf16[32,2,2,112,128]{4,3,2,1,0:T(8,128)(2,1)} broadcast(bf16[32,2,112,128]{3,2,1,0:T(8,128)(2,1)S(1)} %copy.33), dimensions={0,2,3,4} | broadcast | bytes 5505024 | tf_op jit(solution)/shard_map/broadcast_in_dim | solution.py:319
  49.4 5.9 %all-to-all-start.1 = ((bf16[128,112,128]{2,1,0:T(8,128)(2,1)}), bf16[128,112,128]{2,1,0:T(8,128)(2,1)}, u32[]{:S(2)}, u32[]{:S(2)}) async-start(bf16[128,112,128]{2,1,0:T(8,128)(2,1)} %bitcast.28), calls=%async_computation.1 | async-start | bytes 7340032 | tf_op jit(solution)/shard_map/all_to_all | solution.py:324
  55.3 1.3 constant_dynamic-slice_fusion
  56.6 2.9 %copy.29 = bf16[128,112,64]{1,0,2:T(8,128)(2,1)S(1)} copy(bf16[128,112,64]{1,2,0:T(8,128)(2,1)} %all-to-all-done) | data formatting | bytes 3670016 | tf_op jit(solution)/shard_map/all_to_all | solution.py:323
  59.6 3.6 %reshape.40 = bf16[16,2,448,64]{2,1,0,3:T(2,128)(2,1)} reshape(bf16[128,112,64]{1,0,2:T(8,128)(2,1)S(1)} %copy.29) | data formatting | bytes 3670016 | tf_op jit(solution)/shard_map/reshape | solution.py:335
  63.2 2.7 %copy.30 = bf16[16,448,2,64]{1,3,2,0:T(8,128)(2,1)S(1)} copy(bf16[16,448,2,64]{1,2,0,3:T(2,128)(2,1)} %bitcast.31) | data formatting | bytes 3670016 | tf_op jit(solution)/shard_map/transpose | solution.py:335
  65.9 2.3 %copy.31.x_ref = bf16[16,448,128]{2,1,0:T(8,128)(2,1)} copy(bf16[16,448,128]{1,2,0:T(8,128)(2,1)S(1)} %bitcast.32) | data formatting | bytes 3670016 | tf_op jit(solution)/shard_map/reshape | solution.py:335
  68.2 13.8 %shard_map.154 = bf16[16,2,416,128]{3,2,1,0:T(8,128)(2,1)} custom-call(bf16[16,448,128]{2,1,0:T(8,128)(2,1)} %copy.31.x_ref, f32[16,1,128]{2,1,0:T(1,128)} %reshape.42.flag_ref, bf16[832,448]{1,0:T(8,128)(2,1)} %constant.41.clone.high_ref, bf16[832,448]{1,0:T(8,128)(2,1)} %constant.42.clone.low_ref, f32[832,128]{1,0:T(8,128)} %constant.43.clone.sums_ref, ...), custom_call_target="tpu_custom_call" | custom-call | flops 3053453312 | bytes 5505024 | tf_op jit(solution)/shard_map/pallas_call | solution.py:130
  82.0 12.3 %reshape.43 = bf16[16,2,208,2,2,64]{5,4,3,2,1,0:T(2,128)(2,1)} reshape(bf16[16,2,416,128]{3,2,1,0:T(8,128)(2,1)} %shard_map.154) | data formatting | bytes 6815744 | tf_op jit(solution)/shard_map/reshape | solution.py:303
  94.3 0.0 slice-start
  94.3 0.0 slice-start.1
  94.3 7.2 %slice_negate_fusion = (bf16[208,64,2,1,16,2]{1,5,2,0,3,4:T(2,128)(2,1)S(1)}, bf16[208,64,2,1,16,2]{1,5,2,0,3,4:T(2,128)(2,1)S(1)}) fusion(bf16[208,64,2,2,16,2]{1,5,2,0,3,4:T(2,128)(2,1)} %bitcast.23), kind=kLoop, calls=%fused_computation.1 | loop fusion | flops 851968 | bytes 6815744 | tf_op jit(solution)/shard_map/neg | solution.py:305
  101.5 0.0 slice-done
  101.5 0.0 slice-done.1
  101.5 21.0 %maximum_maximum_fusion = bf16[208,128,2,2,16,2]{1,5,2,0,3,4:T(2,128)(2,1)S(1)} fusion(bf16[208,64,2,1,16,2]{1,5,2,0,3,4:T(2,128)(2,1)S(1)} %get-tuple-element.6, bf16[208,64,2,1,16,2]{1,5,2,0,3,4:T(2,128)(2,1)S(1)} %get-tuple-element.5, bf16[208,64,2,2,16,2]{1,5,2,0,3,4:T(2,128)(2,1)S(1)} %bitcast.26), kind=kLoop, calls=%fused_computation | loop fusion | flops 20447232 | bytes 13631488 | tf_op jit(solution)/shard_map/concatenate | solution.py:306
  122.5 4.1 %copy.32 = bf16[208,128,2,2,16,2]{1,0,5,4,3,2:T(8,128)(2,1)} copy(bf16[208,128,2,2,16,2]{1,5,2,0,3,4:T(2,128)(2,1)S(1)} %maximum_maximum_fusion) | data formatting | bytes 13631488 | tf_op jit(solution)/shard_map/concatenate | solution.py:306
  126.5 10.6 %copy.34.left_ref = bf16[208,128,128]{2,1,0:T(8,128)(2,1)} copy(bf16[208,128,128]{1,0,2:T(8,128)(2,1)} %bitcast.27) | data formatting | bytes 13631488 | tf_op jit(solution)/shard_map/reshape | solution.py:306
  137.1 0.0 all-to-all-done.1
  137.1 28.8 %shard_map.155.right_ref = bf16[416,64,128]{2,1,0:T(8,128)(2,1)} custom-call(bf16[32,448,128]{2,1,0:T(8,128)(2,1)} %bitcast.13.x_ref, f32[32,1,128]{2,1,0:T(1,128)} %bitcast.34, bf16[832,448]{1,0:T(8,128)(2,1)} %constant.41.clone.high_ref, bf16[832,448]{1,0:T(8,128)(2,1)} %constant.42.clone.low_ref, f32[832,128]{1,0:T(8,128)} %constant.43.clone.sums_ref, ...), custom_call_target="tpu_custom_call" | custom-call | flops 6106906624 | bytes 11010048 | tf_op jit(solution)/shard_map/pallas_call | solution.py:130
  166.0 23.2 %shard_map.156.real_ref.imag_ref = bf16[128,416,128]{2,1,0:T(8,128)(2,1)} custom-call(bf16[208,128,128]{2,1,0:T(8,128)(2,1)} %copy.34.left_ref, bf16[416,64,128]{2,1,0:T(8,128)(2,1)} %shard_map.155.right_ref), custom_call_target="tpu_custom_call" | custom-call | flops 1744830464 | bytes 31457280 | tf_op jit(solution)/shard_map/pallas_call | solution.py:191
  189.2 8.5 %shard_map.158 = bf16[401,32,128]{2,1,0:T(8,128)(2,1)} custom-call(s32[1]{0:T(128)} %bitcast.place_ref, bf16[128,416,128]{2,1,0:T(8,128)(2,1)} %shard_map.156.real_ref.imag_ref, bf16[128,416,128]{2,1,0:T(8,128)(2,1)} %shard_map.156.real_ref.imag_ref, bf16[2,208,416]{2,1,0:T(8,128)(2,1)} %constant.46.clone.tables_ref, f32[64,128]{1,0:T(8,128)} %fusion.count_ref), custom_call_target="tpu_custom_call" | custom-call | flops 1417674752 | bytes 16777216 | tf_op jit(solution)/shard_map/pallas_call | solution.py:261
  197.7 0.0 collective-permute-start
  197.7 9.3 %shard_map.157.held_ref = f32[401,32,256]{2,1,0:T(8,128)} custom-call(s32[1]{0:T(128)} %bitcast.place_ref, bf16[128,416,128]{2,1,0:T(8,128)(2,1)} %shard_map.156.real_ref.imag_ref, bf16[128,416,128]{2,1,0:T(8,128)(2,1)} %shard_map.156.real_ref.imag_ref, bf16[2,208,416]{2,1,0:T(8,128)(2,1)} %constant.46.clone.tables_ref, f32[64,128]{1,0:T(8,128)} %fusion.count_ref, ...), custom_call_target="tpu_custom_call" | custom-call | flops 1417674752 | bytes 16777216 | tf_op jit(solution)/shard_map/pallas_call | solution.py:261
  206.9 0.0 collective-permute-done.got_ref
  207.0 0.0 copy-start.1
  207.0 1.7 copy-done.1
  208.6 8.1 %shard_map.159 = f32[401,32,256]{2,1,0:T(8,128)} custom-call(s32[1]{0:T(128)} %bitcast.place_ref, f32[401,32,256]{2,1,0:T(8,128)} %shard_map.157.held_ref, bf16[401,32,128]{2,1,0:T(8,128)(2,1)} %copy-done.1, bf16[401,32,256]{2,1,0:T(8,128)(2,1)} %old_ref.3), custom_call_target="tpu_custom_call", output_to_operand_aliasing={{}: (1, {})} | custom-call | flops 1642496 | bytes 13631488 | tf_op jit(solution)/shard_map/pallas_call | solution.py:283
  (3 shorter events, 0.0 us)
Async XLA Ops:
  3.2 13.6 %copy-start.3 = (s32[8192]{0:T(1024)S(1)}, s32[8192]{0:T(1024)}, u32[]{:S(2)}) copy-start(s32[8192]{0:T(1024)} %param.17) | copy-start | bytes 98308
  3.2 13.6 %copy-start = (s32[32,8192]{1,0:T(8,128)S(1)}, s32[32,8192]{1,0:T(8,128)}, u32[]{:S(2)}) copy-start(s32[32,8192]{1,0:T(8,128)} %param.18) | copy-start | bytes 3145732
  5.1 41.9 %all-to-all-start = ((bf16[128,112,64]{1,2,0:T(8,128)(2,1)}), bf16[128,112,64]{1,2,0:T(8,128)(2,1)}, u32[]{:S(2)}, u32[]{:S(2)}) async-start(bf16[128,112,64]{1,2,0:T(8,128)(2,1)} %bitcast.29), calls=%async_computation | async-start | bytes 4194304 | tf_op jit(solution)/shard_map/all_to_all | solution.py:323
  17.8 1.0 copy-start.2
  49.4 87.7 %all-to-all-start.1 = ((bf16[128,112,128]{2,1,0:T(8,128)(2,1)}), bf16[128,112,128]{2,1,0:T(8,128)(2,1)}, u32[]{:S(2)}, u32[]{:S(2)}) async-start(bf16[128,112,128]{2,1,0:T(8,128)(2,1)} %bitcast.28), calls=%async_computation.1 | async-start | bytes 7340032 | tf_op jit(solution)/shard_map/all_to_all | solution.py:324
  94.3 7.2 %slice-start = ((s8[6815744]{0:T(1024)(128)(4,1)}), s8[4194304]{0:T(1024)(128)(4,1)S(1)}, s32[]{:S(2)}) async-start(s8[6815744]{0:T(1024)(128)(4,1)} %bitcast.24), calls=%async_computation.2 | async-start | bytes 8388608
  94.3 7.2 %slice-start.1 = ((s8[6815744]{0:T(1024)(128)(4,1)}), s8[2621440]{0:T(1024)(128)(4,1)S(1)}, s32[]{:S(2)}) async-start(s8[6815744]{0:T(1024)(128)(4,1)} %bitcast.24), calls=%async_computation.3 | async-start | bytes 5242880
  197.7 9.3 %collective-permute-start = (bf16[401,32,128]{2,1,0:T(8,128)(2,1)}, bf16[401,32,128]{2,1,0:T(8,128)(2,1)S(1)}, u32[]{:S(2)}, u32[]{:S(2)}) collective-permute-start(bf16[401,32,128]{2,1,0:T(8,128)(2,1)} %shard_map.158), channel_id=1, source_target_pairs={{0,1},{1,0},{2,3},{3,2},{4,5},{5,4},{6,7},{7,6},{8,9},{9,8},{10,11... | collective-permute-start | bytes 9854984 | tf_op jit(solution)/shard_map/ppermute | solution.py:340
  207.0 1.7 copy-start.1

commit v2 on v1

--- a/solution.py
+++ b/solution.py
@@ -27,6 +27,7 @@
 OWN = 32
 SHIFTS = 208
 PITCH = 72
+SPITCH = 40
 ROWS = 2 * SRC
 XPITCH = ROWS + 8
 BLOCK = 16
@@ -95,20 +96,49 @@
     return real * scale, imag * scale
 
 
-def whiten_sources_kernel(x_ref, flag_ref, high_ref, low_ref, sums_ref, band_ref, inverse_ref, out_ref, spec):
-    real, imag = whiten_pair(x_ref, flag_ref, high_ref, low_ref, sums_ref, band_ref, inverse_ref, spec)
-    for g in range(2):
-        out_ref[g, 0] = real[:, g * HALF : (g + 1) * HALF].astype(jnp.bfloat16)
-        out_ref[g, 1] = imag[:, g * HALF : (g + 1) * HALF].astype(jnp.bfloat16)
-
-
-def whiten_receivers_kernel(x_ref, flag_ref, high_ref, low_ref, sums_ref, band_ref, inverse_ref, out_ref, spec, held):
+def whiten_sources_kernel(
+    x_ref, flag_ref, high_ref, low_ref, sums_ref, band_ref, inverse_ref, out_ref, spec, held
+):
     step = pl.program_id(0)
     real, imag = whiten_pair(x_ref, flag_ref, high_ref, low_ref, sums_ref, band_ref, inverse_ref, spec)
     for g in range(2):
-        window = 2 * step + g
-        held[pl.ds(window, FREQ, stride=PITCH), :] = real[:, g * HALF : (g + 1) * HALF]
-        held[pl.ds(SUB + window, FREQ, stride=PITCH), :] = imag[:, g * HALF : (g + 1) * HALF]
+        group = 2 * step + g
+        first = pl.ds(group, FREQ, stride=SPITCH)
+        second = pl.ds(SUB // 2 + group, FREQ, stride=SPITCH)
+        own_real = real[:, g * HALF : (g + 1) * HALF]
+        own_imag = imag[:, g * HALF : (g + 1) * HALF]
+        held[0, first, :] = own_real
+        held[0, second, :] = own_imag
+        held[1, first, :] = -own_imag
+        held[1, second, :] = own_real
+
+    @pl.when(step == pl.num_programs(0) - 1)
+    def _():
+        low_lanes = lax.broadcasted_iota(jnp.int32, (SRC, HALF), 1) < HALF // 2
+
+        @pl.loop(0, FREQ // 4)
+        def _(quad):
+            for part in range(2):
+                rows = [
+                    held[part, pl.ds(pl.multiple_of((4 * quad + i) * SPITCH, 8), SUB), :] for i in range(4)
+                ]
+                turned = jnp.concatenate(rows, axis=0).T
+                first, second = turned[:SRC], turned[SRC:]
+                pairs = (
+                    jnp.where(low_lanes, first, pltpu.roll(second, HALF // 2, 1)),
+                    jnp.where(low_lanes, pltpu.roll(first, HALF // 2, 1), second),
+                )
+                for i in range(2):
+                    out_ref[2 * quad + i, part * SRC : (part + 1) * SRC] = pairs[i].astype(jnp.bfloat16)
+
+
+def whiten_receivers_kernel(place_ref, x_ref, flag_ref, high_ref, low_ref, sums_ref, band_ref, inverse_ref, out_ref, spec, held):
+    step = pl.program_id(0)
+    real, imag = whiten_pair(x_ref, flag_ref, high_ref, low_ref, sums_ref, band_ref, inverse_ref, spec)
+    for g in range(2):
+        row = g * SUB + step
+        held[pl.ds(row, FREQ, stride=PITCH), :] = real[:, g * HALF : (g + 1) * HALF]
+        held[pl.ds(row + SUB // 2, FREQ, stride=PITCH), :] = imag[:, g * HALF : (g + 1) * HALF]
 
     @pl.when(step == pl.num_programs(0) - 1)
     def _():
@@ -123,63 +153,68 @@
     return pl.BlockSpec(shape, lambda *_: (0,) * len(shape))
 
 
-def whiten_call(kernel, x, flags, out_shape, out_spec, scratch):
-    groups = x.shape[0]
+def whiten_tables():
     high, low, sums = forward_table()
-    band, inverse = band_table()
+    return [jnp.asarray(table) for table in (high, low, sums, *band_table())]
+
+
+def whiten_cost(groups):
+    return pl.CostEstimate(
+        flops=groups * 4 * 2 * FREQ * DEPTH * HALF, bytes_accessed=groups * DEPTH * HALF * 6, transcendentals=0
+    )
+
+
+def whiten_receivers(place, x, flags):
+    tables = whiten_tables()
     return pl.pallas_call(
-        kernel,
-        grid=(groups // 2,),
+        whiten_receivers_kernel,
+        grid_spec=pltpu.PrefetchScalarGridSpec(
+            num_scalar_prefetch=1,
+            grid=(SUB // 2,),
+            in_specs=[
+                pl.BlockSpec((2, DEPTH, HALF), lambda g, place: (lax.bitwise_xor(g, place[1]), 0, 0)),
+                pl.BlockSpec((2, 1, HALF), lambda g, place: (g, 0, 0)),
+            ]
+            + [whole(table.shape) for table in tables],
+            out_specs=whole((FREQ, 2 * SUB, HALF)),
+            scratch_shapes=[
+                pltpu.VMEM((2 * FREQ, 2 * HALF), jnp.float32),
+                pltpu.VMEM((FREQ * PITCH, HALF), jnp.float32),
+            ],
+        ),
+        out_shape=jax.ShapeDtypeStruct((FREQ, 2 * SUB, HALF), jnp.bfloat16),
+        compiler_params=pltpu.CompilerParams(vmem_limit_bytes=VMEM),
+        cost_estimate=whiten_cost(SUB),
+    )(place, x, flags, *tables)
+
+
+def whiten_sources(x, flags):
+    tables = whiten_tables()
+    return pl.pallas_call(
+        whiten_sources_kernel,
+        grid=(SUB // 4,),
         in_specs=[
             pl.BlockSpec((2, DEPTH, HALF), lambda g: (g, 0, 0)),
             pl.BlockSpec((2, 1, HALF), lambda g: (g, 0, 0)),
-            whole(high.shape),
-            whole(low.shape),
-            whole(sums.shape),
-            whole(band.shape),
-            whole(inverse.shape),
+        ]
+        + [whole(table.shape) for table in tables],
+        out_specs=whole((FREQ // 2, ROWS, HALF)),
+        out_shape=jax.ShapeDtypeStruct((FREQ // 2, ROWS, HALF), jnp.bfloat16),
+        scratch_shapes=[
+            pltpu.VMEM((2 * FREQ, 2 * HALF), jnp.float32),
+            pltpu.VMEM((2, FREQ * SPITCH, HALF), jnp.float32),
         ],
-        out_specs=out_spec,
-        out_shape=out_shape,
-        scratch_shapes=[pltpu.VMEM((2 * FREQ, 2 * HALF), jnp.float32)] + scratch,
         compiler_params=pltpu.CompilerParams(vmem_limit_bytes=VMEM),
-        cost_estimate=pl.CostEstimate(
-            flops=groups * 2 * 2 * 2 * FREQ * DEPTH * HALF, bytes_accessed=groups * DEPTH * HALF * 6, transcendentals=0
-        ),
-    )(x, flags, jnp.asarray(high), jnp.asarray(low), jnp.asarray(sums), jnp.asarray(band), jnp.asarray(inverse))
-
-
-def whiten_receivers(x, flags):
-    return whiten_call(
-        whiten_receivers_kernel,
-        x,
-        flags,
-        jax.ShapeDtypeStruct((FREQ, 2 * SUB, HALF), jnp.bfloat16),
-        whole((FREQ, 2 * SUB, HALF)),
-        [pltpu.VMEM((FREQ * PITCH, HALF), jnp.float32)],
-    )
-
-
-def whiten_sources(x, flags):
-    groups = x.shape[0]
-    return whiten_call(
-        whiten_sources_kernel,
-        x,
-        flags,
-        jax.ShapeDtypeStruct((groups, 2, FREQ, HALF), jnp.bfloat16),
-        pl.BlockSpec((2, 2, FREQ, HALF), lambda g: (g, 0, 0, 0)),
-        [],
-    )
+        cost_estimate=whiten_cost(SUB // 2),
+    )(x, flags, *tables)
 
 
 def cross_kernel(left_ref, right_ref, out_ref, held):
     zeros = jnp.zeros((2 * SUB, HALF), jnp.bfloat16)
     for pair in range(BLOCK // 2):
-        first = right_ref[2 * pair]
-        second = right_ref[2 * pair + 1]
-        weights = jnp.concatenate(
-            [jnp.concatenate([first, zeros], axis=1), jnp.concatenate([zeros, second], axis=1)], axis=0
-        )
+        first = jnp.concatenate([right_ref[2 * pair], zeros], axis=1)
+        second = jnp.concatenate([zeros, right_ref[2 * pair + 1]], axis=1)
+        weights = jnp.concatenate([first[:SUB], second[:SUB], first[SUB:], second[SUB:]], axis=0)
         product = dot(left_ref[pair], weights)
         held[pl.ds(2 * pair * XPITCH, ROWS), :] = product[:, :HALF]
         held[pl.ds((2 * pair + 1) * XPITCH, ROWS), :] = product[:, HALF:]
@@ -299,11 +334,41 @@
     )(place, stacks, got, old)
 
 
-def source_operand(whitened):
-    x = whitened.reshape(SUB // 2, 2, FREQ // 2, 2, 2, SRC)
-    real = x.transpose(2, 5, 3, 1, 0, 4)
-    imag = jnp.concatenate([-real[:, :, :, 1:], real[:, :, :, :1]], axis=3)
-    return jnp.concatenate([real, imag], axis=1).reshape(FREQ // 2, ROWS, 4 * SUB)
+def device(x, y, z_low, z_high, core):
+    return ((x * 4 + y) * 2 + z_low) * 4 + z_high * 2 + core
+
+
+def send(value, route):
+    places = [(x, y, l, h, c) for x in range(4) for y in range(4) for l in range(2) for h in range(2) for c in range(2)]
+    return lax.ppermute(value, ("rcv", "src"), [(device(*place), device(*route(*place))) for place in places])
+
+
+def near_sources(record, z_low, z_high):
+    near = record[:, : 2 * SRC]
+    same = jnp.where(z_high == 0, near[:, :SRC], near[:, SRC:])
+    other = jnp.where(z_high == 0, near[:, SRC:], near[:, :SRC])
+    low = send(same, lambda x, y, l, h, c: (x, y, 1 - l, h, c))
+    high = send(other, lambda x, y, l, h, c: (x, y, l, 1 - h, c))
+    both = send(other, lambda x, y, l, h, c: (x, y, 1 - l, 1 - h, c))
+
+    def windows(mine, theirs):
+        return jnp.where(z_low == 0, jnp.concatenate([mine, theirs], 1), jnp.concatenate([theirs, mine], 1))
+
+    mine, theirs = windows(same, low), windows(high, both)
+    rows = jnp.where(z_high == 0, jnp.stack([mine, theirs]), jnp.stack([theirs, mine]))
+    return jnp.pad(rows, ((0, 0), (0, PADDED - PIECE), (0, 0)))
+
+
+def plane_sources(near):
+    column = jnp.stack([near] + [send(near, lambda x, y, l, h, c, d=d: (x, y ^ d, l, h, c)) for d in (1, 2, 3)])
+    plane = jnp.stack([column] + [send(column, lambda x, y, l, h, c, d=d: (x ^ d, y, l, h, c)) for d in (1, 2, 3)])
+    return plane.reshape(SUB // 2, 2, PADDED, HALF)
+
+
+def both_cores(plane, core):
+    other = send(plane, lambda x, y, l, h, c: (x, y, l, h, 1 - c))
+    rows = jnp.where(core == 0, jnp.stack([plane, other], axis=2), jnp.stack([other, plane], axis=2))
+    return rows.reshape(SUB // 2, DEPTH, HALF)
 
 
 def on_device(record, quality, keep_flags, old_stacks):
@@ -311,17 +376,18 @@
     col = lax.axis_index("src")
     core = lax.rem(col, 2)
     chip = lax.div(col, 2)
-    place = jnp.reshape(core, (1,)).astype(jnp.int32)
+    z_low = lax.rem(row, 2)
+    group = lax.div(row, 2)
+    place = jnp.stack([core, group]).astype(jnp.int32)
     blocks = lax.axis_size("rcv")
 
-    padded = jnp.pad(record, ((0, PADDED - PIECE), (0, 0)))
-    pieces = padded.reshape(PADDED, blocks, 1, 2, HALF).transpose(1, 2, 3, 0, 4)
+    pieces = jnp.pad(record, ((0, PADDED - PIECE), (0, 0)))
+    pieces = pieces.reshape(PADDED, blocks, 1, 2, HALF).transpose(1, 2, 3, 0, 4)
     pieces = jnp.broadcast_to(pieces, (blocks, 2, 2, PADDED, HALF)).reshape(4 * blocks, PADDED, HALF)
-    source_pieces = padded[:, : 2 * SRC].reshape(PADDED, 1, 2, 1, SRC).transpose(1, 2, 3, 0, 4)
-    source_pieces = jnp.broadcast_to(source_pieces, (blocks, 2, 2, PADDED, SRC)).reshape(4 * blocks, PADDED, SRC)
-
-    sources = lax.all_to_all(source_pieces, ("rcv", "src"), split_axis=0, concat_axis=0, tiled=True)
+    plane = plane_sources(near_sources(record, z_low, chip))
+    plane, pieces = lax.optimization_barrier((plane, pieces))
     receivers = lax.all_to_all(pieces, ("rcv", "src"), split_axis=0, concat_axis=0, tiled=True)
+    sources = both_cores(plane, core)
 
     keep_all = keep_flags.astype(jnp.float32)
     flags = keep_all * quality.astype(jnp.float32)[None, :]
@@ -329,12 +395,12 @@
     keep_src = lax.dynamic_slice_in_dim(keep_all, chip * SRC, SRC, 1)
     keep_rcv = lax.dynamic_slice_in_dim(keep_all, first_receiver, HALF, 1)
     inverse_count = 1.0 / jnp.maximum(dot(keep_src.T, keep_rcv), 1.0)
-    flags_src = lax.dynamic_slice_in_dim(flags, chip * SRC, SRC, 1).reshape(SUB // 2, 1, 2 * SRC)
-    flags_rcv = lax.dynamic_slice_in_dim(flags, first_receiver, HALF, 1).reshape(SUB, 1, HALF)
-
-    sources = sources.reshape(SUB // 2, 2, DEPTH, SRC).transpose(0, 2, 1, 3).reshape(SUB // 2, DEPTH, 2 * SRC)
-    left = source_operand(whiten_sources(sources, flags_src))
-    right = whiten_receivers(receivers.reshape(SUB, DEPTH, HALF), flags_rcv)
+    order = lax.bitwise_xor(jnp.arange(SUB // 2, dtype=jnp.int32), group.astype(jnp.int32))
+    flags_src = lax.dynamic_slice_in_dim(flags, chip * SRC, SRC, 1).reshape(SUB // 2, 1, 2 * SRC)[order]
+    flags_rcv = lax.dynamic_slice_in_dim(flags, first_receiver, HALF, 1).reshape(SUB // 2, 2, HALF)[order]
+
+    left = whiten_sources(sources, flags_src)
+    right = whiten_receivers(place, receivers.reshape(SUB, DEPTH, HALF), flags_rcv.reshape(SUB, 1, HALF))
     spectra = cross(left, right)
     away = lag_call(lag_partner_kernel, place, spectra, inverse_count, None, lambda place: 1 - place[0])
     got = lax.ppermute(away, "src", [(0, 1), (1, 0), (2, 3), (3, 2)])

time: 220 us -> 176 us (0.80)
  local copies, waits for them, and re-layouts: 55.9 us -> 16.1 us
  Pallas kernels: 91.7 us -> 118 us
  other arithmetic: 29 us -> 4.98 us
  waiting for transfers between devices: 20.7 us -> 12.9 us
  starting transfers between devices: 17.6 us -> 20.4 us
    pallas_call x2, Pallas kernels: 42.6 us -> 66.8 us  [the longest x1 36 us: whiten_sources(): pl.pallas_call(whiten_sources_kernel, grid=(SUB // 4,), in_specs=[pl.Bloc...]
    reshape x4 -> x1, local copies, waits for them, and re-layouts: 28.8 us -> 4.58 us  [on_device(): pieces = pieces.reshape(PADDED, blocks, 1, 2, HALF).transpose(1, 2, 3, 0, 4)]
    concatenate x1 -> x0, other arithmetic: 21 us -> none  [source_operand(): jnp.concatenate([real, imag], axis=1).reshape(FREQ // 2, ROWS, 4 * SUB)]
    all_to_all x1 -> x0, waiting for transfers between devices: 20.7 us -> none  [on_device(): lax.all_to_all(source_pieces, ('rcv', 'src'), split_axis=0, concat_axis=0...]
    ppermute x0 -> x10, starting transfers between devices: none -> 14.5 us  [send(): lax.ppermute(value, ('rcv', 'src'), [(device(*place), device(*route(*plac...]
    all_to_all x1 -> x0, starting transfers between devices: 11.7 us -> none  [on_device(): lax.all_to_all(source_pieces, ('rcv', 'src'), split_axis=0, concat_axis=0...]
    ppermute x0 -> x10, waiting for transfers between devices: none -> 9.21 us  [send(): lax.ppermute(value, ('rcv', 'src'), [(device(*place), device(*route(*plac...]
    neg x1 -> x0, other arithmetic: 7.16 us -> none  [source_operand(): imag = jnp.concatenate([-real[:, :, :, 1:], real[:, :, :, :1]], axis=3)]
  transfers between devices with their start and end apart: 3 -> 12, of which waited for: 1 -> 6; matrix products, arithmetic and copies ran while one was open for 35% -> 10% of each run, Pallas kernels for 11% -> 27%
where the time goes in v2:
time: 176 us; the launch traced here: 173 us
  Pallas kernels  118 us (67%)
  starting transfers between devices  20.4 us (12%)
  local copies, waits for them, and re-layouts  16.1 us (9%)
  waiting for transfers between devices  12.9 us (7%)
  other arithmetic  4.98 us (3%)
    pallas_call x1, Pallas kernels, whiten_sources(): pl.pallas_call(whiten_sources_kernel, grid=(SUB // 4,), in_specs=[pl.Bloc...  36 us
    pallas_call x1, Pallas kernels, whiten_receivers(): pl.pallas_call(whiten_receivers_kernel, grid_spec=pltpu.PrefetchScalarGri...  30.8 us
    pallas_call x1, Pallas kernels, cross(): pl.pallas_call(cross_kernel, grid=(FREQ // BLOCK,), in_specs=[pl.BlockSpe...  23.2 us
    pallas_call x2, Pallas kernels, lag_call(): pl.pallas_call(kernel, grid_spec=pltpu.PrefetchScalarGridSpec(num_scalar_...  19.1 us
    ppermute x10, starting transfers between devices, send(): lax.ppermute(value, ('rcv', 'src'), [(device(*place), device(*route(*plac...  14.5 us
    ppermute x10, waiting for transfers between devices, send(): lax.ppermute(value, ('rcv', 'src'), [(device(*place), device(*route(*plac...  9.21 us
    pallas_call x1, Pallas kernels, merge(): pl.pallas_call(merge_kernel, grid_spec=pltpu.PrefetchScalarGridSpec(num_s...  8.82 us
    all_to_all x1, starting transfers between devices, on_device(): lax.all_to_all(pieces, ('rcv', 'src'), split_axis=0, concat_axis=0, tiled...  5.92 us
  transfers between devices with their start and end apart: 12, of which 6 were waited for; matrix products, arithmetic and copies ran while one was open for 10% of the time, Pallas kernels for 27%

profile of v2, /device:TPU:0, one launch (start us, length us, event | category | flops | bytes accessed | tf_op | source)
XLA Modules:
  0.0 173.4 jit_solution(9996890214939780584)
XLA Ops:
  0.0 0.9 broadcast_select_fusion.1
  0.9 2.1 %collective-permute-start = (bf16[100,64]{1,0:T(8,128)(2,1)S(1)}, bf16[100,64]{1,0:T(8,128)(2,1)S(1)}, u32[]{:S(2)}, u32[]{:S(2)}) collective-permute-start(bf16[100,64]{1,0:T(8,128)(2,1)S(1)} %get-tuple-element.9), channel_id=1, source_target_pairs={{0,4},{1,5},{2,6},{3,7},{4,0},{5,1},{6,2},{7,3},{8,12},{9,13},{10,... | collective-permute-start | bytes 38408 | tf_op jit(solution)/shard_map/ppermute | solution.py:343
  3.0 2.5 %collective-permute-start.2 = (bf16[100,64]{1,0:T(8,128)(2,1)S(1)}, bf16[100,64]{1,0:T(8,128)(2,1)S(1)}, u32[]{:S(2)}, u32[]{:S(2)}) collective-permute-start(bf16[100,64]{1,0:T(8,128)(2,1)S(1)} %get-tuple-element.10), channel_id=1, source_target_pairs={{0,6},{1,7},{2,4},{3,5},{4,2},{5,3},{6,0},{7,1},{8,14},{9,15},{10,... | collective-permute-start | bytes 38408 | tf_op jit(solution)/shard_map/ppermute | solution.py:343
  5.5 1.1 collective-permute-start.1
  6.6 0.0 collective-permute-done
  6.6 0.1 maximum_select_fusion.2
  6.7 1.4 collective-permute-done.2
  8.0 2.8 %collective-permute-done.1 = bf16[100,64]{1,0:T(8,128)(2,1)S(1)} collective-permute-done((bf16[100,64]{1,0:T(8,128)(2,1)S(1)}, bf16[100,64]{1,0:T(8,128)(2,1)S(1)}, u32[]{:S(2)}, u32[]{:S(2)}) %collective-permute-start.1) | collective-permute-done | bytes 12832 | tf_op jit(solution)/shard_map/ppermute | solution.py:343
  10.9 0.1 maximum_select_fusion.3
  11.0 3.3 %collective-permute-start.4 = (bf16[2,112,128]{2,1,0:T(8,128)(2,1)S(1)}, bf16[2,112,128]{2,1,0:T(8,128)(2,1)S(1)}, u32[]{:S(2)}, u32[]{:S(2)}) collective-permute-start(bf16[2,112,128]{2,1,0:T(8,128)(2,1)S(1)} %get-tuple-element.14), channel_id=1, source_target_pairs={{0,16},{1,17},{2,18},{3,19},{4,20},{5,21},{6,22},{7,23},{8,24},{9,... | collective-permute-start | bytes 172040 | tf_op jit(solution)/shard_map/ppermute | solution.py:343
  14.3 0.7 collective-permute-start.3
  15.0 0.4 collective-permute-start.5
  15.3 1.5 collective-permute-done.4
  16.8 1.6 collective-permute-done.3
  18.5 1.9 %collective-permute-done.5 = bf16[2,112,128]{2,1,0:T(8,128)(2,1)S(1)} collective-permute-done((bf16[2,112,128]{2,1,0:T(8,128)(2,1)S(1)}, bf16[2,112,128]{2,1,0:T(8,128)(2,1)S(1)}, u32[]{:S(2)}, u32[]{:S(2)}) %collective-permute-start.5) | collective-permute-done | bytes 57376 | tf_op jit(solution)/shard_map/ppermute | solution.py:343
  20.4 3.1 %collective-permute-start.7 = (bf16[4,2,112,128]{3,2,1,0:T(8,128)(2,1)S(1)}, bf16[4,2,112,128]{3,2,1,0:T(8,128)(2,1)S(1)}, u32[]{:S(2)}, u32[]{:S(2)}) collective-permute-start(bf16[4,2,112,128]{3,2,1,0:T(8,128)(2,1)S(1)} %get-tuple-element.12), channel_id=1, source_target_pairs={{0,64},{1,65},{2,66},{3,67},{4,68},{5,69},{6,70},{7,71},{8,72},{9,... | collective-permute-start | bytes 688136 | tf_op jit(solution)/shard_map/ppermute | solution.py:343
  23.5 0.6 collective-permute-start.6
  24.1 0.6 collective-permute-start.8
  24.6 2.9 %pad.9 = bf16[112,8192]{1,0:T(8,128)(2,1)} pad(bf16[100,8192]{1,0:T(8,128)(2,1)} %param.16, bf16[]{:T(256)} %constant.41.clone.1), padding=0_12x0_0 | pad | bytes 3473410 | tf_op jit(solution)/shard_map/jit(_pad)/pad | solution.py:384
  27.5 4.6 %reshape.154 = bf16[112,32,1,2,128]{4,3,1,0,2:T(2,128)(2,1)S(1)} reshape(bf16[112,8192]{1,0:T(8,128)(2,1)} %pad.9) | data formatting | bytes 3670016 | tf_op jit(solution)/shard_map/reshape | solution.py:385
  32.1 2.1 %copy.18 = bf16[32,2,112,128]{3,2,1,0:T(8,128)(2,1)S(1)} copy(bf16[32,2,112,128]{3,1,0,2:T(2,128)(2,1)S(1)} %bitcast.32) | data formatting | bytes 3670016 | tf_op jit(solution)/shard_map/broadcast_in_dim | solution.py:386
  34.2 0.0 collective-permute-done.7
  34.2 0.0 collective-permute-done.6
  34.2 0.0 collective-permute-done.8
  34.2 0.1 pad_maximum_fusion
  34.4 2.4 %broadcast_in_dim.5 = bf16[32,2,2,112,128]{4,3,2,1,0:T(8,128)(2,1)} broadcast(bf16[32,2,112,128]{3,2,1,0:T(8,128)(2,1)S(1)} %copy.18), dimensions={0,2,3,4} | broadcast | bytes 5505024 | tf_op jit(solution)/shard_map/broadcast_in_dim | solution.py:386
  36.8 5.9 %all-to-all-start = ((bf16[128,112,128]{2,1,0:T(8,128)(2,1)}), bf16[128,112,128]{2,1,0:T(8,128)(2,1)}, u32[]{:S(2)}, u32[]{:S(2)}) async-start(bf16[128,112,128]{2,1,0:T(8,128)(2,1)} %bitcast.30), calls=%async_computation | async-start | bytes 7340032 | tf_op jit(solution)/shard_map/all_to_all | solution.py:389
  42.7 0.3 collective-permute-start.9
  43.0 0.1 broadcast_multiply_fusion
  43.1 0.1 convert_element_type.10
  43.2 0.1 constant_dynamic-slice_fusion.1
  43.3 0.1 reshape.160
  43.4 1.1 gather_fusion
  44.5 1.2 gather_fusion.1
  45.7 0.6 pad_add_fusion.place_ref
  46.3 0.9 fusion.count_ref
  47.1 0.0 collective-permute-done.9
  47.1 3.0 %maximum_select_fusion = bf16[16,2,2,112,128]{4,3,2,1,0:T(8,128)(2,1)} fusion(bf16[16,2,1,112,128]{4,3,2,1,0:T(8,128)(2,1)} %bitcast.19, bf16[16,2,1,112,128]{4,3,2,1,0:T(8,128)(2,1)S(1)} %bitcast.34, pred[]{:T(512)S(6)} %eq.12), kind=kLoop, calls=%fused_computation.2 | loop fusion | flops 2752512 | bytes 3670017 | tf_op jit(solution)/shard_map/jit(_where)/select_n | solution.py:370
  50.1 36.0 %shard_map.154.left_ref = bf16[208,128,128]{2,1,0:T(8,128)(2,1)} custom-call(bf16[16,448,128]{2,1,0:T(8,128)(2,1)} %bitcast.31, f32[16,1,128]{2,1,0:T(1,128)} %bitcast.43, bf16[832,448]{1,0:T(8,128)(2,1)} %constant.48.clone.high_ref, bf16[832,448]{1,0:T(8,128)(2,1)} %constant.49.clone.low_ref, f32[832,128]{1,0:T(8,128)} %constant.50.clone.sums_ref, ...), custom_call_target="tpu_custom_call" | custom-call | flops 3053453312 | bytes 5505024 | tf_op jit(solution)/shard_map/pallas_call | solution.py:193
  86.2 3.6 %all-to-all-done = bf16[128,112,128]{2,1,0:T(8,128)(2,1)} async-done(((bf16[128,112,128]{2,1,0:T(8,128)(2,1)}), bf16[128,112,128]{2,1,0:T(8,128)(2,1)}, u32[]{:S(2)}, u32[]{:S(2)}) %all-to-all-start) | async-done | bytes 3670048 | tf_op jit(solution)/shard_map/all_to_all | solution.py:389
  89.8 30.8 %shard_map.155.right_ref = bf16[416,64,128]{2,1,0:T(8,128)(2,1)} custom-call(s32[2]{0:T(128)} %pad_add_fusion.place_ref, bf16[32,448,128]{2,1,0:T(8,128)(2,1)} %bitcast.23.x_ref, f32[32,1,128]{2,1,0:T(1,128)} %bitcast.47, bf16[832,448]{1,0:T(8,128)(2,1)} %constant.48.clone.high_ref, bf16[832,448]{1,0:T(8,128)(2,1)} %constant.49.clone.low_ref, ...), custom_call_target="tpu_custom_call" | custom-call | flops 6106906624 | bytes 11010048 | tf_op jit(solution)/shard_map/pallas_call | solution.py:169
  120.6 23.2 %shard_map.156.real_ref.imag_ref = bf16[128,416,128]{2,1,0:T(8,128)(2,1)} custom-call(bf16[208,128,128]{2,1,0:T(8,128)(2,1)} %shard_map.154.left_ref, bf16[416,64,128]{2,1,0:T(8,128)(2,1)} %shard_map.155.right_ref), custom_call_target="tpu_custom_call" | custom-call | flops 1744830464 | bytes 31457280 | tf_op jit(solution)/shard_map/pallas_call | solution.py:226
  143.8 9.2 %shard_map.158 = bf16[401,32,128]{2,1,0:T(8,128)(2,1)} custom-call(s32[2]{0:T(128)} %pad_add_fusion.place_ref, bf16[128,416,128]{2,1,0:T(8,128)(2,1)} %shard_map.156.real_ref.imag_ref, bf16[128,416,128]{2,1,0:T(8,128)(2,1)} %shard_map.156.real_ref.imag_ref, bf16[2,208,416]{2,1,0:T(8,128)(2,1)} %constant.53.clone.tables_ref, f32[64,128]{1,0:T(8,128)} %fusion.count_ref), custom_call_target="tpu_custom_call" | custom-call | flops 1417674752 | bytes 16777216 | tf_op jit(solution)/shard_map/pallas_call | solution.py:296
  153.0 0.0 collective-permute-start.10
  153.0 9.9 %shard_map.157.held_ref = f32[401,32,256]{2,1,0:T(8,128)} custom-call(s32[2]{0:T(128)} %pad_add_fusion.place_ref, bf16[128,416,128]{2,1,0:T(8,128)(2,1)} %shard_map.156.real_ref.imag_ref, bf16[128,416,128]{2,1,0:T(8,128)(2,1)} %shard_map.156.real_ref.imag_ref, bf16[2,208,416]{2,1,0:T(8,128)(2,1)} %constant.53.clone.tables_ref, f32[64,128]{1,0:T(8,128)} %fusion.count_ref, ...), custom_call_target="tpu_custom_call" | custom-call | flops 1417674752 | bytes 16777216 | tf_op jit(solution)/shard_map/pallas_call | solution.py:296
  162.9 0.0 collective-permute-done.10.got_ref
  162.9 1.7 copy-done.1
  164.6 8.8 %shard_map.159 = f32[401,32,256]{2,1,0:T(8,128)} custom-call(s32[2]{0:T(128)} %pad_add_fusion.place_ref, f32[401,32,256]{2,1,0:T(8,128)} %shard_map.157.held_ref, bf16[401,32,128]{2,1,0:T(8,128)(2,1)} %copy-done.1, bf16[401,32,256]{2,1,0:T(8,128)(2,1)} %old_ref.3), custom_call_target="tpu_custom_call", output_to_operand_aliasing={{}: (1, {})} | custom-call | flops 1642496 | bytes 13631488 | tf_op jit(solution)/shard_map/pallas_call | solution.py:318
  (12 shorter events, 0.1 us)
Async XLA Ops:
  0.9 5.7 %collective-permute-start = (bf16[100,64]{1,0:T(8,128)(2,1)S(1)}, bf16[100,64]{1,0:T(8,128)(2,1)S(1)}, u32[]{:S(2)}, u32[]{:S(2)}) collective-permute-start(bf16[100,64]{1,0:T(8,128)(2,1)S(1)} %get-tuple-element.9), channel_id=1, source_target_pairs={{0,4},{1,5},{2,6},{3,7},{4,0},{5,1},{6,2},{7,3},{8,12},{9,13},{10,... | collective-permute-start | bytes 38408 | tf_op jit(solution)/shard_map/ppermute | solution.py:343
  3.0 5.1 %collective-permute-start.2 = (bf16[100,64]{1,0:T(8,128)(2,1)S(1)}, bf16[100,64]{1,0:T(8,128)(2,1)S(1)}, u32[]{:S(2)}, u32[]{:S(2)}) collective-permute-start(bf16[100,64]{1,0:T(8,128)(2,1)S(1)} %get-tuple-element.10), channel_id=1, source_target_pairs={{0,6},{1,7},{2,4},{3,5},{4,2},{5,3},{6,0},{7,1},{8,14},{9,15},{10,... | collective-permute-start | bytes 38408 | tf_op jit(solution)/shard_map/ppermute | solution.py:343
  5.5 5.4 %collective-permute-start.1 = (bf16[100,64]{1,0:T(8,128)(2,1)S(1)}, bf16[100,64]{1,0:T(8,128)(2,1)S(1)}, u32[]{:S(2)}, u32[]{:S(2)}) collective-permute-start(bf16[100,64]{1,0:T(8,128)(2,1)S(1)} %get-tuple-element.10), channel_id=1, source_target_pairs={{0,2},{1,3},{2,0},{3,1},{4,6},{5,7},{6,4},{7,5},{8,10},{9,11},{10,... | collective-permute-start | bytes 38408 | tf_op jit(solution)/shard_map/ppermute | solution.py:343
  11.0 5.8 %collective-permute-start.4 = (bf16[2,112,128]{2,1,0:T(8,128)(2,1)S(1)}, bf16[2,112,128]{2,1,0:T(8,128)(2,1)S(1)}, u32[]{:S(2)}, u32[]{:S(2)}) collective-permute-start(bf16[2,112,128]{2,1,0:T(8,128)(2,1)S(1)} %get-tuple-element.14), channel_id=1, source_target_pairs={{0,16},{1,17},{2,18},{3,19},{4,20},{5,21},{6,22},{7,23},{8,24},{9,... | collective-permute-start | bytes 172040 | tf_op jit(solution)/shard_map/ppermute | solution.py:343
  14.3 4.2 %collective-permute-start.3 = (bf16[2,112,128]{2,1,0:T(8,128)(2,1)S(1)}, bf16[2,112,128]{2,1,0:T(8,128)(2,1)S(1)}, u32[]{:S(2)}, u32[]{:S(2)}) collective-permute-start(bf16[2,112,128]{2,1,0:T(8,128)(2,1)S(1)} %get-tuple-element.14), channel_id=1, source_target_pairs={{0,8},{1,9},{2,10},{3,11},{4,12},{5,13},{6,14},{7,15},{8,0},{9,1},... | collective-permute-start | bytes 172040 | tf_op jit(solution)/shard_map/ppermute | solution.py:343
  15.0 5.4 %collective-permute-start.5 = (bf16[2,112,128]{2,1,0:T(8,128)(2,1)S(1)}, bf16[2,112,128]{2,1,0:T(8,128)(2,1)S(1)}, u32[]{:S(2)}, u32[]{:S(2)}) collective-permute-start(bf16[2,112,128]{2,1,0:T(8,128)(2,1)S(1)} %get-tuple-element.14), channel_id=1, source_target_pairs={{0,24},{1,25},{2,26},{3,27},{4,28},{5,29},{6,30},{7,31},{8,16},{9,... | collective-permute-start | bytes 172040 | tf_op jit(solution)/shard_map/ppermute | solution.py:343
  20.4 13.8 %collective-permute-start.7 = (bf16[4,2,112,128]{3,2,1,0:T(8,128)(2,1)S(1)}, bf16[4,2,112,128]{3,2,1,0:T(8,128)(2,1)S(1)}, u32[]{:S(2)}, u32[]{:S(2)}) collective-permute-start(bf16[4,2,112,128]{3,2,1,0:T(8,128)(2,1)S(1)} %get-tuple-element.12), channel_id=1, source_target_pairs={{0,64},{1,65},{2,66},{3,67},{4,68},{5,69},{6,70},{7,71},{8,72},{9,... | collective-permute-start | bytes 688136 | tf_op jit(solution)/shard_map/ppermute | solution.py:343
  23.5 10.7 %collective-permute-start.6 = (bf16[4,2,112,128]{3,2,1,0:T(8,128)(2,1)S(1)}, bf16[4,2,112,128]{3,2,1,0:T(8,128)(2,1)S(1)}, u32[]{:S(2)}, u32[]{:S(2)}) collective-permute-start(bf16[4,2,112,128]{3,2,1,0:T(8,128)(2,1)S(1)} %get-tuple-element.12), channel_id=1, source_target_pairs={{0,32},{1,33},{2,34},{3,35},{4,36},{5,37},{6,38},{7,39},{8,40},{9,... | collective-permute-start | bytes 688136 | tf_op jit(solution)/shard_map/ppermute | solution.py:343
  24.1 10.2 %collective-permute-start.8 = (bf16[4,2,112,128]{3,2,1,0:T(8,128)(2,1)S(1)}, bf16[4,2,112,128]{3,2,1,0:T(8,128)(2,1)S(1)}, u32[]{:S(2)}, u32[]{:S(2)}) collective-permute-start(bf16[4,2,112,128]{3,2,1,0:T(8,128)(2,1)S(1)} %get-tuple-element.12), channel_id=1, source_target_pairs={{0,96},{1,97},{2,98},{3,99},{4,100},{5,101},{6,102},{7,103},{8,104... | collective-permute-start | bytes 688136 | tf_op jit(solution)/shard_map/ppermute | solution.py:343
  36.8 5.9 %copy-start.2 = (s32[8192]{0:T(1024)S(1)}, s32[8192]{0:T(1024)}, u32[]{:S(2)}) copy-start(s32[8192]{0:T(1024)} %param.17) | copy-start | bytes 98308
  36.8 6.2 %copy-start = (s32[32,8192]{1,0:T(8,128)S(1)}, s32[32,8192]{1,0:T(8,128)}, u32[]{:S(2)}) copy-start(s32[32,8192]{1,0:T(8,128)} %param.18) | copy-start | bytes 3145732
  36.8 53.0 %all-to-all-start = ((bf16[128,112,128]{2,1,0:T(8,128)(2,1)}), bf16[128,112,128]{2,1,0:T(8,128)(2,1)}, u32[]{:S(2)}, u32[]{:S(2)}) async-start(bf16[128,112,128]{2,1,0:T(8,128)(2,1)} %bitcast.30), calls=%async_computation | async-start | bytes 7340032 | tf_op jit(solution)/shard_map/all_to_all | solution.py:389
  42.7 4.4 %collective-permute-start.9 = (bf16[16,2,112,128]{3,2,1,0:T(8,128)(2,1)S(1)}, bf16[16,2,112,128]{3,2,1,0:T(8,128)(2,1)}, u32[]{:S(2)}, u32[]{:S(2)}) collective-permute-start(bf16[16,2,112,128]{3,2,1,0:T(8,128)(2,1)S(1)} %bitcast.33), channel_id=1, source_target_pairs={{0,1},{1,0},{2,3},{3,2},{4,5},{5,4},{6,7},{7,6},{8,9},{9,8},{10,11... | collective-permute-start | bytes 2752520 | tf_op jit(solution)/shard_map/ppermute | solution.py:343
  153.0 9.9 %collective-permute-start.10 = (bf16[401,32,128]{2,1,0:T(8,128)(2,1)}, bf16[401,32,128]{2,1,0:T(8,128)(2,1)S(1)}, u32[]{:S(2)}, u32[]{:S(2)}) collective-permute-start(bf16[401,32,128]{2,1,0:T(8,128)(2,1)} %shard_map.158), channel_id=1, source_target_pairs={{0,1},{1,0},{2,3},{3,2},{4,5},{5,4},{6,7},{7,6},{8,9},{9,8},{10,11... | collective-permute-start | bytes 9854984 | tf_op jit(solution)/shard_map/ppermute | solution.py:406
  162.9 1.7 copy-start.1

commit v3 on v2

v3 whole, which is shorter than its diff:
```python
import functools
import math

import jax
import jax.numpy as jnp
import numpy as np
from jax import lax
from jax.experimental import pallas as pl
from jax.experimental.pallas import tpu as pltpu
from jax.sharding import PartitionSpec as P

WIN = 400
NFFT = 800
BINS = 401
LARGEST_LAG = 200
LAGS = 401
HALFBAND = 32
SUB = 32
EPSILON = 1e-06

PIECE = WIN // 4
PADDED = 112
DEPTH = 4 * PADDED
FREQ = 416
HALF = 128
SRC = 64
OWN = 32
SHIFTS = 208
PITCH = 72
SPITCH = 40
ROWS = 2 * SRC
XPITCH = ROWS + 8
BLOCK = 16
PAIRS = 4
VMEM = 56 * 1024 * 1024


def split(table):
    high = table.astype(jnp.bfloat16)
    low = (table - high.astype(np.float32)).astype(jnp.bfloat16)
    return high, low


def forward_table():
    samples = np.arange(WIN)[None, :]
    bins = np.arange(BINS)[:, None]
    phases = (samples * bins % NFFT) * (2.0 * math.pi / NFFT)
    table = np.zeros((2, FREQ, 4, PADDED), np.float32)
    table[0, :BINS, :, :PIECE] = np.cos(phases).reshape(BINS, 4, PIECE)
    table[1, :BINS, :, :PIECE] = -np.sin(phases).reshape(BINS, 4, PIECE)
    high, low = split(table.reshape(2 * FREQ, DEPTH))
    sums = (high.astype(np.float64) + low.astype(np.float64)).sum(axis=1, keepdims=True)
    sums = np.broadcast_to((sums / WIN).astype(np.float32), (2 * FREQ, HALF)).copy()
    return np.concatenate([high, low], axis=1), sums


def band_table():
    bins = np.arange(FREQ)
    inside = np.abs(bins[:, None] - bins[None, :]) <= HALFBAND
    inside &= (bins[:, None] < BINS) & (bins[None, :] < BINS)
    counts = np.maximum(inside.sum(axis=1, keepdims=True), 1)
    inverse = np.broadcast_to((1.0 / (2.0 * counts)).astype(np.float32), (FREQ, HALF)).copy()
    return np.concatenate([inside, inside], axis=1).astype(jnp.bfloat16), inverse


def lag_tables():
    shifts = np.arange(LARGEST_LAG + 1)[:, None]
    bins = np.arange(BINS)[None, :]
    phases = (shifts * bins % NFFT) * (2.0 * math.pi / NFFT)
    weights = np.where((bins == 0) | (bins == NFFT // 2), 1.0, 2.0) / math.sqrt(NFFT)
    tables = np.zeros((2, SHIFTS, FREQ), np.float32)
    tables[0, : LARGEST_LAG + 1, :BINS] = weights * np.cos(phases)
    tables[1, : LARGEST_LAG + 1, :BINS] = -weights * np.sin(phases)
    return tables.astype(jnp.bfloat16)


def dot(a, b):
    return jnp.dot(a, b, preferred_element_type=jnp.float32)


def clear_pad(samples):
    samples[...] = jnp.zeros(samples.shape, samples.dtype)


def whiten_pair(pieces, flags, samples, table_ref, sums_ref, band_ref, inverse_ref, spec):
    for g in range(2):
        for j in range(4):
            samples[pl.ds(j * PADDED, PIECE), g * HALF : (g + 1) * HALF] = pieces[g][j][...]
    x = samples[...]
    x = jnp.concatenate([x, x], axis=0)
    for i in range(4):
        rows = pl.ds(i * SHIFTS, SHIFTS)
        spec[rows, :] = dot(table_ref[rows, :], x)
    total = spec[0:1, :]
    sums = sums_ref[...]
    sums = jnp.concatenate([sums, sums], axis=1)
    real = spec[:FREQ] - sums[:FREQ] * total
    imag = spec[FREQ:] - sums[FREQ:] * total
    power = real * real + imag * imag
    power_high = power.astype(jnp.bfloat16)
    power_low = (power - power_high.astype(jnp.float32)).astype(jnp.bfloat16)
    power = jnp.concatenate([power_high, power_low], axis=0)
    smooth = jnp.concatenate([dot(band_ref[:SHIFTS], power), dot(band_ref[SHIFTS:], power)], axis=0)
    inverse = inverse_ref[...]
    inverse = jnp.concatenate([inverse, inverse], axis=1)
    scale = flags * lax.rsqrt(smooth * inverse + EPSILON)
    return real * scale, imag * scale


def whiten_sources_kernel(
    x_ref, flag_ref, table_ref, sums_ref, band_ref, inverse_ref, out_ref, samples, spec, held
):
    step = pl.program_id(0)

    @pl.when(step == 0)
    def _():
        clear_pad(samples)

    pieces = [[x_ref.at[g, j] for j in range(4)] for g in range(2)]
    flags = jnp.concatenate([flag_ref[0], flag_ref[1]], axis=1)
    real, imag = whiten_pair(pieces, flags, samples, table_ref, sums_ref, band_ref, inverse_ref, spec)
    for g in range(2):
        group = 2 * step + g
        first = pl.ds(group, FREQ, stride=SPITCH)
        second = pl.ds(SUB // 2 + group, FREQ, stride=SPITCH)
        own_real = real[:, g * HALF : (g + 1) * HALF]
        own_imag = imag[:, g * HALF : (g + 1) * HALF]
        held[0, first, :] = own_real
        held[0, second, :] = own_imag
        held[1, first, :] = -own_imag
        held[1, second, :] = own_real

    @pl.when(step == pl.num_programs(0) - 1)
    def _():
        low_lanes = lax.broadcasted_iota(jnp.int32, (SRC, HALF), 1) < HALF // 2

        @pl.loop(0, FREQ // 4)
        def _(quad):
            for part in range(2):
                rows = [
                    held[part, pl.ds(pl.multiple_of((4 * quad + i) * SPITCH, 8), SUB), :] for i in range(4)
                ]
                turned = jnp.concatenate(rows, axis=0).T
                first, second = turned[:SRC], turned[SRC:]
                pairs = (
                    jnp.where(low_lanes, first, pltpu.roll(second, HALF // 2, 1)),
                    jnp.where(low_lanes, pltpu.roll(first, HALF // 2, 1), second),
                )
                for i in range(2):
                    out_ref[2 * quad + i, part * SRC : (part + 1) * SRC] = pairs[i].astype(jnp.bfloat16)


def whole(shape):
    return pl.BlockSpec(shape, lambda *_: (0,) * len(shape))


def whiten_tables():
    return [jnp.asarray(table) for table in (*forward_table(), *band_table())]


def whiten_cost(groups):
    return pl.CostEstimate(
        flops=groups * 4 * 2 * FREQ * DEPTH * HALF, bytes_accessed=groups * DEPTH * HALF * 6, transcendentals=0
    )


def whiten_sources(x, flags):
    tables = whiten_tables()
    return pl.pallas_call(
        whiten_sources_kernel,
        grid=(SUB // 4,),
        in_specs=[
            pl.BlockSpec((2, 4, PIECE, HALF), lambda g: (g, 0, 0, 0)),
            pl.BlockSpec((2, 1, HALF), lambda g: (g, 0, 0)),
        ]
        + [whole(table.shape) for table in tables],
        out_specs=whole((FREQ // 2, ROWS, HALF)),
        out_shape=jax.ShapeDtypeStruct((FREQ // 2, ROWS, HALF), jnp.bfloat16),
        scratch_shapes=[
            pltpu.VMEM((DEPTH, 2 * HALF), jnp.bfloat16),
            pltpu.VMEM((2 * FREQ, 2 * HALF), jnp.float32),
            pltpu.VMEM((2, FREQ * SPITCH, HALF), jnp.float32),
        ],
        compiler_params=pltpu.CompilerParams(vmem_limit_bytes=VMEM),
        cost_estimate=whiten_cost(SUB // 2),
    )(x, flags, *tables)


def lag_sums(real_ref, imag_ref, tables_ref, even, odd):
    for pair in range(BLOCK // 2):
        real = jnp.concatenate([real_ref[2 * pair], real_ref[2 * pair + 1]], axis=1)
        imag = jnp.concatenate([imag_ref[2 * pair], imag_ref[2 * pair + 1]], axis=1)
        cosine = dot(tables_ref[0], real)
        sine = dot(tables_ref[1], imag)
        for i in range(2):
            rows = pl.ds(2 * pair + i, SHIFTS, stride=BLOCK)
            even[rows, :] = cosine[:, i * HALF : (i + 1) * HALF]
            odd[rows, :] = sine[:, i * HALF : (i + 1) * HALF]


def shift_rows(m):
    return pl.ds(pl.multiple_of(m * BLOCK, BLOCK), BLOCK)


def stack_kernel(
    place_ref,
    x_ref,
    flag_ref,
    table_ref,
    sums_ref,
    band_ref,
    inverse_ref,
    tables_ref,
    count_ref,
    left_hbm,
    away_ref,
    own_hbm,
    samples,
    spec,
    held,
    left_ref,
    spectra,
    products,
    even,
    odd,
    sems,
):
    step = pl.program_id(0)
    core = place_ref[0]
    inner = lax.rem(place_ref[1], PAIRS)
    left_copy = pltpu.make_async_copy(left_hbm, left_ref, sems.at[0])

    @pl.when(step == 0)
    def _():
        left_copy.start()
        clear_pad(samples)

    for p in range(PAIRS):
        source = lax.bitwise_xor(p, inner)
        pieces = [[x_ref.at[source, g, j] for j in range(4)] for g in range(2)]
        flags = jnp.concatenate([flag_ref[p, 0], flag_ref[p, 1]], axis=1)
        real, imag = whiten_pair(
            pieces, flags, samples.at[p % 2], table_ref, sums_ref, band_ref, inverse_ref, spec.at[p % 2]
        )
        for g in range(2):
            row = g * SUB + step * PAIRS + p
            held[pl.ds(row, FREQ, stride=PITCH), :] = real[:, g * HALF : (g + 1) * HALF]
            held[pl.ds(row + SUB // 2, FREQ, stride=PITCH), :] = imag[:, g * HALF : (g + 1) * HALF]

    @pl.when(step == pl.num_programs(0) - 1)
    def _():
        left_copy.wait()
        zeros = jnp.zeros((2 * SUB, HALF), jnp.bfloat16)

        def receivers(f):
            return held[pl.ds(pl.multiple_of(f * PITCH, 8), 2 * SUB), :].astype(jnp.bfloat16)

        @pl.loop(0, FREQ // (2 * BLOCK))
        def _(outer):
            for side in range(2):
                block = 2 * outer + side
                for pair in range(BLOCK // 2):
                    f = block * BLOCK + 2 * pair
                    first = jnp.concatenate([receivers(f), zeros], axis=1)
                    second = jnp.concatenate([zeros, receivers(f + 1)], axis=1)
                    weights = jnp.concatenate([first[:SUB], second[:SUB], first[SUB:], second[SUB:]], axis=0)
                    product = dot(left_ref[block * (BLOCK // 2) + pair], weights)
                    products[side, pl.ds(2 * pair * XPITCH, ROWS), :] = product[:, :HALF]
                    products[side, pl.ds((2 * pair + 1) * XPITCH, ROWS), :] = product[:, HALF:]
                bins = pl.ds(pl.multiple_of(block * BLOCK, BLOCK), BLOCK)
                for row in range(ROWS):
                    spectra[row, bins, :] = products[side, pl.ds(row, BLOCK, stride=XPITCH), :].astype(jnp.bfloat16)

        copies = [
            pltpu.make_async_copy(
                spectra.at[pl.ds(part * SRC + core * OWN, OWN)], own_hbm.at[pl.ds(part * OWN, OWN)], sems.at[1 + part]
            )
            for part in range(2)
        ]
        for copy in copies:
            copy.start()
        for g in range(OWN // BLOCK):
            first = (1 - core) * OWN + g * BLOCK
            lag_sums(
                spectra.at[pl.ds(first, BLOCK)], spectra.at[pl.ds(SRC + first, BLOCK)], tables_ref, even, odd
            )
            count = count_ref[pl.ds(pl.multiple_of(first, BLOCK), BLOCK), :]

            @pl.loop(0, LARGEST_LAG + 1, unroll=3)
            def _(m):
                e, o = even[shift_rows(m), :], odd[shift_rows(m), :]
                sources = pl.ds(g * BLOCK, BLOCK)
                away_ref[LARGEST_LAG + m, sources, :] = ((e + o) * count).astype(jnp.bfloat16)
                away_ref[LARGEST_LAG - m, sources, :] = ((e - o) * count).astype(jnp.bfloat16)

        for copy in copies:
            copy.wait()


def stack_partner(place, x, flags, left, inverse_count):
    tables = whiten_tables() + [jnp.asarray(lag_tables()), inverse_count]
    return pl.pallas_call(
        stack_kernel,
        grid_spec=pltpu.PrefetchScalarGridSpec(
            num_scalar_prefetch=1,
            grid=(SUB // 2 // PAIRS,),
            in_specs=[
                pl.BlockSpec(
                    (None, PAIRS, 2, 4, PIECE, HALF),
                    lambda g, place: (lax.bitwise_xor(g, lax.div(place[1], PAIRS)), 0, 0, 0, 0, 0),
                ),
                pl.BlockSpec((PAIRS, 2, 1, HALF), lambda g, place: (g, 0, 0, 0)),
            ]
            + [whole(table.shape) for table in tables]
            + [pl.BlockSpec(memory_space=pl.ANY)],
            out_specs=[whole((LAGS, OWN, HALF)), pl.BlockSpec(memory_space=pl.ANY)],
            scratch_shapes=[
                pltpu.VMEM((2, DEPTH, 2 * HALF), jnp.bfloat16),
                pltpu.VMEM((2, 2 * FREQ, 2 * HALF), jnp.float32),
                pltpu.VMEM((FREQ * PITCH, HALF), jnp.float32),
                pltpu.VMEM(left.shape, left.dtype),
                pltpu.VMEM((ROWS, FREQ, HALF), jnp.bfloat16),
                pltpu.VMEM((2, BLOCK * XPITCH, HALF), jnp.float32),
                pltpu.VMEM((SHIFTS * BLOCK, HALF), jnp.float32),
                pltpu.VMEM((SHIFTS * BLOCK, HALF), jnp.float32),
                pltpu.SemaphoreType.DMA((3,)),
            ],
        ),
        out_shape=[
            jax.ShapeDtypeStruct((LAGS, OWN, HALF), jnp.bfloat16),
            jax.ShapeDtypeStruct((2 * OWN, FREQ, HALF), jnp.bfloat16),
        ],
        compiler_params=pltpu.CompilerParams(vmem_limit_bytes=VMEM),
        cost_estimate=pl.CostEstimate(flops=30 * 10**9, bytes_accessed=24 << 20, transcendentals=0),
    )(place, x, flags, *tables, left)


def lag_own_kernel(place_ref, real_ref, imag_ref, tables_ref, count_ref, old_ref, out_ref, even, odd):
    lag_sums(real_ref, imag_ref, tables_ref, even, odd)

    @pl.loop(0, LARGEST_LAG + 1, unroll=8)
    def _(m):
        e, o = even[shift_rows(m), :], odd[shift_rows(m), :]
        above, below = LARGEST_LAG + m, LARGEST_LAG - m
        out_ref[above] = old_ref[above].astype(jnp.float32) + (e + o) * count_ref[...]
        out_ref[below] = old_ref[below].astype(jnp.float32) + (e - o) * count_ref[...]


def stack_own(place, spectra, inverse_count, old):
    steps = OWN // BLOCK
    tables = lag_tables()
    return pl.pallas_call(
        lag_own_kernel,
        grid_spec=pltpu.PrefetchScalarGridSpec(
            num_scalar_prefetch=1,
            grid=(steps,),
            in_specs=[
                pl.BlockSpec((BLOCK, FREQ, HALF), lambda g, place: (g, 0, 0)),
                pl.BlockSpec((BLOCK, FREQ, HALF), lambda g, place: (steps + g, 0, 0)),
                whole(tables.shape),
                pl.BlockSpec((BLOCK, HALF), lambda g, place: (place[0] * steps + g, 0)),
                pl.BlockSpec((LAGS, BLOCK, HALF), lambda g, place: (0, g, place[0])),
            ],
            out_specs=pl.BlockSpec((LAGS, BLOCK, HALF), lambda g, place: (0, g, place[0])),
            scratch_shapes=[pltpu.VMEM((SHIFTS * BLOCK, HALF), jnp.float32)] * 2,
        ),
        out_shape=jax.ShapeDtypeStruct((LAGS, OWN, 2 * HALF), jnp.float32),
        compiler_params=pltpu.CompilerParams(vmem_limit_bytes=VMEM),
        cost_estimate=pl.CostEstimate(flops=OWN * SHIFTS * FREQ * HALF * 4, bytes_accessed=16 << 20, transcendentals=0),
    )(place, spectra, spectra, jnp.asarray(tables), inverse_count, old)


def merge_kernel(place_ref, held_ref, got_ref, old_ref, out_ref):
    out_ref[...] = old_ref[...].astype(jnp.float32) + got_ref[...].astype(jnp.float32)


def merge(place, stacks, got, old):
    rows = 201
    spec = pl.BlockSpec((rows, OWN, HALF), lambda l, place: (l, 0, 1 - place[0]))
    return pl.pallas_call(
        merge_kernel,
        grid_spec=pltpu.PrefetchScalarGridSpec(
            num_scalar_prefetch=1,
            grid=(pl.cdiv(LAGS, rows),),
            in_specs=[
                pl.BlockSpec(memory_space=pl.ANY),
                pl.BlockSpec((rows, OWN, HALF), lambda l, place: (l, 0, 0)),
                spec,
            ],
            out_specs=spec,
        ),
        out_shape=jax.ShapeDtypeStruct(stacks.shape, stacks.dtype),
        input_output_aliases={1: 0},
        compiler_params=pltpu.CompilerParams(vmem_limit_bytes=VMEM),
        cost_estimate=pl.CostEstimate(flops=LAGS * OWN * HALF, bytes_accessed=13 << 20, transcendentals=0),
    )(place, stacks, got, old)


def outgoing_kernel(record_ref, out_ref):
    for i in range(out_ref.shape[0]):
        for core in range(2):
            column = (2 * i + core) * HALF
            piece = record_ref[:, column : column + HALF]
            for chip in range(2):
                out_ref[i, chip, core] = piece


def outgoing(record):
    blocks = record.shape[1] // (2 * HALF)
    steps = 4
    pieces = pl.pallas_call(
        outgoing_kernel,
        grid=(steps,),
        in_specs=[pl.BlockSpec((PIECE, record.shape[1] // steps), lambda i: (0, i))],
        out_specs=pl.BlockSpec((blocks // steps, 2, 2, PIECE, HALF), lambda i: (i, 0, 0, 0, 0)),
        out_shape=jax.ShapeDtypeStruct((blocks, 2, 2, PIECE, HALF), record.dtype),
        compiler_params=pltpu.CompilerParams(vmem_limit_bytes=VMEM),
        cost_estimate=pl.CostEstimate(flops=0, bytes_accessed=5 << 20, transcendentals=0),
    )(record)
    return pieces.reshape(4 * blocks, PIECE, HALF)


def device(x, y, z_low, z_high, core):
    return ((x * 4 + y) * 2 + z_low) * 4 + z_high * 2 + core


def send(value, route):
    places = [(x, y, l, h, c) for x in range(4) for y in range(4) for l in range(2) for h in range(2) for c in range(2)]
    return lax.ppermute(value, ("rcv", "src"), [(device(*place), device(*route(*place))) for place in places])


def near_sources(record, z_low, z_high):
    near = record[:, : 2 * SRC]
    same = jnp.where(z_high == 0, near[:, :SRC], near[:, SRC:])
    other = jnp.where(z_high == 0, near[:, SRC:], near[:, :SRC])
    low = send(same, lambda x, y, l, h, c: (x, y, 1 - l, h, c))
    high = send(other, lambda x, y, l, h, c: (x, y, l, 1 - h, c))
    both = send(other, lambda x, y, l, h, c: (x, y, 1 - l, 1 - h, c))

    def windows(mine, theirs):
        return jnp.where(z_low == 0, jnp.concatenate([mine, theirs], 1), jnp.concatenate([theirs, mine], 1))

    mine, theirs = windows(same, low), windows(high, both)
    return jnp.where(z_high == 0, jnp.stack([mine, theirs]), jnp.stack([theirs, mine]))


def plane_sources(near):
    column = jnp.stack([near] + [send(near, lambda x, y, l, h, c, d=d: (x, y ^ d, l, h, c)) for d in (1, 2, 3)])
    plane = jnp.stack([column] + [send(column, lambda x, y, l, h, c, d=d: (x ^ d, y, l, h, c)) for d in (1, 2, 3)])
    return plane.reshape(SUB // 2, 2, PIECE, HALF)


def both_cores(plane, core):
    other = send(plane, lambda x, y, l, h, c: (x, y, l, h, 1 - c))
    rows = jnp.where(core == 0, jnp.stack([plane, other], axis=2), jnp.stack([other, plane], axis=2))
    return rows.reshape(SUB // 2, 4, PIECE, HALF)


def on_device(record, quality, keep_flags, old_stacks):
    row = lax.axis_index("rcv")
    col = lax.axis_index("src")
    core = lax.rem(col, 2)
    chip = lax.div(col, 2)
    z_low = lax.rem(row, 2)
    group = lax.div(row, 2)
    place = jnp.stack([core, group]).astype(jnp.int32)

    pieces = outgoing(record)
    plane = plane_sources(near_sources(record, z_low, chip))
    plane, pieces = lax.optimization_barrier((plane, pieces))
    receivers = lax.all_to_all(pieces, ("rcv", "src"), split_axis=0, concat_axis=0, tiled=True)
    sources = both_cores(plane, core)

    keep_all = keep_flags.astype(jnp.float32)
    flags = keep_all * quality.astype(jnp.float32)[None, :]
    first_receiver = row * 2 * HALF + core * HALF
    keep_src = lax.dynamic_slice_in_dim(keep_all, chip * SRC, SRC, 1)
    keep_rcv = lax.dynamic_slice_in_dim(keep_all, first_receiver, HALF, 1)
    inverse_count = 1.0 / jnp.maximum(dot(keep_src.T, keep_rcv), 1.0)
    order = lax.bitwise_xor(jnp.arange(SUB // 2, dtype=jnp.int32), group.astype(jnp.int32))
    flags_src = lax.dynamic_slice_in_dim(flags, chip * SRC, SRC, 1).reshape(SUB // 2, 1, 2 * SRC)[order]
    flags_rcv = lax.dynamic_slice_in_dim(flags, first_receiver, HALF, 1).reshape(SUB // 2, 2, HALF)[order]

    left = whiten_sources(sources, flags_src)
    receivers = receivers.reshape(SUB // 2 // PAIRS, PAIRS, 2, 4, PIECE, HALF)
    flags_rcv = flags_rcv.reshape(SUB // 2, 2, 1, HALF)
    away, spectra = stack_partner(place, receivers, flags_rcv, left, inverse_count)
    got = lax.ppermute(away, "src", [(0, 1), (1, 0), (2, 3), (3, 2)])
    stacks = stack_own(place, spectra, inverse_count, old_stacks)
    return merge(place, stacks, got, old_stacks)


def solution(mesh):
    return jax.shard_map(
        on_device,
        mesh=mesh,
        in_specs=(P(("rcv", "src"), None), P(), P(), P(None, "src", "rcv")),
        out_specs=P(None, "src", "rcv"),
        check_vma=False,
    )
```

time: 176 us -> 136 us (0.77)
  Pallas kernels: 118 us -> 89.1 us
  local copies, waits for them, and re-layouts: 16.1 us -> 6.08 us
    pallas_call x4 -> x3, Pallas kernels: 73.1 us -> 49.1 us  [the longest x1 35.6 us: stack_partner(): pl.pallas_call(stack_kernel, grid_spec=pltpu.PrefetchScalarGridSpec(num_s...]
    reshape x1 -> x0, local copies, waits for them, and re-layouts: 4.58 us -> none  [on_device(): pieces = pieces.reshape(PADDED, blocks, 1, 2, HALF).transpose(1, 2, 3, 0, 4)]
    broadcast_in_dim x2 -> x0, local copies, waits for them, and re-layouts: 4.55 us -> none  [on_device(): jnp.broadcast_to(pieces, (blocks, 2, 2, PADDED, HALF))]
    pallas_call x1, Pallas kernels: 8.82 us -> 5.73 us  [merge(): pl.pallas_call(merge_kernel, grid_spec=pltpu.PrefetchScalarGridSpec(num_s...]
    pad x1 -> x0, local copies, waits for them, and re-layouts: 2.85 us -> none  [on_device(): pieces = jnp.pad(record, ((0, PADDED - PIECE), (0, 0)))]
    ppermute x10, waiting for transfers between devices: 9.21 us -> 11.2 us  [send(): lax.ppermute(value, ('rcv', 'src'), [(device(*place), device(*route(*plac...]
  transfers between devices with their start and end apart: 12 -> 12, of which waited for: 6 -> 7; matrix products, arithmetic and copies ran while one was open for 10% -> 6% of each run, Pallas kernels for 27% -> 36%
where the time goes in v3:
time: 136 us; the launch traced here: 135 us
  Pallas kernels  89.1 us (66%)
  starting transfers between devices  21.2 us (16%)
  waiting for transfers between devices  13.4 us (10%)
  local copies, waits for them, and re-layouts  6.08 us (4%)
  other arithmetic  3.72 us (3%)
    pallas_call x1, Pallas kernels, stack_partner(): pl.pallas_call(stack_kernel, grid_spec=pltpu.PrefetchScalarGridSpec(num_s...  35.6 us
    pallas_call x1, Pallas kernels, whiten_sources(): pl.pallas_call(whiten_sources_kernel, grid=(SUB // 4,), in_specs=[pl.Bloc...  34.3 us
    ppermute x10, starting transfers between devices, send(): lax.ppermute(value, ('rcv', 'src'), [(device(*place), device(*route(*plac...  14.4 us
    ppermute x10, waiting for transfers between devices, send(): lax.ppermute(value, ('rcv', 'src'), [(device(*place), device(*route(*plac...  11.2 us
    pallas_call x1, Pallas kernels, stack_own(): pl.pallas_call(lag_own_kernel, grid_spec=pltpu.PrefetchScalarGridSpec(num...  9.41 us
    all_to_all x1, starting transfers between devices, on_device(): lax.all_to_all(pieces, ('rcv', 'src'), split_axis=0, concat_axis=0, tiled...  6.77 us
    pallas_call x1, Pallas kernels, merge(): pl.pallas_call(merge_kernel, grid_spec=pltpu.PrefetchScalarGridSpec(num_s...  5.73 us
    pallas_call x1, Pallas kernels, outgoing(): pl.pallas_call(outgoing_kernel, grid=(steps,), in_specs=[pl.BlockSpec((PI...  4.07 us
  transfers between devices with their start and end apart: 12, of which 7 were waited for; matrix products, arithmetic and copies ran while one was open for 6% of the time, Pallas kernels for 36%

profile of v3, /device:TPU:0, one launch (start us, length us, event | category | flops | bytes accessed | tf_op | source)
XLA Modules:
  0.0 134.5 jit_solution(16980143409527362732)
XLA Ops:
  0.0 0.9 broadcast_select_fusion.1
  0.9 2.1 %collective-permute-start = (bf16[100,64]{1,0:T(8,128)(2,1)S(1)}, bf16[100,64]{1,0:T(8,128)(2,1)S(1)}, u32[]{:S(2)}, u32[]{:S(2)}) collective-permute-start(bf16[100,64]{1,0:T(8,128)(2,1)S(1)} %get-tuple-element.13), channel_id=1, source_target_pairs={{0,4},{1,5},{2,6},{3,7},{4,0},{5,1},{6,2},{7,3},{8,12},{9,13},{10,... | collective-permute-start | bytes 38408 | tf_op jit(solution)/shard_map/ppermute | solution.py:429
  3.0 2.5 %collective-permute-start.2 = (bf16[100,64]{1,0:T(8,128)(2,1)S(1)}, bf16[100,64]{1,0:T(8,128)(2,1)S(1)}, u32[]{:S(2)}, u32[]{:S(2)}) collective-permute-start(bf16[100,64]{1,0:T(8,128)(2,1)S(1)} %get-tuple-element.14), channel_id=1, source_target_pairs={{0,6},{1,7},{2,4},{3,5},{4,2},{5,3},{6,0},{7,1},{8,14},{9,15},{10,... | collective-permute-start | bytes 38408 | tf_op jit(solution)/shard_map/ppermute | solution.py:429
  5.5 1.1 collective-permute-start.1
  6.6 0.0 collective-permute-done
  6.6 0.1 maximum_select_fusion.3
  6.7 1.4 %collective-permute-done.2 = bf16[100,64]{1,0:T(8,128)(2,1)S(1)} collective-permute-done((bf16[100,64]{1,0:T(8,128)(2,1)S(1)}, bf16[100,64]{1,0:T(8,128)(2,1)S(1)}, u32[]{:S(2)}, u32[]{:S(2)}) %collective-permute-start.2) | collective-permute-done | bytes 12832 | tf_op jit(solution)/shard_map/ppermute | solution.py:429
  8.0 2.8 %collective-permute-done.1 = bf16[100,64]{1,0:T(8,128)(2,1)S(1)} collective-permute-done((bf16[100,64]{1,0:T(8,128)(2,1)S(1)}, bf16[100,64]{1,0:T(8,128)(2,1)S(1)}, u32[]{:S(2)}, u32[]{:S(2)}) %collective-permute-start.1) | collective-permute-done | bytes 12832 | tf_op jit(solution)/shard_map/ppermute | solution.py:429
  10.9 0.1 maximum_select_fusion.4
  11.0 3.1 %collective-permute-start.5 = (bf16[2,100,128]{2,1,0:T(8,128)(2,1)S(1)}, bf16[2,100,128]{2,1,0:T(8,128)(2,1)S(1)}, u32[]{:S(2)}, u32[]{:S(2)}) collective-permute-start(bf16[2,100,128]{2,1,0:T(8,128)(2,1)S(1)} %maximum_select_fusion.2), channel_id=1, source_target_pairs={{0,24},{1,25},{2,26},{3,27},{4,28},{5,29},{6,30},{7,31},{8,16},{9,... | collective-permute-start | bytes 153608 | tf_op jit(solution)/shard_map/ppermute | solution.py:429
  14.1 0.6 collective-permute-start.4
  14.7 0.5 collective-permute-start.3
  15.2 1.8 %collective-permute-done.5 = bf16[2,100,128]{2,1,0:T(8,128)(2,1)S(1)} collective-permute-done((bf16[2,100,128]{2,1,0:T(8,128)(2,1)S(1)}, bf16[2,100,128]{2,1,0:T(8,128)(2,1)S(1)}, u32[]{:S(2)}, u32[]{:S(2)}) %collective-permute-start.5) | collective-permute-done | bytes 51232 | tf_op jit(solution)/shard_map/ppermute | solution.py:429
  17.0 2.7 %collective-permute-done.4 = bf16[2,100,128]{2,1,0:T(8,128)(2,1)S(1)} collective-permute-done((bf16[2,100,128]{2,1,0:T(8,128)(2,1)S(1)}, bf16[2,100,128]{2,1,0:T(8,128)(2,1)S(1)}, u32[]{:S(2)}, u32[]{:S(2)}) %collective-permute-start.4) | collective-permute-done | bytes 51232 | tf_op jit(solution)/shard_map/ppermute | solution.py:429
  19.7 0.0 collective-permute-done.3
  19.8 3.1 %collective-permute-start.7 = (bf16[4,2,100,128]{3,2,1,0:T(8,128)(2,1)S(1)}, bf16[4,2,100,128]{3,2,1,0:T(8,128)(2,1)S(1)}, u32[]{:S(2)}, u32[]{:S(2)}) collective-permute-start(bf16[4,2,100,128]{3,2,1,0:T(8,128)(2,1)S(1)} %get-tuple-element.16), channel_id=1, source_target_pairs={{0,64},{1,65},{2,66},{3,67},{4,68},{5,69},{6,70},{7,71},{8,72},{9,... | collective-permute-start | bytes 614408 | tf_op jit(solution)/shard_map/ppermute | solution.py:429
  22.9 0.6 collective-permute-start.6
  23.5 0.6 collective-permute-start.8
  24.0 4.1 %shard_map.136 = bf16[32,2,2,100,128]{4,3,2,1,0:T(8,128)(2,1)} custom-call(bf16[100,8192]{1,0:T(8,128)(2,1)} %record_ref.1), custom_call_target="tpu_custom_call" | custom-call | bytes 5242880 | tf_op jit(solution)/shard_map/pallas_call | solution.py:411
  28.1 0.0 collective-permute-done.7
  28.1 1.9 %collective-permute-done.6 = bf16[4,2,100,128]{3,2,1,0:T(8,128)(2,1)S(1)} collective-permute-done((bf16[4,2,100,128]{3,2,1,0:T(8,128)(2,1)S(1)}, bf16[4,2,100,128]{3,2,1,0:T(8,128)(2,1)S(1)}, u32[]{:S(2)}, u32[]{:S(2)}) %collective-permute-start.6) | collective-permute-done | bytes 204832 | tf_op jit(solution)/shard_map/ppermute | solution.py:429
  30.0 0.5 collective-permute-done.8
  30.5 0.1 pad_maximum_fusion
  30.6 0.3 copy.16
  31.0 0.0 copy-start.2
  31.0 0.0 copy-start
  31.0 6.8 %all-to-all-start = ((bf16[128,100,128]{2,1,0:T(8,128)(2,1)}), bf16[128,100,128]{2,1,0:T(8,128)(2,1)}, u32[]{:S(2)}, u32[]{:S(2)}) async-start(bf16[128,100,128]{2,1,0:T(8,128)(2,1)} %bitcast.27), calls=%async_computation | async-start | bytes 6815744 | tf_op jit(solution)/shard_map/all_to_all | solution.py:471
  37.8 0.0 copy-done.2
  37.8 0.3 collective-permute-start.9
  38.1 0.1 broadcast_multiply_fusion
  38.2 0.1 convert_element_type.6
  38.2 0.1 constant_dynamic-slice_fusion
  38.3 0.1 reshape.339
  38.4 1.1 gather_fusion.1
  39.6 1.2 gather_fusion
  40.7 0.7 pad_add_fusion.place_ref
  41.4 0.9 fusion.count_ref
  42.3 0.0 collective-permute-done.9
  42.3 1.6 %maximum_select_fusion = bf16[16,2,2,100,128]{4,0,3,1,2:T(8,128)(2,1)S(1)} fusion(bf16[16,2,1,100,128]{4,0,3,1,2:T(8,128)(2,1)} %bitcast.22, bf16[16,2,1,100,128]{4,0,3,1,2:T(8,128)(2,1)S(1)} %bitcast.30, pred[]{:T(512)S(6)} %eq.14), kind=kLoop, calls=%fused_computation.2 | loop fusion | flops 2457600 | bytes 3276801 | tf_op jit(solution)/shard_map/jit(_where)/select_n | solution.py:455
  43.9 1.6 %copy.17 = bf16[16,2,2,100,128]{4,3,2,1,0:T(8,128)(2,1)} copy(bf16[16,2,2,100,128]{4,0,3,1,2:T(8,128)(2,1)S(1)} %maximum_select_fusion) | data formatting | bytes 3276800 | tf_op jit(solution)/shard_map/jit(_where)/select_n | solution.py:455
  45.5 34.3 %shard_map.137.left_hbm = bf16[208,128,128]{2,1,0:T(8,128)(2,1)} custom-call(bf16[16,4,100,128]{3,2,1,0:T(8,128)(2,1)} %bitcast.28, f32[16,1,128]{2,1,0:T(1,128)} %bitcast.41, bf16[832,896]{1,0:T(8,128)(2,1)} %constant.44.clone.table_ref, f32[832,128]{1,0:T(8,128)} %constant.45.clone.sums_ref, bf16[416,832]{1,0:T(8,128)(2,1)} %constant.46.clone.band_ref, ...), custom_call_target="tpu_custom_call" | custom-call | flops 3053453312 | bytes 5505024 | tf_op jit(solution)/shard_map/pallas_call | solution.py:169
  79.8 2.2 %all-to-all-done = bf16[128,100,128]{2,1,0:T(8,128)(2,1)} async-done(((bf16[128,100,128]{2,1,0:T(8,128)(2,1)}), bf16[128,100,128]{2,1,0:T(8,128)(2,1)}, u32[]{:S(2)}, u32[]{:S(2)}) %all-to-all-start) | async-done | bytes 3276832 | tf_op jit(solution)/shard_map/all_to_all | solution.py:471
  82.0 35.6 %shard_map.138 = (bf16[401,32,128]{2,1,0:T(8,128)(2,1)}, bf16[64,416,128]{2,1,0:T(8,128)(2,1)}) custom-call(s32[2]{0:T(128)} %pad_add_fusion.place_ref, bf16[4,4,2,4,100,128]{5,4,3,2,1,0:T(8,128)(2,1)} %bitcast.17.x_ref, f32[16,2,1,128]{3,2,1,0:T(1,128)} %bitcast.45, bf16[832,896]{1,0:T(8,128)(2,1)} %constant.44.clone.table_ref, ...), custom_call_target="tpu_custom_call" | custom-call | flops 30000001024 | bytes 25165824 | tf_op jit(solution)/shard_map/pallas_call | solution.py:302
  117.6 0.1 collective-permute-start.10
  117.7 9.4 %shard_map.139.held_ref = f32[401,32,256]{2,1,0:T(8,128)} custom-call(s32[2]{0:T(128)} %pad_add_fusion.place_ref, bf16[64,416,128]{2,1,0:T(8,128)(2,1)} %get-tuple-element.11.real_ref.imag_ref, bf16[64,416,128]{2,1,0:T(8,128)(2,1)} %get-tuple-element.11.real_ref.imag_ref, bf16[2,208,416]{2,1,0:T(8,128)(2,1)} %constant.48.clone.tables_ref, ...), custom_call_target="tpu_custom_call" | custom-call | flops 1417674752 | bytes 16777216 | tf_op jit(solution)/shard_map/pallas_call | solution.py:352
  127.1 0.0 collective-permute-done.10.got_ref
  127.1 1.7 %copy-done.1 = bf16[401,32,128]{2,1,0:T(8,128)(2,1)} copy-done((bf16[401,32,128]{2,1,0:T(8,128)(2,1)}, bf16[401,32,128]{2,1,0:T(8,128)(2,1)S(1)}, u32[]{:S(2)}) %copy-start.1) | copy-done | bytes 3285016
  128.8 5.7 %shard_map.140 = f32[401,32,256]{2,1,0:T(8,128)} custom-call(s32[2]{0:T(128)} %pad_add_fusion.place_ref, f32[401,32,256]{2,1,0:T(8,128)} %shard_map.139.held_ref, bf16[401,32,128]{2,1,0:T(8,128)(2,1)} %copy-done.1, bf16[401,32,256]{2,1,0:T(8,128)(2,1)} %old_ref.3), custom_call_target="tpu_custom_call", output_to_operand_aliasing={{}: (1, {})} | custom-call | flops 1642496 | bytes 13631488 | tf_op jit(solution)/shard_map/pallas_call | solution.py:380
  (9 shorter events, 0.1 us)
Async XLA Ops:
  0.9 5.7 %collective-permute-start = (bf16[100,64]{1,0:T(8,128)(2,1)S(1)}, bf16[100,64]{1,0:T(8,128)(2,1)S(1)}, u32[]{:S(2)}, u32[]{:S(2)}) collective-permute-start(bf16[100,64]{1,0:T(8,128)(2,1)S(1)} %get-tuple-element.13), channel_id=1, source_target_pairs={{0,4},{1,5},{2,6},{3,7},{4,0},{5,1},{6,2},{7,3},{8,12},{9,13},{10,... | collective-permute-start | bytes 38408 | tf_op jit(solution)/shard_map/ppermute | solution.py:429
  3.0 5.1 %collective-permute-start.2 = (bf16[100,64]{1,0:T(8,128)(2,1)S(1)}, bf16[100,64]{1,0:T(8,128)(2,1)S(1)}, u32[]{:S(2)}, u32[]{:S(2)}) collective-permute-start(bf16[100,64]{1,0:T(8,128)(2,1)S(1)} %get-tuple-element.14), channel_id=1, source_target_pairs={{0,6},{1,7},{2,4},{3,5},{4,2},{5,3},{6,0},{7,1},{8,14},{9,15},{10,... | collective-permute-start | bytes 38408 | tf_op jit(solution)/shard_map/ppermute | solution.py:429
  5.5 5.4 %collective-permute-start.1 = (bf16[100,64]{1,0:T(8,128)(2,1)S(1)}, bf16[100,64]{1,0:T(8,128)(2,1)S(1)}, u32[]{:S(2)}, u32[]{:S(2)}) collective-permute-start(bf16[100,64]{1,0:T(8,128)(2,1)S(1)} %get-tuple-element.14), channel_id=1, source_target_pairs={{0,2},{1,3},{2,0},{3,1},{4,6},{5,7},{6,4},{7,5},{8,10},{9,11},{10,... | collective-permute-start | bytes 38408 | tf_op jit(solution)/shard_map/ppermute | solution.py:429
  11.0 6.0 %collective-permute-start.5 = (bf16[2,100,128]{2,1,0:T(8,128)(2,1)S(1)}, bf16[2,100,128]{2,1,0:T(8,128)(2,1)S(1)}, u32[]{:S(2)}, u32[]{:S(2)}) collective-permute-start(bf16[2,100,128]{2,1,0:T(8,128)(2,1)S(1)} %maximum_select_fusion.2), channel_id=1, source_target_pairs={{0,24},{1,25},{2,26},{3,27},{4,28},{5,29},{6,30},{7,31},{8,16},{9,... | collective-permute-start | bytes 153608 | tf_op jit(solution)/shard_map/ppermute | solution.py:429
  14.1 5.6 %collective-permute-start.4 = (bf16[2,100,128]{2,1,0:T(8,128)(2,1)S(1)}, bf16[2,100,128]{2,1,0:T(8,128)(2,1)S(1)}, u32[]{:S(2)}, u32[]{:S(2)}) collective-permute-start(bf16[2,100,128]{2,1,0:T(8,128)(2,1)S(1)} %maximum_select_fusion.2), channel_id=1, source_target_pairs={{0,16},{1,17},{2,18},{3,19},{4,20},{5,21},{6,22},{7,23},{8,24},{9,... | collective-permute-start | bytes 153608 | tf_op jit(solution)/shard_map/ppermute | solution.py:429
  14.7 5.0 %collective-permute-start.3 = (bf16[2,100,128]{2,1,0:T(8,128)(2,1)S(1)}, bf16[2,100,128]{2,1,0:T(8,128)(2,1)S(1)}, u32[]{:S(2)}, u32[]{:S(2)}) collective-permute-start(bf16[2,100,128]{2,1,0:T(8,128)(2,1)S(1)} %maximum_select_fusion.2), channel_id=1, source_target_pairs={{0,8},{1,9},{2,10},{3,11},{4,12},{5,13},{6,14},{7,15},{8,0},{9,1},... | collective-permute-start | bytes 153608 | tf_op jit(solution)/shard_map/ppermute | solution.py:429
  19.8 8.3 %collective-permute-start.7 = (bf16[4,2,100,128]{3,2,1,0:T(8,128)(2,1)S(1)}, bf16[4,2,100,128]{3,2,1,0:T(8,128)(2,1)S(1)}, u32[]{:S(2)}, u32[]{:S(2)}) collective-permute-start(bf16[4,2,100,128]{3,2,1,0:T(8,128)(2,1)S(1)} %get-tuple-element.16), channel_id=1, source_target_pairs={{0,64},{1,65},{2,66},{3,67},{4,68},{5,69},{6,70},{7,71},{8,72},{9,... | collective-permute-start | bytes 614408 | tf_op jit(solution)/shard_map/ppermute | solution.py:429
  22.9 7.1 %collective-permute-start.6 = (bf16[4,2,100,128]{3,2,1,0:T(8,128)(2,1)S(1)}, bf16[4,2,100,128]{3,2,1,0:T(8,128)(2,1)S(1)}, u32[]{:S(2)}, u32[]{:S(2)}) collective-permute-start(bf16[4,2,100,128]{3,2,1,0:T(8,128)(2,1)S(1)} %get-tuple-element.16), channel_id=1, source_target_pairs={{0,32},{1,33},{2,34},{3,35},{4,36},{5,37},{6,38},{7,39},{8,40},{9,... | collective-permute-start | bytes 614408 | tf_op jit(solution)/shard_map/ppermute | solution.py:429
  23.5 7.1 %collective-permute-start.8 = (bf16[4,2,100,128]{3,2,1,0:T(8,128)(2,1)S(1)}, bf16[4,2,100,128]{3,2,1,0:T(8,128)(2,1)S(1)}, u32[]{:S(2)}, u32[]{:S(2)}) collective-permute-start(bf16[4,2,100,128]{3,2,1,0:T(8,128)(2,1)S(1)} %get-tuple-element.16), channel_id=1, source_target_pairs={{0,96},{1,97},{2,98},{3,99},{4,100},{5,101},{6,102},{7,103},{8,104... | collective-permute-start | bytes 614408 | tf_op jit(solution)/shard_map/ppermute | solution.py:429
  31.0 6.8 %copy-start.2 = (s32[8192]{0:T(1024)S(1)}, s32[8192]{0:T(1024)}, u32[]{:S(2)}) copy-start(s32[8192]{0:T(1024)} %param.15) | copy-start | bytes 98308
  31.0 7.1 %copy-start = (s32[32,8192]{1,0:T(8,128)S(1)}, s32[32,8192]{1,0:T(8,128)}, u32[]{:S(2)}) copy-start(s32[32,8192]{1,0:T(8,128)} %param.16) | copy-start | bytes 3145732
  31.0 51.1 %all-to-all-start = ((bf16[128,100,128]{2,1,0:T(8,128)(2,1)}), bf16[128,100,128]{2,1,0:T(8,128)(2,1)}, u32[]{:S(2)}, u32[]{:S(2)}) async-start(bf16[128,100,128]{2,1,0:T(8,128)(2,1)} %bitcast.27), calls=%async_computation | async-start | bytes 6815744 | tf_op jit(solution)/shard_map/all_to_all | solution.py:471
  37.8 4.5 %collective-permute-start.9 = (bf16[16,2,100,128]{3,0,2,1:T(8,128)(2,1)S(1)}, bf16[16,2,100,128]{3,0,2,1:T(8,128)(2,1)}, u32[]{:S(2)}, u32[]{:S(2)}) collective-permute-start(bf16[16,2,100,128]{3,0,2,1:T(8,128)(2,1)S(1)} %bitcast.29), channel_id=1, source_target_pairs={{0,1},{1,0},{2,3},{3,2},{4,5},{5,4},{6,7},{7,6},{8,9},{9,8},{10,11... | collective-permute-start | bytes 2457608 | tf_op jit(solution)/shard_map/ppermute | solution.py:429
  117.6 9.5 %collective-permute-start.10 = (bf16[401,32,128]{2,1,0:T(8,128)(2,1)}, bf16[401,32,128]{2,1,0:T(8,128)(2,1)S(1)}, u32[]{:S(2)}, u32[]{:S(2)}) collective-permute-start(bf16[401,32,128]{2,1,0:T(8,128)(2,1)} %get-tuple-element.12), channel_id=1, source_target_pairs={{0,1},{1,0},{2,3},{3,2},{4,5},{5,4},{6,7},{7,6},{8,9},{9,8},{10,11... | collective-permute-start | bytes 9854984 | tf_op jit(solution)/shard_map/ppermute | solution.py:488
  127.1 1.7 %copy-start.1 = (bf16[401,32,128]{2,1,0:T(8,128)(2,1)}, bf16[401,32,128]{2,1,0:T(8,128)(2,1)S(1)}, u32[]{:S(2)}) copy-start(bf16[401,32,128]{2,1,0:T(8,128)(2,1)S(1)} %collective-permute-done.10.got_ref) | copy-start | bytes 9854980

commit v4 on v3

--- a/solution.py
+++ b/solution.py
@@ -25,6 +25,7 @@
 HALF = 128
 SRC = 64
 OWN = 32
+REACH = 256
 SHIFTS = 208
 PITCH = 72
 SPITCH = 40
@@ -33,6 +34,7 @@
 BLOCK = 16
 PAIRS = 4
 VMEM = 56 * 1024 * 1024
+ADD_VMEM = 62 * 1024 * 1024
 
 
 def split(table):
@@ -60,7 +62,9 @@
     inside &= (bins[:, None] < BINS) & (bins[None, :] < BINS)
     counts = np.maximum(inside.sum(axis=1, keepdims=True), 1)
     inverse = np.broadcast_to((1.0 / (2.0 * counts)).astype(np.float32), (FREQ, HALF)).copy()
-    return np.concatenate([inside, inside], axis=1).astype(jnp.bfloat16), inverse
+    halves = np.stack([inside[:SHIFTS, :REACH], inside[SHIFTS:, FREQ - REACH :]])
+    assert halves.sum() == inside.sum()
+    return np.concatenate([halves, halves], axis=2).astype(jnp.bfloat16), inverse
 
 
 def lag_tables():
@@ -99,8 +103,13 @@
     power = real * real + imag * imag
     power_high = power.astype(jnp.bfloat16)
     power_low = (power - power_high.astype(jnp.float32)).astype(jnp.bfloat16)
-    power = jnp.concatenate([power_high, power_low], axis=0)
-    smooth = jnp.concatenate([dot(band_ref[:SHIFTS], power), dot(band_ref[SHIFTS:], power)], axis=0)
+    smooth = jnp.concatenate(
+        [
+            dot(band_ref[i], jnp.concatenate([part[first : first + REACH] for part in (power_high, power_low)], axis=0))
+            for i, first in enumerate((0, FREQ - REACH))
+        ],
+        axis=0,
+    )
     inverse = inverse_ref[...]
     inverse = jnp.concatenate([inverse, inverse], axis=1)
     scale = flags * lax.rsqrt(smooth * inverse + EPSILON)
@@ -214,7 +223,7 @@
     count_ref,
     left_hbm,
     away_ref,
-    own_hbm,
+    mine_ref,
     samples,
     spec,
     held,
@@ -223,12 +232,12 @@
     products,
     even,
     odd,
-    sems,
+    sem,
 ):
     step = pl.program_id(0)
     core = place_ref[0]
     inner = lax.rem(place_ref[1], PAIRS)
-    left_copy = pltpu.make_async_copy(left_hbm, left_ref, sems.at[0])
+    left_copy = pltpu.make_async_copy(left_hbm, left_ref, sem)
 
     @pl.when(step == 0)
     def _():
@@ -271,33 +280,23 @@
                 for row in range(ROWS):
                     spectra[row, bins, :] = products[side, pl.ds(row, BLOCK, stride=XPITCH), :].astype(jnp.bfloat16)
 
-        copies = [
-            pltpu.make_async_copy(
-                spectra.at[pl.ds(part * SRC + core * OWN, OWN)], own_hbm.at[pl.ds(part * OWN, OWN)], sems.at[1 + part]
-            )
-            for part in range(2)
-        ]
-        for copy in copies:
-            copy.start()
-        for g in range(OWN // BLOCK):
-            first = (1 - core) * OWN + g * BLOCK
-            lag_sums(
-                spectra.at[pl.ds(first, BLOCK)], spectra.at[pl.ds(SRC + first, BLOCK)], tables_ref, even, odd
-            )
-            count = count_ref[pl.ds(pl.multiple_of(first, BLOCK), BLOCK), :]
-
-            @pl.loop(0, LARGEST_LAG + 1, unroll=3)
-            def _(m):
-                e, o = even[shift_rows(m), :], odd[shift_rows(m), :]
-                sources = pl.ds(g * BLOCK, BLOCK)
-                away_ref[LARGEST_LAG + m, sources, :] = ((e + o) * count).astype(jnp.bfloat16)
-                away_ref[LARGEST_LAG - m, sources, :] = ((e - o) * count).astype(jnp.bfloat16)
-
-        for copy in copies:
-            copy.wait()
-
-
-def stack_partner(place, x, flags, left, inverse_count):
+        for half, out_ref in ((1 - core, away_ref), (core, mine_ref)):
+            for g in range(OWN // BLOCK):
+                first = half * OWN + g * BLOCK
+                lag_sums(
+                    spectra.at[pl.ds(first, BLOCK)], spectra.at[pl.ds(SRC + first, BLOCK)], tables_ref, even, odd
+                )
+                count = count_ref[pl.ds(pl.multiple_of(first, BLOCK), BLOCK), :]
+
+                @pl.loop(0, LARGEST_LAG + 1, unroll=8)
+                def _(m):
+                    e, o = even[shift_rows(m), :], odd[shift_rows(m), :]
+                    sources = pl.ds(g * BLOCK, BLOCK)
+                    out_ref[LARGEST_LAG + m, sources, :] = ((e + o) * count).astype(jnp.bfloat16)
+                    out_ref[LARGEST_LAG - m, sources, :] = ((e - o) * count).astype(jnp.bfloat16)
+
+
+def stack_halves(place, x, flags, left, inverse_count):
     tables = whiten_tables() + [jnp.asarray(lag_tables()), inverse_count]
     return pl.pallas_call(
         stack_kernel,
@@ -313,7 +312,7 @@
             ]
             + [whole(table.shape) for table in tables]
             + [pl.BlockSpec(memory_space=pl.ANY)],
-            out_specs=[whole((LAGS, OWN, HALF)), pl.BlockSpec(memory_space=pl.ANY)],
+            out_specs=[whole((LAGS, OWN, HALF))] * 2,
             scratch_shapes=[
                 pltpu.VMEM((2, DEPTH, 2 * HALF), jnp.bfloat16),
                 pltpu.VMEM((2, 2 * FREQ, 2 * HALF), jnp.float32),
@@ -323,77 +322,42 @@
                 pltpu.VMEM((2, BLOCK * XPITCH, HALF), jnp.float32),
                 pltpu.VMEM((SHIFTS * BLOCK, HALF), jnp.float32),
                 pltpu.VMEM((SHIFTS * BLOCK, HALF), jnp.float32),
-                pltpu.SemaphoreType.DMA((3,)),
+                pltpu.SemaphoreType.DMA,
             ],
         ),
-        out_shape=[
-            jax.ShapeDtypeStruct((LAGS, OWN, HALF), jnp.bfloat16),
-            jax.ShapeDtypeStruct((2 * OWN, FREQ, HALF), jnp.bfloat16),
-        ],
+        out_shape=[jax.ShapeDtypeStruct((LAGS, OWN, HALF), jnp.bfloat16)] * 2,
         compiler_params=pltpu.CompilerParams(vmem_limit_bytes=VMEM),
         cost_estimate=pl.CostEstimate(flops=30 * 10**9, bytes_accessed=24 << 20, transcendentals=0),
     )(place, x, flags, *tables, left)
 
 
-def lag_own_kernel(place_ref, real_ref, imag_ref, tables_ref, count_ref, old_ref, out_ref, even, odd):
-    lag_sums(real_ref, imag_ref, tables_ref, even, odd)
-
-    @pl.loop(0, LARGEST_LAG + 1, unroll=8)
-    def _(m):
-        e, o = even[shift_rows(m), :], odd[shift_rows(m), :]
-        above, below = LARGEST_LAG + m, LARGEST_LAG - m
-        out_ref[above] = old_ref[above].astype(jnp.float32) + (e + o) * count_ref[...]
-        out_ref[below] = old_ref[below].astype(jnp.float32) + (e - o) * count_ref[...]
-
-
-def stack_own(place, spectra, inverse_count, old):
-    steps = OWN // BLOCK
-    tables = lag_tables()
+def add_kernel(place_ref, added_ref, old_ref, out_ref):
+    out_ref[...] = old_ref[...].astype(jnp.float32) + added_ref[...].astype(jnp.float32)
+
+
+def add_rest_kernel(place_ref, stacks_ref, added_ref, old_ref, out_ref):
+    add_kernel(place_ref, added_ref, old_ref, out_ref)
+
+
+def add_half(place, added, old, stacks=None):
+    rows = 201
+    first = stacks is None
+    column = (lambda place: place[0]) if first else (lambda place: 1 - place[0])
+    spec = pl.BlockSpec((rows, OWN, HALF), lambda l, place: (l, 0, column(place)))
     return pl.pallas_call(
-        lag_own_kernel,
-        grid_spec=pltpu.PrefetchScalarGridSpec(
-            num_scalar_prefetch=1,
-            grid=(steps,),
-            in_specs=[
-                pl.BlockSpec((BLOCK, FREQ, HALF), lambda g, place: (g, 0, 0)),
-                pl.BlockSpec((BLOCK, FREQ, HALF), lambda g, place: (steps + g, 0, 0)),
-                whole(tables.shape),
-                pl.BlockSpec((BLOCK, HALF), lambda g, place: (place[0] * steps + g, 0)),
-                pl.BlockSpec((LAGS, BLOCK, HALF), lambda g, place: (0, g, place[0])),
-            ],
-            out_specs=pl.BlockSpec((LAGS, BLOCK, HALF), lambda g, place: (0, g, place[0])),
-            scratch_shapes=[pltpu.VMEM((SHIFTS * BLOCK, HALF), jnp.float32)] * 2,
-        ),
-        out_shape=jax.ShapeDtypeStruct((LAGS, OWN, 2 * HALF), jnp.float32),
-        compiler_params=pltpu.CompilerParams(vmem_limit_bytes=VMEM),
-        cost_estimate=pl.CostEstimate(flops=OWN * SHIFTS * FREQ * HALF * 4, bytes_accessed=16 << 20, transcendentals=0),
-    )(place, spectra, spectra, jnp.asarray(tables), inverse_count, old)
-
-
-def merge_kernel(place_ref, held_ref, got_ref, old_ref, out_ref):
-    out_ref[...] = old_ref[...].astype(jnp.float32) + got_ref[...].astype(jnp.float32)
-
-
-def merge(place, stacks, got, old):
-    rows = 201
-    spec = pl.BlockSpec((rows, OWN, HALF), lambda l, place: (l, 0, 1 - place[0]))
-    return pl.pallas_call(
-        merge_kernel,
+        add_kernel if first else add_rest_kernel,
         grid_spec=pltpu.PrefetchScalarGridSpec(
             num_scalar_prefetch=1,
             grid=(pl.cdiv(LAGS, rows),),
-            in_specs=[
-                pl.BlockSpec(memory_space=pl.ANY),
-                pl.BlockSpec((rows, OWN, HALF), lambda l, place: (l, 0, 0)),
-                spec,
-            ],
+            in_specs=([] if first else [pl.BlockSpec(memory_space=pl.ANY)])
+            + [pl.BlockSpec((rows, OWN, HALF), lambda l, place: (l, 0, 0)), spec],
             out_specs=spec,
         ),
-        out_shape=jax.ShapeDtypeStruct(stacks.shape, stacks.dtype),
-        input_output_aliases={1: 0},
-        compiler_params=pltpu.CompilerParams(vmem_limit_bytes=VMEM),
+        out_shape=jax.ShapeDtypeStruct((LAGS, OWN, 2 * HALF), jnp.float32),
+        input_output_aliases={} if first else {1: 0},
+        compiler_params=pltpu.CompilerParams(vmem_limit_bytes=ADD_VMEM),
         cost_estimate=pl.CostEstimate(flops=LAGS * OWN * HALF, bytes_accessed=13 << 20, transcendentals=0),
-    )(place, stacks, got, old)
+    )(place, *([] if first else [stacks]), added, old)
 
 
 def outgoing_kernel(record_ref, out_ref):
@@ -444,8 +408,11 @@
     return jnp.where(z_high == 0, jnp.stack([mine, theirs]), jnp.stack([theirs, mine]))
 
 
-def plane_sources(near):
-    column = jnp.stack([near] + [send(near, lambda x, y, l, h, c, d=d: (x, y ^ d, l, h, c)) for d in (1, 2, 3)])
+def along_y(near):
+    return jnp.stack([near] + [send(near, lambda x, y, l, h, c, d=d: (x, y ^ d, l, h, c)) for d in (1, 2, 3)])
+
+
+def along_x(column):
     plane = jnp.stack([column] + [send(column, lambda x, y, l, h, c, d=d: (x ^ d, y, l, h, c)) for d in (1, 2, 3)])
     return plane.reshape(SUB // 2, 2, PIECE, HALF)
 
@@ -466,8 +433,9 @@
     place = jnp.stack([core, group]).astype(jnp.int32)
 
     pieces = outgoing(record)
-    plane = plane_sources(near_sources(record, z_low, chip))
-    plane, pieces = lax.optimization_barrier((plane, pieces))
+    near, pieces = lax.optimization_barrier((near_sources(record, z_low, chip), pieces))
+    column, pieces = lax.optimization_barrier((along_y(near), pieces))
+    plane = along_x(column)
     receivers = lax.all_to_all(pieces, ("rcv", "src"), split_axis=0, concat_axis=0, tiled=True)
     sources = both_cores(plane, core)
 
@@ -484,10 +452,10 @@
     left = whiten_sources(sources, flags_src)
     receivers = receivers.reshape(SUB // 2 // PAIRS, PAIRS, 2, 4, PIECE, HALF)
     flags_rcv = flags_rcv.reshape(SUB // 2, 2, 1, HALF)
-    away, spectra = stack_partner(place, receivers, flags_rcv, left, inverse_count)
+    away, mine = stack_halves(place, receivers, flags_rcv, left, inverse_count)
     got = lax.ppermute(away, "src", [(0, 1), (1, 0), (2, 3), (3, 2)])
-    stacks = stack_own(place, spectra, inverse_count, old_stacks)
-    return merge(place, stacks, got, old_stacks)
+    stacks = add_half(place, mine, old_stacks)
+    return add_half(place, got, old_stacks, stacks)
 
 
 def solution(mesh):

time: 136 us -> 129 us (0.949)
  waiting for transfers between devices: 13.4 us -> 7.7 us
  Pallas kernels: 89.1 us -> 86.5 us
  starting transfers between devices: 21.2 us -> 23.2 us
    ppermute x10, waiting for transfers between devices: 11.2 us -> 4.69 us  [send(): lax.ppermute(value, ('rcv', 'src'), [(device(*place), device(*route(*plac...]
    all_to_all x1, starting transfers between devices: 6.77 us -> 8.85 us  [on_device(): lax.all_to_all(pieces, ('rcv', 'src'), split_axis=0, concat_axis=0, tiled...]
  transfers between devices with their start and end apart: 12 -> 12, of which waited for: 7 -> 5; matrix products, arithmetic and copies ran while one was open for 6% -> 6% of each run, Pallas kernels for 36% -> 34%
where the time goes in v4:
time: 129 us; the launch traced here: 127 us
  Pallas kernels  86.5 us (67%)
  starting transfers between devices  23.2 us (18%)
  waiting for transfers between devices  7.7 us (6%)
  local copies, waits for them, and re-layouts  4.95 us (4%)
  other arithmetic  3.61 us (3%)
    pallas_call x1, Pallas kernels, stack_halves(): pl.pallas_call(stack_kernel, grid_spec=pltpu.PrefetchScalarGridSpec(num_s...  38 us
    pallas_call x1, Pallas kernels, whiten_sources(): pl.pallas_call(whiten_sources_kernel, grid=(SUB // 4,), in_specs=[pl.Bloc...  33 us
    ppermute x10, starting transfers between devices, send(): lax.ppermute(value, ('rcv', 'src'), [(device(*place), device(*route(*plac...  14.3 us
    pallas_call x2, Pallas kernels, add_half(): pl.pallas_call(add_kernel if first else add_rest_kernel, grid_spec=pltpu....  11.5 us
    all_to_all x1, starting transfers between devices, on_device(): lax.all_to_all(pieces, ('rcv', 'src'), split_axis=0, concat_axis=0, tiled...  8.85 us
    ppermute x10, waiting for transfers between devices, send(): lax.ppermute(value, ('rcv', 'src'), [(device(*place), device(*route(*plac...  4.69 us
    pallas_call x1, Pallas kernels, outgoing(): pl.pallas_call(outgoing_kernel, grid=(steps,), in_specs=[pl.BlockSpec((PI...  4.07 us
  transfers between devices with their start and end apart: 12, of which 5 were waited for; matrix products, arithmetic and copies ran while one was open for 6% of the time, Pallas kernels for 34%

profile of v4, /device:TPU:0, one launch (start us, length us, event | category | flops | bytes accessed | tf_op | source)
XLA Modules:
  0.0 127.1 jit_solution(18262502402298288828)
XLA Ops:
  0.0 0.9 broadcast_select_fusion.1
  0.9 2.1 %collective-permute-start = (bf16[100,64]{1,0:T(8,128)(2,1)S(1)}, bf16[100,64]{1,0:T(8,128)(2,1)S(1)}, u32[]{:S(2)}, u32[]{:S(2)}) collective-permute-start(bf16[100,64]{1,0:T(8,128)(2,1)S(1)} %get-tuple-element.17), channel_id=1, source_target_pairs={{0,4},{1,5},{2,6},{3,7},{4,0},{5,1},{6,2},{7,3},{8,12},{9,13},{10,... | collective-permute-start | bytes 38408 | tf_op jit(solution)/shard_map/ppermute | solution.py:393
  3.0 2.5 %collective-permute-start.2 = (bf16[100,64]{1,0:T(8,128)(2,1)S(1)}, bf16[100,64]{1,0:T(8,128)(2,1)S(1)}, u32[]{:S(2)}, u32[]{:S(2)}) collective-permute-start(bf16[100,64]{1,0:T(8,128)(2,1)S(1)} %get-tuple-element.18), channel_id=1, source_target_pairs={{0,6},{1,7},{2,4},{3,5},{4,2},{5,3},{6,0},{7,1},{8,14},{9,15},{10,... | collective-permute-start | bytes 38408 | tf_op jit(solution)/shard_map/ppermute | solution.py:393
  5.5 1.1 collective-permute-start.1
  6.6 4.1 %shard_map.127 = bf16[32,2,2,100,128]{4,3,2,1,0:T(8,128)(2,1)} custom-call(bf16[100,8192]{1,0:T(8,128)(2,1)} %record_ref.1), custom_call_target="tpu_custom_call" | custom-call | bytes 5242880 | tf_op jit(solution)/shard_map/pallas_call | solution.py:375
  10.6 0.0 collective-permute-done
  10.6 0.1 maximum_select_fusion.2
  10.7 0.0 collective-permute-done.2
  10.8 0.1 collective-permute-done.1
  10.9 0.1 maximum_select_fusion.3
  11.0 3.1 %collective-permute-start.5 = (bf16[2,100,128]{2,1,0:T(8,128)(2,1)S(1)}, bf16[2,100,128]{2,1,0:T(8,128)(2,1)S(1)}, u32[]{:S(2)}, u32[]{:S(2)}) collective-permute-start(bf16[2,100,128]{2,1,0:T(8,128)(2,1)S(1)} %maximum_select_fusion.1), channel_id=1, source_target_pairs={{0,24},{1,25},{2,26},{3,27},{4,28},{5,29},{6,30},{7,31},{8,16},{9,... | collective-permute-start | bytes 153608 | tf_op jit(solution)/shard_map/ppermute | solution.py:393
  14.1 0.6 collective-permute-start.4
  14.7 0.5 collective-permute-start.3
  15.2 1.2 collective-permute-done.5
  16.4 3.3 %collective-permute-done.4 = bf16[2,100,128]{2,1,0:T(8,128)(2,1)S(1)} collective-permute-done((bf16[2,100,128]{2,1,0:T(8,128)(2,1)S(1)}, bf16[2,100,128]{2,1,0:T(8,128)(2,1)S(1)}, u32[]{:S(2)}, u32[]{:S(2)}) %collective-permute-start.4) | collective-permute-done | bytes 51232 | tf_op jit(solution)/shard_map/ppermute | solution.py:393
  19.7 0.0 collective-permute-done.3
  19.8 0.0 copy-start.1
  19.8 2.8 %collective-permute-start.8 = (bf16[4,2,100,128]{3,2,1,0:T(8,128)(2,1)S(1)}, bf16[4,2,100,128]{3,2,1,0:T(8,128)(2,1)S(1)}, u32[]{:S(2)}, u32[]{:S(2)}) collective-permute-start(bf16[4,2,100,128]{3,2,1,0:T(8,128)(2,1)S(1)} %pad_maximum_fusion.1), channel_id=1, source_target_pairs={{0,96},{1,97},{2,98},{3,99},{4,100},{5,101},{6,102},{7,103},{8,104... | collective-permute-start | bytes 614408 | tf_op jit(solution)/shard_map/ppermute | solution.py:393
  22.6 0.8 collective-permute-start.7
  23.4 0.5 collective-permute-start.6
  23.9 8.8 %all-to-all-start = ((bf16[128,100,128]{2,1,0:T(8,128)(2,1)}), bf16[128,100,128]{2,1,0:T(8,128)(2,1)}, u32[]{:S(2)}, u32[]{:S(2)}) async-start(bf16[128,100,128]{2,1,0:T(8,128)(2,1)} %bitcast.25), calls=%async_computation | async-start | bytes 6815744 | tf_op jit(solution)/shard_map/all_to_all | solution.py:439
  32.8 0.0 copy-done.1
  32.8 0.0 copy-start
  32.8 0.0 collective-permute-done.8
  32.8 0.0 collective-permute-done.7
  32.9 0.0 collective-permute-done.6
  32.9 0.1 pad_maximum_fusion
  33.0 0.3 copy.17
  33.3 0.3 collective-permute-start.9
  33.6 0.5 copy-done
  34.0 0.1 broadcast_multiply_fusion
  34.2 0.1 convert_element_type.6
  34.2 0.1 constant_dynamic-slice_fusion
  34.3 0.1 reshape.164
  34.4 1.1 gather_fusion.1
  35.5 1.2 gather_fusion
  36.7 0.6 pad_add_fusion.place_ref
  37.3 0.9 fusion.count_ref
  38.1 0.0 collective-permute-done.9
  38.1 1.7 %maximum_select_fusion = bf16[16,2,2,100,128]{4,0,3,1,2:T(8,128)(2,1)S(1)} fusion(bf16[16,2,1,100,128]{4,0,3,1,2:T(8,128)(2,1)} %bitcast.21, bf16[16,2,1,100,128]{4,0,3,1,2:T(8,128)(2,1)S(1)} %bitcast.27, pred[]{:T(512)S(6)} %eq.14), kind=kLoop, calls=%fused_computation.2 | loop fusion | flops 2457600 | bytes 3276801 | tf_op jit(solution)/shard_map/jit(_where)/select_n | solution.py:422
  39.8 1.7 %copy.19 = bf16[16,2,2,100,128]{4,3,2,1,0:T(8,128)(2,1)} copy(bf16[16,2,2,100,128]{4,0,3,1,2:T(8,128)(2,1)S(1)} %maximum_select_fusion) | data formatting | bytes 3276800 | tf_op jit(solution)/shard_map/jit(_where)/select_n | solution.py:422
  41.5 33.0 %shard_map.128.left_hbm = bf16[208,128,128]{2,1,0:T(8,128)(2,1)} custom-call(bf16[16,4,100,128]{3,2,1,0:T(8,128)(2,1)} %bitcast.28, f32[16,1,128]{2,1,0:T(1,128)} %bitcast.43, bf16[832,896]{1,0:T(8,128)(2,1)} %constant.44.clone.table_ref, f32[832,128]{1,0:T(8,128)} %constant.45.clone.sums_ref, bf16[2,208,512]{2,1,0:T(8,128)(2,1)} %constant.46.clone.band_ref, ...), custom_call_target="tpu_custom_call" | custom-call | flops 3053453312 | bytes 5505024 | tf_op jit(solution)/shard_map/pallas_call | solution.py:178
  74.5 2.6 %all-to-all-done = bf16[128,100,128]{2,1,0:T(8,128)(2,1)} async-done(((bf16[128,100,128]{2,1,0:T(8,128)(2,1)}), bf16[128,100,128]{2,1,0:T(8,128)(2,1)}, u32[]{:S(2)}, u32[]{:S(2)}) %all-to-all-start) | async-done | bytes 3276832 | tf_op jit(solution)/shard_map/all_to_all | solution.py:439
  77.1 38.0 %shard_map.129 = (bf16[401,32,128]{2,1,0:T(8,128)(2,1)}, bf16[401,32,128]{2,1,0:T(8,128)(2,1)}) custom-call(s32[2]{0:T(128)} %pad_add_fusion.place_ref, bf16[4,4,2,4,100,128]{5,4,3,2,1,0:T(8,128)(2,1)} %bitcast.11.x_ref, f32[16,2,1,128]{3,2,1,0:T(1,128)} %bitcast.42, bf16[832,896]{1,0:T(8,128)(2,1)} %constant.44.clone.table_ref, ...), custom_call_target="tpu_custom_call" | custom-call | flops 30000001024 | bytes 25165824 | tf_op jit(solution)/shard_map/pallas_call | solution.py:301
  115.1 0.1 collective-permute-start.10
  115.2 5.7 %shard_map.130.stacks_ref = f32[401,32,256]{2,1,0:T(8,128)} custom-call(s32[2]{0:T(128)} %pad_add_fusion.place_ref, bf16[401,32,128]{2,1,0:T(8,128)(2,1)} %get-tuple-element.15.added_ref, bf16[401,32,256]{2,1,0:T(8,128)(2,1)} %old_ref.3), custom_call_target="tpu_custom_call" | custom-call | flops 1642496 | bytes 13631488 | tf_op jit(solution)/shard_map/pallas_call | solution.py:347
  120.9 0.5 collective-permute-done.10.added_ref
  121.4 5.7 %shard_map.131 = f32[401,32,256]{2,1,0:T(8,128)} custom-call(s32[2]{0:T(128)} %pad_add_fusion.place_ref, f32[401,32,256]{2,1,0:T(8,128)} %shard_map.130.stacks_ref, bf16[401,32,128]{2,1,0:T(8,128)(2,1)} %collective-permute-done.10.added_ref, bf16[401,32,256]{2,1,0:T(8,128)(2,1)} %old_ref.3), custom_call_target="tpu_custom_call", output_to_operand_aliasing={{}: (1, {})} | custom-call | flops 1642496 | bytes 13631488 | tf_op jit(solution)/shard_map/pallas_call | solution.py:347
  (6 shorter events, 0.1 us)
Async XLA Ops:
  0.9 9.7 %collective-permute-start = (bf16[100,64]{1,0:T(8,128)(2,1)S(1)}, bf16[100,64]{1,0:T(8,128)(2,1)S(1)}, u32[]{:S(2)}, u32[]{:S(2)}) collective-permute-start(bf16[100,64]{1,0:T(8,128)(2,1)S(1)} %get-tuple-element.17), channel_id=1, source_target_pairs={{0,4},{1,5},{2,6},{3,7},{4,0},{5,1},{6,2},{7,3},{8,12},{9,13},{10,... | collective-permute-start | bytes 38408 | tf_op jit(solution)/shard_map/ppermute | solution.py:393
  3.0 7.8 %collective-permute-start.2 = (bf16[100,64]{1,0:T(8,128)(2,1)S(1)}, bf16[100,64]{1,0:T(8,128)(2,1)S(1)}, u32[]{:S(2)}, u32[]{:S(2)}) collective-permute-start(bf16[100,64]{1,0:T(8,128)(2,1)S(1)} %get-tuple-element.18), channel_id=1, source_target_pairs={{0,6},{1,7},{2,4},{3,5},{4,2},{5,3},{6,0},{7,1},{8,14},{9,15},{10,... | collective-permute-start | bytes 38408 | tf_op jit(solution)/shard_map/ppermute | solution.py:393
  5.5 5.4 %collective-permute-start.1 = (bf16[100,64]{1,0:T(8,128)(2,1)S(1)}, bf16[100,64]{1,0:T(8,128)(2,1)S(1)}, u32[]{:S(2)}, u32[]{:S(2)}) collective-permute-start(bf16[100,64]{1,0:T(8,128)(2,1)S(1)} %get-tuple-element.18), channel_id=1, source_target_pairs={{0,2},{1,3},{2,0},{3,1},{4,6},{5,7},{6,4},{7,5},{8,10},{9,11},{10,... | collective-permute-start | bytes 38408 | tf_op jit(solution)/shard_map/ppermute | solution.py:393
  11.0 5.4 %collective-permute-start.5 = (bf16[2,100,128]{2,1,0:T(8,128)(2,1)S(1)}, bf16[2,100,128]{2,1,0:T(8,128)(2,1)S(1)}, u32[]{:S(2)}, u32[]{:S(2)}) collective-permute-start(bf16[2,100,128]{2,1,0:T(8,128)(2,1)S(1)} %maximum_select_fusion.1), channel_id=1, source_target_pairs={{0,24},{1,25},{2,26},{3,27},{4,28},{5,29},{6,30},{7,31},{8,16},{9,... | collective-permute-start | bytes 153608 | tf_op jit(solution)/shard_map/ppermute | solution.py:393
  14.1 5.6 %collective-permute-start.4 = (bf16[2,100,128]{2,1,0:T(8,128)(2,1)S(1)}, bf16[2,100,128]{2,1,0:T(8,128)(2,1)S(1)}, u32[]{:S(2)}, u32[]{:S(2)}) collective-permute-start(bf16[2,100,128]{2,1,0:T(8,128)(2,1)S(1)} %maximum_select_fusion.1), channel_id=1, source_target_pairs={{0,16},{1,17},{2,18},{3,19},{4,20},{5,21},{6,22},{7,23},{8,24},{9,... | collective-permute-start | bytes 153608 | tf_op jit(solution)/shard_map/ppermute | solution.py:393
  14.7 5.0 %collective-permute-start.3 = (bf16[2,100,128]{2,1,0:T(8,128)(2,1)S(1)}, bf16[2,100,128]{2,1,0:T(8,128)(2,1)S(1)}, u32[]{:S(2)}, u32[]{:S(2)}) collective-permute-start(bf16[2,100,128]{2,1,0:T(8,128)(2,1)S(1)} %maximum_select_fusion.1), channel_id=1, source_target_pairs={{0,8},{1,9},{2,10},{3,11},{4,12},{5,13},{6,14},{7,15},{8,0},{9,1},... | collective-permute-start | bytes 153608 | tf_op jit(solution)/shard_map/ppermute | solution.py:393
  19.8 13.0 %copy-start.1 = (s32[8192]{0:T(1024)S(1)}, s32[8192]{0:T(1024)}, u32[]{:S(2)}) copy-start(s32[8192]{0:T(1024)} %param.14) | copy-start | bytes 98308
  19.8 13.1 %collective-permute-start.8 = (bf16[4,2,100,128]{3,2,1,0:T(8,128)(2,1)S(1)}, bf16[4,2,100,128]{3,2,1,0:T(8,128)(2,1)S(1)}, u32[]{:S(2)}, u32[]{:S(2)}) collective-permute-start(bf16[4,2,100,128]{3,2,1,0:T(8,128)(2,1)S(1)} %pad_maximum_fusion.1), channel_id=1, source_target_pairs={{0,96},{1,97},{2,98},{3,99},{4,100},{5,101},{6,102},{7,103},{8,104... | collective-permute-start | bytes 614408 | tf_op jit(solution)/shard_map/ppermute | solution.py:393
  22.6 10.2 %collective-permute-start.7 = (bf16[4,2,100,128]{3,2,1,0:T(8,128)(2,1)S(1)}, bf16[4,2,100,128]{3,2,1,0:T(8,128)(2,1)S(1)}, u32[]{:S(2)}, u32[]{:S(2)}) collective-permute-start(bf16[4,2,100,128]{3,2,1,0:T(8,128)(2,1)S(1)} %pad_maximum_fusion.1), channel_id=1, source_target_pairs={{0,64},{1,65},{2,66},{3,67},{4,68},{5,69},{6,70},{7,71},{8,72},{9,... | collective-permute-start | bytes 614408 | tf_op jit(solution)/shard_map/ppermute | solution.py:393
  23.4 9.4 %collective-permute-start.6 = (bf16[4,2,100,128]{3,2,1,0:T(8,128)(2,1)S(1)}, bf16[4,2,100,128]{3,2,1,0:T(8,128)(2,1)S(1)}, u32[]{:S(2)}, u32[]{:S(2)}) collective-permute-start(bf16[4,2,100,128]{3,2,1,0:T(8,128)(2,1)S(1)} %pad_maximum_fusion.1), channel_id=1, source_target_pairs={{0,32},{1,33},{2,34},{3,35},{4,36},{5,37},{6,38},{7,39},{8,40},{9,... | collective-permute-start | bytes 614408 | tf_op jit(solution)/shard_map/ppermute | solution.py:393
  23.9 53.1 %all-to-all-start = ((bf16[128,100,128]{2,1,0:T(8,128)(2,1)}), bf16[128,100,128]{2,1,0:T(8,128)(2,1)}, u32[]{:S(2)}, u32[]{:S(2)}) async-start(bf16[128,100,128]{2,1,0:T(8,128)(2,1)} %bitcast.25), calls=%async_computation | async-start | bytes 6815744 | tf_op jit(solution)/shard_map/all_to_all | solution.py:439
  32.8 1.2 copy-start
  33.3 4.8 %collective-permute-start.9 = (bf16[16,2,100,128]{3,0,2,1:T(8,128)(2,1)S(1)}, bf16[16,2,100,128]{3,0,2,1:T(8,128)(2,1)}, u32[]{:S(2)}, u32[]{:S(2)}) collective-permute-start(bf16[16,2,100,128]{3,0,2,1:T(8,128)(2,1)S(1)} %bitcast.26), channel_id=1, source_target_pairs={{0,1},{1,0},{2,3},{3,2},{4,5},{5,4},{6,7},{7,6},{8,9},{9,8},{10,11... | collective-permute-start | bytes 2457608 | tf_op jit(solution)/shard_map/ppermute | solution.py:393
  115.1 6.3 %collective-permute-start.10 = (bf16[401,32,128]{2,1,0:T(8,128)(2,1)}, bf16[401,32,128]{2,1,0:T(8,128)(2,1)}, u32[]{:S(2)}, u32[]{:S(2)}) collective-permute-start(bf16[401,32,128]{2,1,0:T(8,128)(2,1)} %get-tuple-element.16), channel_id=1, source_target_pairs={{0,1},{1,0},{2,3},{3,2},{4,5},{5,4},{6,7},{7,6},{8,9},{9,8},{10,11... | collective-permute-start | bytes 9854984 | tf_op jit(solution)/shard_map/ppermute | solution.py:456

commit v5 on v4

--- a/solution.py
+++ b/solution.py
@@ -22,6 +22,8 @@
 PADDED = 112
 DEPTH = 4 * PADDED
 FREQ = 416
+MIDDLE = 200
+EVENS = 48
 HALF = 128
 SRC = 64
 OWN = 32
@@ -33,7 +35,7 @@
 XPITCH = ROWS + 8
 BLOCK = 16
 PAIRS = 4
-VMEM = 56 * 1024 * 1024
+VMEM = 60 * 1024 * 1024
 ADD_VMEM = 62 * 1024 * 1024
 
 
@@ -43,38 +45,75 @@
     return high, low
 
 
+def bin_order():
+    order = np.full(FREQ, -1)
+    order[: MIDDLE + 1] = np.arange(MIDDLE + 1)
+    order[SHIFTS : SHIFTS + MIDDLE] = 2 * MIDDLE - np.arange(MIDDLE)
+    return order
+
+
 def forward_table():
     samples = np.arange(WIN)[None, :]
-    bins = np.arange(BINS)[:, None]
-    phases = (samples * bins % NFFT) * (2.0 * math.pi / NFFT)
+    order = bin_order()
+    valid = (order >= 0)[:, None, None]
+    phases = (samples * order[:, None] % NFFT) * (2.0 * math.pi / NFFT)
     table = np.zeros((2, FREQ, 4, PADDED), np.float32)
-    table[0, :BINS, :, :PIECE] = np.cos(phases).reshape(BINS, 4, PIECE)
-    table[1, :BINS, :, :PIECE] = -np.sin(phases).reshape(BINS, 4, PIECE)
+    table[0, :, :, :PIECE] = np.cos(phases).reshape(FREQ, 4, PIECE) * valid
+    table[1, :, :, :PIECE] = -np.sin(phases).reshape(FREQ, 4, PIECE) * valid
     high, low = split(table.reshape(2 * FREQ, DEPTH))
     sums = (high.astype(np.float64) + low.astype(np.float64)).sum(axis=1, keepdims=True)
     sums = np.broadcast_to((sums / WIN).astype(np.float32), (2 * FREQ, HALF)).copy()
     return np.concatenate([high, low], axis=1), sums
 
 
+def piece_order():
+    return np.concatenate([np.arange(0, 2 * EVENS, 2), np.arange(1, 2 * EVENS, 2), [96, 98, 97, 99]])
+
+
+def parity_tables():
+    times = np.full((2, REACH), -1)
+    pieces = piece_order()
+    for j in range(4):
+        for parity in range(2):
+            times[parity, j * EVENS : (j + 1) * EVENS] = j * PIECE + pieces[parity * EVENS : (parity + 1) * EVENS]
+            last = 4 * EVENS + j * BLOCK + 2 * parity
+            times[parity, last : last + 2] = j * PIECE + pieces[2 * EVENS + 2 * parity : 2 * EVENS + 2 * parity + 2]
+    assert sorted(times[times >= 0]) == list(range(WIN))
+    bins = np.arange(SHIFTS)[:, None]
+    phases = (times[:, None, :] * bins % NFFT) * (2.0 * math.pi / NFFT)
+    valid = (times >= 0)[:, None, :] & (bins <= MIDDLE)
+    table = np.concatenate([np.cos(phases) * valid, -np.sin(phases) * valid], axis=1).astype(np.float32)
+    high, low = split(table)
+    even, odd = (high.astype(np.float64) + low.astype(np.float64)).sum(axis=2, keepdims=True)
+    (er, ei), (orr, oi) = (np.split(part, 2) for part in (even, odd))
+    sums = np.concatenate([er + orr, er - orr, ei + oi, oi - ei]) / WIN
+    sums = np.broadcast_to(sums.astype(np.float32), (2 * FREQ, HALF)).copy()
+    return np.concatenate([high, low], axis=2), sums
+
+
 def band_table():
-    bins = np.arange(FREQ)
-    inside = np.abs(bins[:, None] - bins[None, :]) <= HALFBAND
-    inside &= (bins[:, None] < BINS) & (bins[None, :] < BINS)
+    order = bin_order()
+    columns = (order >= 0)[None, :]
+    rows = order.copy()
+    rows[SHIFTS + MIDDLE] = MIDDLE
+    inside = (np.abs(rows[:, None] - order[None, :]) <= HALFBAND) & columns & (rows >= 0)[:, None]
     counts = np.maximum(inside.sum(axis=1, keepdims=True), 1)
     inverse = np.broadcast_to((1.0 / (2.0 * counts)).astype(np.float32), (FREQ, HALF)).copy()
-    halves = np.stack([inside[:SHIFTS, :REACH], inside[SHIFTS:, FREQ - REACH :]])
+    near = FREQ - REACH + SHIFTS
+    first = np.concatenate([inside[:SHIFTS, :SHIFTS], inside[:SHIFTS, near:]], axis=1)
+    halves = np.stack([first, inside[SHIFTS:, FREQ - REACH :]])
     assert halves.sum() == inside.sum()
     return np.concatenate([halves, halves], axis=2).astype(jnp.bfloat16), inverse
 
 
 def lag_tables():
     shifts = np.arange(LARGEST_LAG + 1)[:, None]
-    bins = np.arange(BINS)[None, :]
+    bins = bin_order()[None, :]
     phases = (shifts * bins % NFFT) * (2.0 * math.pi / NFFT)
-    weights = np.where((bins == 0) | (bins == NFFT // 2), 1.0, 2.0) / math.sqrt(NFFT)
+    weights = np.where((bins == 0) | (bins == NFFT // 2), 1.0, 2.0) / math.sqrt(NFFT) * (bins >= 0)
     tables = np.zeros((2, SHIFTS, FREQ), np.float32)
-    tables[0, : LARGEST_LAG + 1, :BINS] = weights * np.cos(phases)
-    tables[1, : LARGEST_LAG + 1, :BINS] = -weights * np.sin(phases)
+    tables[0, : LARGEST_LAG + 1] = weights * np.cos(phases)
+    tables[1, : LARGEST_LAG + 1] = -weights * np.sin(phases)
     return tables.astype(jnp.bfloat16)
 
 
@@ -86,7 +125,7 @@
     samples[...] = jnp.zeros(samples.shape, samples.dtype)
 
 
-def whiten_pair(pieces, flags, samples, table_ref, sums_ref, band_ref, inverse_ref, spec):
+def transform(pieces, samples, table_ref, spec):
     for g in range(2):
         for j in range(4):
             samples[pl.ds(j * PADDED, PIECE), g * HALF : (g + 1) * HALF] = pieces[g][j][...]
@@ -95,21 +134,45 @@
     for i in range(4):
         rows = pl.ds(i * SHIFTS, SHIFTS)
         spec[rows, :] = dot(table_ref[rows, :], x)
-    total = spec[0:1, :]
+    return spec[:FREQ], spec[FREQ:]
+
+
+def transform_parities(pieces, samples, table_ref, spec):
+    for g in range(2):
+        lanes = slice(g * HALF, (g + 1) * HALF)
+        for j in range(4):
+            last = pieces[g][j][pl.ds(2 * EVENS, PIECE - 2 * EVENS), :]
+            for parity in range(2):
+                samples[parity, pl.ds(j * EVENS, EVENS), lanes] = pieces[g][j][pl.ds(parity * EVENS, EVENS), :]
+                samples[parity, pl.ds(4 * EVENS + j * BLOCK, PIECE - 2 * EVENS), lanes] = last
+    for parity in range(2):
+        x = samples[parity]
+        x = jnp.concatenate([x, x], axis=0)
+        for i in range(2):
+            rows = pl.ds(i * SHIFTS, SHIFTS)
+            spec[parity, rows, :] = dot(table_ref[parity, rows, :], x)
+    even_real, even_imag = spec[0, :SHIFTS], spec[0, SHIFTS:]
+    odd_real, odd_imag = spec[1, :SHIFTS], spec[1, SHIFTS:]
+    real = jnp.concatenate([even_real + odd_real, even_real - odd_real], axis=0)
+    imag = jnp.concatenate([even_imag + odd_imag, odd_imag - even_imag], axis=0)
+    return real, imag
+
+
+def whiten_pair(spectrum, flags, sums_ref, band_ref, inverse_ref):
+    real, imag = spectrum
+    total = real[0:1, :]
     sums = sums_ref[...]
     sums = jnp.concatenate([sums, sums], axis=1)
-    real = spec[:FREQ] - sums[:FREQ] * total
-    imag = spec[FREQ:] - sums[FREQ:] * total
+    real = real - sums[:FREQ] * total
+    imag = imag - sums[FREQ:] * total
     power = real * real + imag * imag
     power_high = power.astype(jnp.bfloat16)
     power_low = (power - power_high.astype(jnp.float32)).astype(jnp.bfloat16)
-    smooth = jnp.concatenate(
-        [
-            dot(band_ref[i], jnp.concatenate([part[first : first + REACH] for part in (power_high, power_low)], axis=0))
-            for i, first in enumerate((0, FREQ - REACH))
-        ],
-        axis=0,
-    )
+    near = FREQ - REACH + SHIFTS
+    first = [rows for part in (power_high, power_low) for rows in (part[:SHIFTS], part[near:])]
+    second = [part[FREQ - REACH :] for part in (power_high, power_low)]
+    smooth = [dot(band_ref[i], jnp.concatenate(rows, axis=0)) for i, rows in enumerate((first, second))]
+    smooth = jnp.concatenate(smooth, axis=0)
     inverse = inverse_ref[...]
     inverse = jnp.concatenate([inverse, inverse], axis=1)
     scale = flags * lax.rsqrt(smooth * inverse + EPSILON)
@@ -127,7 +190,8 @@
 
     pieces = [[x_ref.at[g, j] for j in range(4)] for g in range(2)]
     flags = jnp.concatenate([flag_ref[0], flag_ref[1]], axis=1)
-    real, imag = whiten_pair(pieces, flags, samples, table_ref, sums_ref, band_ref, inverse_ref, spec)
+    spectrum = transform(pieces, samples, table_ref, spec)
+    real, imag = whiten_pair(spectrum, flags, sums_ref, band_ref, inverse_ref)
     for g in range(2):
         group = 2 * step + g
         first = pl.ds(group, FREQ, stride=SPITCH)
@@ -163,8 +227,8 @@
     return pl.BlockSpec(shape, lambda *_: (0,) * len(shape))
 
 
-def whiten_tables():
-    return [jnp.asarray(table) for table in (*forward_table(), *band_table())]
+def whiten_tables(forward):
+    return [jnp.asarray(table) for table in (*forward(), *band_table())]
 
 
 def whiten_cost(groups):
@@ -174,7 +238,7 @@
 
 
 def whiten_sources(x, flags):
-    tables = whiten_tables()
+    tables = whiten_tables(forward_table)
     return pl.pallas_call(
         whiten_sources_kernel,
         grid=(SUB // 4,),
@@ -195,20 +259,24 @@
     )(x, flags, *tables)
 
 
-def lag_sums(real_ref, imag_ref, tables_ref, even, odd):
-    for pair in range(BLOCK // 2):
-        real = jnp.concatenate([real_ref[2 * pair], real_ref[2 * pair + 1]], axis=1)
-        imag = jnp.concatenate([imag_ref[2 * pair], imag_ref[2 * pair + 1]], axis=1)
-        cosine = dot(tables_ref[0], real)
-        sine = dot(tables_ref[1], imag)
-        for i in range(2):
-            rows = pl.ds(2 * pair + i, SHIFTS, stride=BLOCK)
-            even[rows, :] = cosine[:, i * HALF : (i + 1) * HALF]
-            odd[rows, :] = sine[:, i * HALF : (i + 1) * HALF]
-
-
-def shift_rows(m):
-    return pl.ds(pl.multiple_of(m * BLOCK, BLOCK), BLOCK)
+def lag_pair(pair, real_ref, imag_ref, tables_ref, even, odd):
+    real = jnp.concatenate([real_ref[2 * pair], real_ref[2 * pair + 1]], axis=1)
+    imag = jnp.concatenate([imag_ref[2 * pair], imag_ref[2 * pair + 1]], axis=1)
+    cosine = dot(tables_ref[0], real)
+    sine = dot(tables_ref[1], imag)
+    for i in range(2):
+        rows = pl.ds(2 * pair + i, SHIFTS, stride=BLOCK)
+        even[rows, :] = cosine[:, i * HALF : (i + 1) * HALF]
+        odd[rows, :] = sine[:, i * HALF : (i + 1) * HALF]
+
+
+def combine(first, last, count, even, odd, out_ref):
+    for m in range(first, last):
+        rows = pl.ds(m * BLOCK, BLOCK)
+        e, o = even[rows, :], odd[rows, :]
+        out_ref[LARGEST_LAG + m] = ((e + o) * count).astype(jnp.bfloat16)
+        if m > 0:
+            out_ref[LARGEST_LAG - m] = ((e - o) * count).astype(jnp.bfloat16)
 
 
 def stack_kernel(
@@ -222,8 +290,8 @@
     tables_ref,
     count_ref,
     left_hbm,
-    away_ref,
-    mine_ref,
+    away_hbm,
+    mine_hbm,
     samples,
     spec,
     held,
@@ -232,12 +300,13 @@
     products,
     even,
     odd,
-    sem,
+    halves,
+    sems,
 ):
     step = pl.program_id(0)
     core = place_ref[0]
     inner = lax.rem(place_ref[1], PAIRS)
-    left_copy = pltpu.make_async_copy(left_hbm, left_ref, sem)
+    left_copy = pltpu.make_async_copy(left_hbm, left_ref, sems.at[0])
 
     @pl.when(step == 0)
     def _():
@@ -248,9 +317,8 @@
         source = lax.bitwise_xor(p, inner)
         pieces = [[x_ref.at[source, g, j] for j in range(4)] for g in range(2)]
         flags = jnp.concatenate([flag_ref[p, 0], flag_ref[p, 1]], axis=1)
-        real, imag = whiten_pair(
-            pieces, flags, samples.at[p % 2], table_ref, sums_ref, band_ref, inverse_ref, spec.at[p % 2]
-        )
+        spectrum = transform_parities(pieces, samples.at[p % 2], table_ref, spec.at[p % 2])
+        real, imag = whiten_pair(spectrum, flags, sums_ref, band_ref, inverse_ref)
         for g in range(2):
             row = g * SUB + step * PAIRS + p
             held[pl.ds(row, FREQ, stride=PITCH), :] = real[:, g * HALF : (g + 1) * HALF]
@@ -280,24 +348,43 @@
                 for row in range(ROWS):
                     spectra[row, bins, :] = products[side, pl.ds(row, BLOCK, stride=XPITCH), :].astype(jnp.bfloat16)
 
-        for half, out_ref in ((1 - core, away_ref), (core, mine_ref)):
-            for g in range(OWN // BLOCK):
-                first = half * OWN + g * BLOCK
-                lag_sums(
-                    spectra.at[pl.ds(first, BLOCK)], spectra.at[pl.ds(SRC + first, BLOCK)], tables_ref, even, odd
+        groups = [(half, g) for half in range(2) for g in range(OWN // BLOCK)]
+        starts = [lax.bitwise_xor(core, 1 - half) * OWN + g * BLOCK for half, g in groups]
+        shares = [(LARGEST_LAG + 1) * i // (BLOCK // 2) for i in range(BLOCK // 2 + 1)]
+        copies = [
+            pltpu.make_async_copy(
+                halves.at[i],
+                (away_hbm, mine_hbm)[half].at[:, pl.ds(g * BLOCK, BLOCK)],
+                sems.at[1 + i],
+            )
+            for i, (half, g) in enumerate(groups)
+        ]
+
+        def finish(i, first, last):
+            count = count_ref[pl.ds(pl.multiple_of(starts[i], BLOCK), BLOCK), :]
+            combine(first, last, count, even.at[i % 2], odd.at[i % 2], halves.at[i])
+            if last > LARGEST_LAG:
+                copies[i].start()
+
+        for i, start in enumerate(starts):
+            for pair in range(BLOCK // 2):
+                lag_pair(
+                    pair,
+                    spectra.at[pl.ds(start, BLOCK)],
+                    spectra.at[pl.ds(SRC + start, BLOCK)],
+                    tables_ref,
+                    even.at[i % 2],
+                    odd.at[i % 2],
                 )
-                count = count_ref[pl.ds(pl.multiple_of(first, BLOCK), BLOCK), :]
-
-                @pl.loop(0, LARGEST_LAG + 1, unroll=8)
-                def _(m):
-                    e, o = even[shift_rows(m), :], odd[shift_rows(m), :]
-                    sources = pl.ds(g * BLOCK, BLOCK)
-                    out_ref[LARGEST_LAG + m, sources, :] = ((e + o) * count).astype(jnp.bfloat16)
-                    out_ref[LARGEST_LAG - m, sources, :] = ((e - o) * count).astype(jnp.bfloat16)
+                if i > 0:
+                    finish(i - 1, shares[pair], shares[pair + 1])
+        finish(len(starts) - 1, 0, LARGEST_LAG + 1)
+        for copy in copies:
+            copy.wait()
 
 
 def stack_halves(place, x, flags, left, inverse_count):
-    tables = whiten_tables() + [jnp.asarray(lag_tables()), inverse_count]
+    tables = whiten_tables(parity_tables) + [jnp.asarray(lag_tables()), inverse_count]
     return pl.pallas_call(
         stack_kernel,
         grid_spec=pltpu.PrefetchScalarGridSpec(
@@ -312,17 +399,18 @@
             ]
             + [whole(table.shape) for table in tables]
             + [pl.BlockSpec(memory_space=pl.ANY)],
-            out_specs=[whole((LAGS, OWN, HALF))] * 2,
+            out_specs=[pl.BlockSpec(memory_space=pl.ANY)] * 2,
             scratch_shapes=[
-                pltpu.VMEM((2, DEPTH, 2 * HALF), jnp.bfloat16),
-                pltpu.VMEM((2, 2 * FREQ, 2 * HALF), jnp.float32),
+                pltpu.VMEM((2, 2, REACH, 2 * HALF), jnp.bfloat16),
+                pltpu.VMEM((2, 2, FREQ, 2 * HALF), jnp.float32),
                 pltpu.VMEM((FREQ * PITCH, HALF), jnp.float32),
                 pltpu.VMEM(left.shape, left.dtype),
                 pltpu.VMEM((ROWS, FREQ, HALF), jnp.bfloat16),
                 pltpu.VMEM((2, BLOCK * XPITCH, HALF), jnp.float32),
-                pltpu.VMEM((SHIFTS * BLOCK, HALF), jnp.float32),
-                pltpu.VMEM((SHIFTS * BLOCK, HALF), jnp.float32),
-                pltpu.SemaphoreType.DMA,
+                pltpu.VMEM((2, SHIFTS * BLOCK, HALF), jnp.float32),
+                pltpu.VMEM((2, SHIFTS * BLOCK, HALF), jnp.float32),
+                pltpu.VMEM((SRC // BLOCK, LAGS, BLOCK, HALF), jnp.bfloat16),
+                pltpu.SemaphoreType.DMA((1 + SRC // BLOCK,)),
             ],
         ),
         out_shape=[jax.ShapeDtypeStruct((LAGS, OWN, HALF), jnp.bfloat16)] * 2,
@@ -360,11 +448,11 @@
     )(place, *([] if first else [stacks]), added, old)
 
 
-def outgoing_kernel(record_ref, out_ref):
+def outgoing_kernel(record_ref, order_ref, out_ref):
     for i in range(out_ref.shape[0]):
         for core in range(2):
             column = (2 * i + core) * HALF
-            piece = record_ref[:, column : column + HALF]
+            piece = dot(order_ref[...], record_ref[:, column : column + HALF]).astype(record_ref.dtype)
             for chip in range(2):
                 out_ref[i, chip, core] = piece
 
@@ -372,15 +460,16 @@
 def outgoing(record):
     blocks = record.shape[1] // (2 * HALF)
     steps = 4
+    order = (piece_order()[:, None] == np.arange(PIECE)[None, :]).astype(jnp.bfloat16)
     pieces = pl.pallas_call(
         outgoing_kernel,
         grid=(steps,),
-        in_specs=[pl.BlockSpec((PIECE, record.shape[1] // steps), lambda i: (0, i))],
+        in_specs=[pl.BlockSpec((PIECE, record.shape[1] // steps), lambda i: (0, i)), whole(order.shape)],
         out_specs=pl.BlockSpec((blocks // steps, 2, 2, PIECE, HALF), lambda i: (i, 0, 0, 0, 0)),
         out_shape=jax.ShapeDtypeStruct((blocks, 2, 2, PIECE, HALF), record.dtype),
         compiler_params=pltpu.CompilerParams(vmem_limit_bytes=VMEM),
         cost_estimate=pl.CostEstimate(flops=0, bytes_accessed=5 << 20, transcendentals=0),
-    )(record)
+    )(record, jnp.asarray(order))
     return pieces.reshape(4 * blocks, PIECE, HALF)
 
 

time: 129 us -> 124 us (0.961)
  Pallas kernels: 86.5 us -> 81.8 us
    pallas_call x1, Pallas kernels: 38 us -> 32.6 us  [stack_halves(): pl.pallas_call(stack_kernel, grid_spec=pltpu.PrefetchScalarGridSpec(num_s...]
  transfers between devices with their start and end apart: 12 -> 12, of which waited for: 5 -> 4; matrix products, arithmetic and copies ran while one was open for 6% -> 6% of each run, Pallas kernels for 34% -> 36%
where the time goes in v5:
time: 124 us; the launch traced here: 122 us
  Pallas kernels  81.8 us (66%)
  starting transfers between devices  23.3 us (19%)
  waiting for transfers between devices  7.53 us (6%)
  local copies, waits for them, and re-layouts  4.95 us (4%)
  other arithmetic  3.61 us (3%)
    pallas_call x1, Pallas kernels, whiten_sources(): pl.pallas_call(whiten_sources_kernel, grid=(SUB // 4,), in_specs=[pl.Bloc...  33.1 us
    pallas_call x1, Pallas kernels, stack_halves(): pl.pallas_call(stack_kernel, grid_spec=pltpu.PrefetchScalarGridSpec(num_s...  32.6 us
    ppermute x10, starting transfers between devices, send(): lax.ppermute(value, ('rcv', 'src'), [(device(*place), device(*route(*plac...  14.3 us
    pallas_call x2, Pallas kernels, add_half(): pl.pallas_call(add_kernel if first else add_rest_kernel, grid_spec=pltpu....  11.5 us
    all_to_all x1, starting transfers between devices, on_device(): lax.all_to_all(pieces, ('rcv', 'src'), split_axis=0, concat_axis=0, tiled...  8.94 us
    pallas_call x1, Pallas kernels, outgoing(): pl.pallas_call(outgoing_kernel, grid=(steps,), in_specs=[pl.BlockSpec((PI...  4.63 us
    ppermute x10, waiting for transfers between devices, send(): lax.ppermute(value, ('rcv', 'src'), [(device(*place), device(*route(*plac...  4.58 us
    all_to_all x1, waiting for transfers between devices, on_device(): lax.all_to_all(pieces, ('rcv', 'src'), split_axis=0, concat_axis=0, tiled...  2.49 us
  transfers between devices with their start and end apart: 12, of which 4 were waited for; matrix products, arithmetic and copies ran while one was open for 6% of the time, Pallas kernels for 36%

profile of v5, /device:TPU:0, one launch (start us, length us, event | category | flops | bytes accessed | tf_op | source)
XLA Modules:
  0.0 122.3 jit_solution(6865379205973571289)
XLA Ops:
  0.0 0.9 broadcast_select_fusion.1
  0.9 2.1 %collective-permute-start = (bf16[100,64]{1,0:T(8,128)(2,1)S(1)}, bf16[100,64]{1,0:T(8,128)(2,1)S(1)}, u32[]{:S(2)}, u32[]{:S(2)}) collective-permute-start(bf16[100,64]{1,0:T(8,128)(2,1)S(1)} %get-tuple-element.17), channel_id=1, source_target_pairs={{0,4},{1,5},{2,6},{3,7},{4,0},{5,1},{6,2},{7,3},{8,12},{9,13},{10,... | collective-permute-start | bytes 38408 | tf_op jit(solution)/shard_map/ppermute | solution.py:482
  3.0 2.5 %collective-permute-start.2 = (bf16[100,64]{1,0:T(8,128)(2,1)S(1)}, bf16[100,64]{1,0:T(8,128)(2,1)S(1)}, u32[]{:S(2)}, u32[]{:S(2)}) collective-permute-start(bf16[100,64]{1,0:T(8,128)(2,1)S(1)} %get-tuple-element.18), channel_id=1, source_target_pairs={{0,6},{1,7},{2,4},{3,5},{4,2},{5,3},{6,0},{7,1},{8,14},{9,15},{10,... | collective-permute-start | bytes 38408 | tf_op jit(solution)/shard_map/ppermute | solution.py:482
  5.5 1.1 collective-permute-start.1
  6.6 4.6 %shard_map.136 = bf16[32,2,2,100,128]{4,3,2,1,0:T(8,128)(2,1)} custom-call(bf16[100,8192]{1,0:T(8,128)(2,1)} %record_ref.1, bf16[100,100]{1,0:T(8,128)(2,1)} %constant.50.clone.order_ref), custom_call_target="tpu_custom_call" | custom-call | bytes 5242880 | tf_op jit(solution)/shard_map/pallas_call | solution.py:464
  11.2 0.0 collective-permute-done
  11.2 0.1 maximum_select_fusion.2
  11.3 0.0 collective-permute-done.2
  11.3 0.0 collective-permute-done.1
  11.3 0.1 maximum_select_fusion.3
  11.4 3.1 %collective-permute-start.5 = (bf16[2,100,128]{2,1,0:T(8,128)(2,1)S(1)}, bf16[2,100,128]{2,1,0:T(8,128)(2,1)S(1)}, u32[]{:S(2)}, u32[]{:S(2)}) collective-permute-start(bf16[2,100,128]{2,1,0:T(8,128)(2,1)S(1)} %maximum_select_fusion.1), channel_id=1, source_target_pairs={{0,24},{1,25},{2,26},{3,27},{4,28},{5,29},{6,30},{7,31},{8,16},{9,... | collective-permute-start | bytes 153608 | tf_op jit(solution)/shard_map/ppermute | solution.py:482
  14.5 0.6 collective-permute-start.4
  15.2 0.5 collective-permute-start.3
  15.6 1.2 %collective-permute-done.5 = bf16[2,100,128]{2,1,0:T(8,128)(2,1)S(1)} collective-permute-done((bf16[2,100,128]{2,1,0:T(8,128)(2,1)S(1)}, bf16[2,100,128]{2,1,0:T(8,128)(2,1)S(1)}, u32[]{:S(2)}, u32[]{:S(2)}) %collective-permute-start.5) | collective-permute-done | bytes 51232 | tf_op jit(solution)/shard_map/ppermute | solution.py:482
  16.9 3.3 %collective-permute-done.4 = bf16[2,100,128]{2,1,0:T(8,128)(2,1)S(1)} collective-permute-done((bf16[2,100,128]{2,1,0:T(8,128)(2,1)S(1)}, bf16[2,100,128]{2,1,0:T(8,128)(2,1)S(1)}, u32[]{:S(2)}, u32[]{:S(2)}) %collective-permute-start.4) | collective-permute-done | bytes 51232 | tf_op jit(solution)/shard_map/ppermute | solution.py:482
  20.2 0.0 collective-permute-done.3
  20.2 0.0 copy-start.1
  20.2 2.8 %collective-permute-start.8 = (bf16[4,2,100,128]{3,2,1,0:T(8,128)(2,1)S(1)}, bf16[4,2,100,128]{3,2,1,0:T(8,128)(2,1)S(1)}, u32[]{:S(2)}, u32[]{:S(2)}) collective-permute-start(bf16[4,2,100,128]{3,2,1,0:T(8,128)(2,1)S(1)} %pad_maximum_fusion.1), channel_id=1, source_target_pairs={{0,96},{1,97},{2,98},{3,99},{4,100},{5,101},{6,102},{7,103},{8,104... | collective-permute-start | bytes 614408 | tf_op jit(solution)/shard_map/ppermute | solution.py:482
  23.1 0.8 collective-permute-start.7
  23.9 0.5 collective-permute-start.6
  24.4 8.9 %all-to-all-start = ((bf16[128,100,128]{2,1,0:T(8,128)(2,1)}), bf16[128,100,128]{2,1,0:T(8,128)(2,1)}, u32[]{:S(2)}, u32[]{:S(2)}) async-start(bf16[128,100,128]{2,1,0:T(8,128)(2,1)} %bitcast.25), calls=%async_computation | async-start | bytes 6815744 | tf_op jit(solution)/shard_map/all_to_all | solution.py:528
  33.4 0.0 copy-done.1
  33.4 0.0 copy-start
  33.4 0.0 collective-permute-done.8
  33.4 0.0 collective-permute-done.7
  33.4 0.0 collective-permute-done.6
  33.4 0.1 pad_maximum_fusion
  33.5 0.3 copy.18
  33.9 0.3 collective-permute-start.9
  34.1 0.5 copy-done
  34.6 0.1 broadcast_multiply_fusion
  34.7 0.1 convert_element_type.6
  34.8 0.1 constant_dynamic-slice_fusion
  34.9 0.1 reshape.164
  35.0 1.1 gather_fusion.1
  36.1 1.2 gather_fusion
  37.3 0.6 pad_add_fusion.place_ref
  37.8 0.9 fusion.count_ref
  38.7 0.0 collective-permute-done.9
  38.7 1.7 %maximum_select_fusion = bf16[16,2,2,100,128]{4,0,3,1,2:T(8,128)(2,1)S(1)} fusion(bf16[16,2,1,100,128]{4,0,3,1,2:T(8,128)(2,1)} %bitcast.21, bf16[16,2,1,100,128]{4,0,3,1,2:T(8,128)(2,1)S(1)} %bitcast.27, pred[]{:T(512)S(6)} %eq.14), kind=kLoop, calls=%fused_computation.2 | loop fusion | flops 2457600 | bytes 3276801 | tf_op jit(solution)/shard_map/jit(_where)/select_n | solution.py:511
  40.4 1.7 %copy.20 = bf16[16,2,2,100,128]{4,3,2,1,0:T(8,128)(2,1)} copy(bf16[16,2,2,100,128]{4,0,3,1,2:T(8,128)(2,1)S(1)} %maximum_select_fusion) | data formatting | bytes 3276800 | tf_op jit(solution)/shard_map/jit(_where)/select_n | solution.py:511
  42.0 33.1 %shard_map.137.left_hbm = bf16[208,128,128]{2,1,0:T(8,128)(2,1)} custom-call(bf16[16,4,100,128]{3,2,1,0:T(8,128)(2,1)} %bitcast.28, f32[16,1,128]{2,1,0:T(1,128)} %bitcast.43, bf16[832,896]{1,0:T(8,128)(2,1)} %constant.51.clone.table_ref, f32[832,128]{1,0:T(8,128)} %constant.52.clone.sums_ref, bf16[2,208,512]{2,1,0:T(8,128)(2,1)} %constant.53.clone.band_ref, ...), custom_call_target="tpu_custom_call" | custom-call | flops 3053453312 | bytes 5505024 | tf_op jit(solution)/shard_map/pallas_call | solution.py:242
  75.1 2.5 %all-to-all-done = bf16[128,100,128]{2,1,0:T(8,128)(2,1)} async-done(((bf16[128,100,128]{2,1,0:T(8,128)(2,1)}), bf16[128,100,128]{2,1,0:T(8,128)(2,1)}, u32[]{:S(2)}, u32[]{:S(2)}) %all-to-all-start) | async-done | bytes 3276832 | tf_op jit(solution)/shard_map/all_to_all | solution.py:528
  77.6 32.6 %shard_map.138 = (bf16[401,32,128]{2,1,0:T(8,128)(2,1)}, bf16[401,32,128]{2,1,0:T(8,128)(2,1)}) custom-call(s32[2]{0:T(128)} %pad_add_fusion.place_ref, bf16[4,4,2,4,100,128]{5,4,3,2,1,0:T(8,128)(2,1)} %bitcast.11.x_ref, f32[16,2,1,128]{3,2,1,0:T(1,128)} %bitcast.42, bf16[2,416,512]{2,1,0:T(8,128)(2,1)} %constant.55.clone.table_ref, ...), custom_call_target="tpu_custom_call" | custom-call | flops 30000001024 | bytes 25165824 | tf_op jit(solution)/shard_map/pallas_call | solution.py:388
  110.3 0.1 collective-permute-start.10
  110.4 5.7 %shard_map.139.stacks_ref = f32[401,32,256]{2,1,0:T(8,128)} custom-call(s32[2]{0:T(128)} %pad_add_fusion.place_ref, bf16[401,32,128]{2,1,0:T(8,128)(2,1)} %get-tuple-element.15.added_ref, bf16[401,32,256]{2,1,0:T(8,128)(2,1)} %old_ref.3), custom_call_target="tpu_custom_call" | custom-call | flops 1642496 | bytes 13631488 | tf_op jit(solution)/shard_map/pallas_call | solution.py:435
  116.1 0.5 collective-permute-done.10.added_ref
  116.5 5.7 %shard_map.140 = f32[401,32,256]{2,1,0:T(8,128)} custom-call(s32[2]{0:T(128)} %pad_add_fusion.place_ref, f32[401,32,256]{2,1,0:T(8,128)} %shard_map.139.stacks_ref, bf16[401,32,128]{2,1,0:T(8,128)(2,1)} %collective-permute-done.10.added_ref, bf16[401,32,256]{2,1,0:T(8,128)(2,1)} %old_ref.3), custom_call_target="tpu_custom_call", output_to_operand_aliasing={{}: (1, {})} | custom-call | flops 1642496 | bytes 13631488 | tf_op jit(solution)/shard_map/pallas_call | solution.py:435
  (6 shorter events, 0.1 us)
Async XLA Ops:
  0.9 10.3 %collective-permute-start = (bf16[100,64]{1,0:T(8,128)(2,1)S(1)}, bf16[100,64]{1,0:T(8,128)(2,1)S(1)}, u32[]{:S(2)}, u32[]{:S(2)}) collective-permute-start(bf16[100,64]{1,0:T(8,128)(2,1)S(1)} %get-tuple-element.17), channel_id=1, source_target_pairs={{0,4},{1,5},{2,6},{3,7},{4,0},{5,1},{6,2},{7,3},{8,12},{9,13},{10,... | collective-permute-start | bytes 38408 | tf_op jit(solution)/shard_map/ppermute | solution.py:482
  3.0 8.3 %collective-permute-start.2 = (bf16[100,64]{1,0:T(8,128)(2,1)S(1)}, bf16[100,64]{1,0:T(8,128)(2,1)S(1)}, u32[]{:S(2)}, u32[]{:S(2)}) collective-permute-start(bf16[100,64]{1,0:T(8,128)(2,1)S(1)} %get-tuple-element.18), channel_id=1, source_target_pairs={{0,6},{1,7},{2,4},{3,5},{4,2},{5,3},{6,0},{7,1},{8,14},{9,15},{10,... | collective-permute-start | bytes 38408 | tf_op jit(solution)/shard_map/ppermute | solution.py:482
  5.5 5.8 %collective-permute-start.1 = (bf16[100,64]{1,0:T(8,128)(2,1)S(1)}, bf16[100,64]{1,0:T(8,128)(2,1)S(1)}, u32[]{:S(2)}, u32[]{:S(2)}) collective-permute-start(bf16[100,64]{1,0:T(8,128)(2,1)S(1)} %get-tuple-element.18), channel_id=1, source_target_pairs={{0,2},{1,3},{2,0},{3,1},{4,6},{5,7},{6,4},{7,5},{8,10},{9,11},{10,... | collective-permute-start | bytes 38408 | tf_op jit(solution)/shard_map/ppermute | solution.py:482
  11.4 5.4 %collective-permute-start.5 = (bf16[2,100,128]{2,1,0:T(8,128)(2,1)S(1)}, bf16[2,100,128]{2,1,0:T(8,128)(2,1)S(1)}, u32[]{:S(2)}, u32[]{:S(2)}) collective-permute-start(bf16[2,100,128]{2,1,0:T(8,128)(2,1)S(1)} %maximum_select_fusion.1), channel_id=1, source_target_pairs={{0,24},{1,25},{2,26},{3,27},{4,28},{5,29},{6,30},{7,31},{8,16},{9,... | collective-permute-start | bytes 153608 | tf_op jit(solution)/shard_map/ppermute | solution.py:482
  14.5 5.6 %collective-permute-start.4 = (bf16[2,100,128]{2,1,0:T(8,128)(2,1)S(1)}, bf16[2,100,128]{2,1,0:T(8,128)(2,1)S(1)}, u32[]{:S(2)}, u32[]{:S(2)}) collective-permute-start(bf16[2,100,128]{2,1,0:T(8,128)(2,1)S(1)} %maximum_select_fusion.1), channel_id=1, source_target_pairs={{0,16},{1,17},{2,18},{3,19},{4,20},{5,21},{6,22},{7,23},{8,24},{9,... | collective-permute-start | bytes 153608 | tf_op jit(solution)/shard_map/ppermute | solution.py:482
  15.2 5.0 %collective-permute-start.3 = (bf16[2,100,128]{2,1,0:T(8,128)(2,1)S(1)}, bf16[2,100,128]{2,1,0:T(8,128)(2,1)S(1)}, u32[]{:S(2)}, u32[]{:S(2)}) collective-permute-start(bf16[2,100,128]{2,1,0:T(8,128)(2,1)S(1)} %maximum_select_fusion.1), channel_id=1, source_target_pairs={{0,8},{1,9},{2,10},{3,11},{4,12},{5,13},{6,14},{7,15},{8,0},{9,1},... | collective-permute-start | bytes 153608 | tf_op jit(solution)/shard_map/ppermute | solution.py:482
  20.2 13.1 %copy-start.1 = (s32[8192]{0:T(1024)S(1)}, s32[8192]{0:T(1024)}, u32[]{:S(2)}) copy-start(s32[8192]{0:T(1024)} %param.15) | copy-start | bytes 98308
  20.2 13.2 %collective-permute-start.8 = (bf16[4,2,100,128]{3,2,1,0:T(8,128)(2,1)S(1)}, bf16[4,2,100,128]{3,2,1,0:T(8,128)(2,1)S(1)}, u32[]{:S(2)}, u32[]{:S(2)}) collective-permute-start(bf16[4,2,100,128]{3,2,1,0:T(8,128)(2,1)S(1)} %pad_maximum_fusion.1), channel_id=1, source_target_pairs={{0,96},{1,97},{2,98},{3,99},{4,100},{5,101},{6,102},{7,103},{8,104... | collective-permute-start | bytes 614408 | tf_op jit(solution)/shard_map/ppermute | solution.py:482
  23.1 10.3 %collective-permute-start.7 = (bf16[4,2,100,128]{3,2,1,0:T(8,128)(2,1)S(1)}, bf16[4,2,100,128]{3,2,1,0:T(8,128)(2,1)S(1)}, u32[]{:S(2)}, u32[]{:S(2)}) collective-permute-start(bf16[4,2,100,128]{3,2,1,0:T(8,128)(2,1)S(1)} %pad_maximum_fusion.1), channel_id=1, source_target_pairs={{0,64},{1,65},{2,66},{3,67},{4,68},{5,69},{6,70},{7,71},{8,72},{9,... | collective-permute-start | bytes 614408 | tf_op jit(solution)/shard_map/ppermute | solution.py:482
  23.9 9.5 %collective-permute-start.6 = (bf16[4,2,100,128]{3,2,1,0:T(8,128)(2,1)S(1)}, bf16[4,2,100,128]{3,2,1,0:T(8,128)(2,1)S(1)}, u32[]{:S(2)}, u32[]{:S(2)}) collective-permute-start(bf16[4,2,100,128]{3,2,1,0:T(8,128)(2,1)S(1)} %pad_maximum_fusion.1), channel_id=1, source_target_pairs={{0,32},{1,33},{2,34},{3,35},{4,36},{5,37},{6,38},{7,39},{8,40},{9,... | collective-permute-start | bytes 614408 | tf_op jit(solution)/shard_map/ppermute | solution.py:482
  24.4 53.2 %all-to-all-start = ((bf16[128,100,128]{2,1,0:T(8,128)(2,1)}), bf16[128,100,128]{2,1,0:T(8,128)(2,1)}, u32[]{:S(2)}, u32[]{:S(2)}) async-start(bf16[128,100,128]{2,1,0:T(8,128)(2,1)} %bitcast.25), calls=%async_computation | async-start | bytes 6815744 | tf_op jit(solution)/shard_map/all_to_all | solution.py:528
  33.4 1.2 %copy-start = (s32[32,8192]{1,0:T(8,128)S(1)}, s32[32,8192]{1,0:T(8,128)}, u32[]{:S(2)}) copy-start(s32[32,8192]{1,0:T(8,128)} %param.16) | copy-start | bytes 3145732
  33.9 4.8 %collective-permute-start.9 = (bf16[16,2,100,128]{3,0,2,1:T(8,128)(2,1)S(1)}, bf16[16,2,100,128]{3,0,2,1:T(8,128)(2,1)}, u32[]{:S(2)}, u32[]{:S(2)}) collective-permute-start(bf16[16,2,100,128]{3,0,2,1:T(8,128)(2,1)S(1)} %bitcast.26), channel_id=1, source_target_pairs={{0,1},{1,0},{2,3},{3,2},{4,5},{5,4},{6,7},{7,6},{8,9},{9,8},{10,11... | collective-permute-start | bytes 2457608 | tf_op jit(solution)/shard_map/ppermute | solution.py:482
  110.3 6.3 %collective-permute-start.10 = (bf16[401,32,128]{2,1,0:T(8,128)(2,1)}, bf16[401,32,128]{2,1,0:T(8,128)(2,1)}, u32[]{:S(2)}, u32[]{:S(2)}) collective-permute-start(bf16[401,32,128]{2,1,0:T(8,128)(2,1)} %get-tuple-element.16), channel_id=1, source_target_pairs={{0,1},{1,0},{2,3},{3,2},{4,5},{5,4},{6,7},{7,6},{8,9},{9,8},{10,11... | collective-permute-start | bytes 9854984 | tf_op jit(solution)/shard_map/ppermute | solution.py:545

commit v6 on v5

--- a/solution.py
+++ b/solution.py
@@ -206,15 +206,22 @@
     @pl.when(step == pl.num_programs(0) - 1)
     def _():
         low_lanes = lax.broadcasted_iota(jnp.int32, (SRC, HALF), 1) < HALF // 2
-
-        @pl.loop(0, FREQ // 4)
+        unit = lax.broadcasted_iota(jnp.int32, (HALF, HALF), 0) == lax.broadcasted_iota(jnp.int32, (HALF, HALF), 1)
+        unit = unit.astype(jnp.bfloat16)
+
+        @pl.loop(0, FREQ // 4, unroll=4)
         def _(quad):
+            rows = [
+                held[part, pl.ds(pl.multiple_of((4 * quad + i) * SPITCH, 8), SUB), :]
+                for part in range(2)
+                for i in range(4)
+            ]
+            rows = jnp.concatenate(rows, axis=0).astype(jnp.bfloat16)
+            turned = lax.dot_general(unit, rows, (((1,), (1,)), ((), ())), preferred_element_type=jnp.float32)
             for part in range(2):
-                rows = [
-                    held[part, pl.ds(pl.multiple_of((4 * quad + i) * SPITCH, 8), SUB), :] for i in range(4)
-                ]
-                turned = jnp.concatenate(rows, axis=0).T
-                first, second = turned[:SRC], turned[SRC:]
+                first, second = (
+                    turned[i * SRC : (i + 1) * SRC, part * HALF : (part + 1) * HALF] for i in range(2)
+                )
                 pairs = (
                     jnp.where(low_lanes, first, pltpu.roll(second, HALF // 2, 1)),
                     jnp.where(low_lanes, pltpu.roll(first, HALF // 2, 1), second),
@@ -252,7 +259,7 @@
         scratch_shapes=[
             pltpu.VMEM((DEPTH, 2 * HALF), jnp.bfloat16),
             pltpu.VMEM((2 * FREQ, 2 * HALF), jnp.float32),
-            pltpu.VMEM((2, FREQ * SPITCH, HALF), jnp.float32),
+            pltpu.VMEM((2, (FREQ + 1) * SPITCH, HALF), jnp.float32),
         ],
         compiler_params=pltpu.CompilerParams(vmem_limit_bytes=VMEM),
         cost_estimate=whiten_cost(SUB // 2),
@@ -403,12 +410,12 @@
             scratch_shapes=[
                 pltpu.VMEM((2, 2, REACH, 2 * HALF), jnp.bfloat16),
                 pltpu.VMEM((2, 2, FREQ, 2 * HALF), jnp.float32),
-                pltpu.VMEM((FREQ * PITCH, HALF), jnp.float32),
+                pltpu.VMEM(((FREQ + 1) * PITCH, HALF), jnp.float32),
                 pltpu.VMEM(left.shape, left.dtype),
                 pltpu.VMEM((ROWS, FREQ, HALF), jnp.bfloat16),
-                pltpu.VMEM((2, BLOCK * XPITCH, HALF), jnp.float32),
-                pltpu.VMEM((2, SHIFTS * BLOCK, HALF), jnp.float32),
-                pltpu.VMEM((2, SHIFTS * BLOCK, HALF), jnp.float32),
+                pltpu.VMEM((2, (BLOCK + 1) * XPITCH, HALF), jnp.float32),
+                pltpu.VMEM((2, (SHIFTS + 1) * BLOCK, HALF), jnp.float32),
+                pltpu.VMEM((2, (SHIFTS + 1) * BLOCK, HALF), jnp.float32),
                 pltpu.VMEM((SRC // BLOCK, LAGS, BLOCK, HALF), jnp.bfloat16),
                 pltpu.SemaphoreType.DMA((1 + SRC // BLOCK,)),
             ],
@@ -497,12 +504,19 @@
     return jnp.where(z_high == 0, jnp.stack([mine, theirs]), jnp.stack([theirs, mine]))
 
 
-def along_y(near):
-    return jnp.stack([near] + [send(near, lambda x, y, l, h, c, d=d: (x, y ^ d, l, h, c)) for d in (1, 2, 3)])
-
-
-def along_x(column):
-    plane = jnp.stack([column] + [send(column, lambda x, y, l, h, c, d=d: (x ^ d, y, l, h, c)) for d in (1, 2, 3)])
+def first_round(near):
+    def route(d):
+        return lambda x, y, l, h, c: (x, y ^ d, l, h, c) if c == 0 else (x ^ d, y, l, h, c)
+
+    return jnp.stack([near] + [send(near, route(d)) for d in (1, 2, 3)])
+
+
+def second_round(line, core):
+    def route(d):
+        return lambda x, y, l, h, c: (x ^ d, y, l, h, c) if c == 0 else (x, y ^ d, l, h, c)
+
+    plane = jnp.stack([line] + [send(line, route(d)) for d in (1, 2, 3)])
+    plane = jnp.where(core == 0, plane, plane.swapaxes(0, 1))
     return plane.reshape(SUB // 2, 2, PIECE, HALF)
 
 
@@ -523,8 +537,8 @@
 
     pieces = outgoing(record)
     near, pieces = lax.optimization_barrier((near_sources(record, z_low, chip), pieces))
-    column, pieces = lax.optimization_barrier((along_y(near), pieces))
-    plane = along_x(column)
+    line, pieces = lax.optimization_barrier((first_round(near), pieces))
+    plane = second_round(line, core)
     receivers = lax.all_to_all(pieces, ("rcv", "src"), split_axis=0, concat_axis=0, tiled=True)
     sources = both_cores(plane, core)
 

time: 124 us -> 124 us (level)
  waiting for transfers between devices: 7.53 us -> 17.8 us
  Pallas kernels: 81.8 us -> 71.8 us
    pallas_call x1, Pallas kernels: 33.1 us -> 22.7 us  [whiten_sources(): pl.pallas_call(whiten_sources_kernel, grid=(SUB // 4,), in_specs=[pl.Bloc...]
    all_to_all x1, waiting for transfers between devices: 2.49 us -> 12.8 us  [on_device(): lax.all_to_all(pieces, ('rcv', 'src'), split_axis=0, concat_axis=0, tiled...]
  transfers between devices with their start and end apart: 12 -> 12, of which waited for: 4 -> 4; matrix products, arithmetic and copies ran while one was open for 6% -> 7% of each run, Pallas kernels for 36% -> 27%
where the time goes in v6:
time: 124 us; the launch traced here: 123 us
  Pallas kernels  71.8 us (58%)
  starting transfers between devices  23.3 us (19%)
  waiting for transfers between devices  17.8 us (14%)
  local copies, waits for them, and re-layouts  5.03 us (4%)
  other arithmetic  3.67 us (3%)
    pallas_call x1, Pallas kernels, stack_halves(): pl.pallas_call(stack_kernel, grid_spec=pltpu.PrefetchScalarGridSpec(num_s...  33 us
    pallas_call x1, Pallas kernels, whiten_sources(): pl.pallas_call(whiten_sources_kernel, grid=(SUB // 4,), in_specs=[pl.Bloc...  22.7 us
    ppermute x10, starting transfers between devices, send(): lax.ppermute(value, ('rcv', 'src'), [(device(*place), device(*route(*plac...  14.3 us
    all_to_all x1, waiting for transfers between devices, on_device(): lax.all_to_all(pieces, ('rcv', 'src'), split_axis=0, concat_axis=0, tiled...  12.8 us
    pallas_call x2, Pallas kernels, add_half(): pl.pallas_call(add_kernel if first else add_rest_kernel, grid_spec=pltpu....  11.5 us
    all_to_all x1, starting transfers between devices, on_device(): lax.all_to_all(pieces, ('rcv', 'src'), split_axis=0, concat_axis=0, tiled...  8.95 us
    pallas_call x1, Pallas kernels, outgoing(): pl.pallas_call(outgoing_kernel, grid=(steps,), in_specs=[pl.BlockSpec((PI...  4.64 us
    ppermute x10, waiting for transfers between devices, send(): lax.ppermute(value, ('rcv', 'src'), [(device(*place), device(*route(*plac...  4.58 us
  transfers between devices with their start and end apart: 12, of which 4 were waited for; matrix products, arithmetic and copies ran while one was open for 7% of the time, Pallas kernels for 27%

profile of v6, /device:TPU:0, one launch (start us, length us, event | category | flops | bytes accessed | tf_op | source)
XLA Modules:
  0.0 122.7 jit_solution(3740185479370154395)
XLA Ops:
  0.0 0.9 broadcast_select_fusion.1
  0.9 2.1 %collective-permute-start = (bf16[100,64]{1,0:T(8,128)(2,1)S(1)}, bf16[100,64]{1,0:T(8,128)(2,1)S(1)}, u32[]{:S(2)}, u32[]{:S(2)}) collective-permute-start(bf16[100,64]{1,0:T(8,128)(2,1)S(1)} %get-tuple-element.17), channel_id=1, source_target_pairs={{0,4},{1,5},{2,6},{3,7},{4,0},{5,1},{6,2},{7,3},{8,12},{9,13},{10,... | collective-permute-start | bytes 38408 | tf_op jit(solution)/shard_map/ppermute | solution.py:489
  3.0 2.5 %collective-permute-start.2 = (bf16[100,64]{1,0:T(8,128)(2,1)S(1)}, bf16[100,64]{1,0:T(8,128)(2,1)S(1)}, u32[]{:S(2)}, u32[]{:S(2)}) collective-permute-start(bf16[100,64]{1,0:T(8,128)(2,1)S(1)} %get-tuple-element.18), channel_id=1, source_target_pairs={{0,6},{1,7},{2,4},{3,5},{4,2},{5,3},{6,0},{7,1},{8,14},{9,15},{10,... | collective-permute-start | bytes 38408 | tf_op jit(solution)/shard_map/ppermute | solution.py:489
  5.5 1.1 collective-permute-start.1
  6.6 4.6 %shard_map.136 = bf16[32,2,2,100,128]{4,3,2,1,0:T(8,128)(2,1)} custom-call(bf16[100,8192]{1,0:T(8,128)(2,1)} %record_ref.1, bf16[100,100]{1,0:T(8,128)(2,1)} %constant.50.clone.order_ref), custom_call_target="tpu_custom_call" | custom-call | bytes 5242880 | tf_op jit(solution)/shard_map/pallas_call | solution.py:471
  11.2 0.0 collective-permute-done
  11.2 0.1 maximum_select_fusion.2
  11.3 0.0 collective-permute-done.2
  11.3 0.0 collective-permute-done.1
  11.3 0.1 maximum_select_fusion.3
  11.5 3.1 %collective-permute-start.5 = (bf16[2,100,128]{2,1,0:T(8,128)(2,1)S(1)}, bf16[2,100,128]{2,1,0:T(8,128)(2,1)S(1)}, u32[]{:S(2)}, u32[]{:S(2)}) collective-permute-start(bf16[2,100,128]{2,1,0:T(8,128)(2,1)S(1)} %maximum_select_fusion.1), channel_id=1, source_target_pairs={{0,24},{1,97},{2,26},{3,99},{4,28},{5,101},{6,30},{7,103},{8,16},{... | collective-permute-start | bytes 153608 | tf_op jit(solution)/shard_map/ppermute | solution.py:489
  14.5 0.6 collective-permute-start.4
  15.2 0.5 collective-permute-start.3
  15.6 1.2 %collective-permute-done.5 = bf16[2,100,128]{2,1,0:T(8,128)(2,1)S(1)} collective-permute-done((bf16[2,100,128]{2,1,0:T(8,128)(2,1)S(1)}, bf16[2,100,128]{2,1,0:T(8,128)(2,1)S(1)}, u32[]{:S(2)}, u32[]{:S(2)}) %collective-permute-start.5) | collective-permute-done | bytes 51232 | tf_op jit(solution)/shard_map/ppermute | solution.py:489
  16.9 3.3 %collective-permute-done.4 = bf16[2,100,128]{2,1,0:T(8,128)(2,1)S(1)} collective-permute-done((bf16[2,100,128]{2,1,0:T(8,128)(2,1)S(1)}, bf16[2,100,128]{2,1,0:T(8,128)(2,1)S(1)}, u32[]{:S(2)}, u32[]{:S(2)}) %collective-permute-start.4) | collective-permute-done | bytes 51232 | tf_op jit(solution)/shard_map/ppermute | solution.py:489
  20.2 0.0 collective-permute-done.3
  20.2 2.8 %collective-permute-start.8 = (bf16[4,2,100,128]{3,2,1,0:T(8,128)(2,1)S(1)}, bf16[4,2,100,128]{3,2,1,0:T(8,128)(2,1)S(1)}, u32[]{:S(2)}, u32[]{:S(2)}) collective-permute-start(bf16[4,2,100,128]{3,2,1,0:T(8,128)(2,1)S(1)} %pad_maximum_fusion.1), channel_id=1, source_target_pairs={{0,96},{1,25},{2,98},{3,27},{4,100},{5,29},{6,102},{7,31},{8,104},... | collective-permute-start | bytes 614408 | tf_op jit(solution)/shard_map/ppermute | solution.py:489
  23.1 0.8 collective-permute-start.7
  23.9 0.5 collective-permute-start.6
  24.4 0.0 copy-done.1
  24.4 8.9 %all-to-all-start = ((bf16[128,100,128]{2,1,0:T(8,128)(2,1)}), bf16[128,100,128]{2,1,0:T(8,128)(2,1)}, u32[]{:S(2)}, u32[]{:S(2)}) async-start(bf16[128,100,128]{2,1,0:T(8,128)(2,1)} %bitcast.27), calls=%async_computation | async-start | bytes 6815744 | tf_op jit(solution)/shard_map/all_to_all | solution.py:542
  33.4 0.0 collective-permute-done.8
  33.4 0.0 collective-permute-done.7
  33.4 0.0 collective-permute-done.6
  33.4 0.1 pad_maximum_fusion
  33.5 0.0 copy-start
  33.5 0.1 bitcast_select_fusion
  33.6 0.3 copy.20
  33.9 0.3 collective-permute-start.9
  34.2 0.5 copy-done
  34.7 0.1 broadcast_multiply_fusion
  34.8 0.1 convert_element_type.6
  34.9 0.1 constant_dynamic-slice_fusion
  35.0 0.1 reshape.164
  35.1 1.1 gather_fusion.1
  36.2 1.2 gather_fusion
  37.4 0.6 pad_add_fusion.place_ref
  38.0 0.9 fusion.count_ref
  38.8 0.0 collective-permute-done.9
  38.8 1.7 %maximum_select_fusion = bf16[16,2,2,100,128]{4,0,3,1,2:T(8,128)(2,1)S(1)} fusion(bf16[16,2,1,100,128]{4,0,3,1,2:T(8,128)(2,1)} %bitcast.22, bf16[16,2,1,100,128]{4,0,3,1,2:T(8,128)(2,1)S(1)} %bitcast.29, pred[]{:T(512)S(6)} %eq.15), kind=kLoop, calls=%fused_computation.2 | loop fusion | flops 2457600 | bytes 3276801 | tf_op jit(solution)/shard_map/jit(_where)/select_n | solution.py:525
  40.5 1.7 %copy.22 = bf16[16,2,2,100,128]{4,3,2,1,0:T(8,128)(2,1)} copy(bf16[16,2,2,100,128]{4,0,3,1,2:T(8,128)(2,1)S(1)} %maximum_select_fusion) | data formatting | bytes 3276800 | tf_op jit(solution)/shard_map/jit(_where)/select_n | solution.py:525
  42.2 22.7 %shard_map.137.left_hbm = bf16[208,128,128]{2,1,0:T(8,128)(2,1)} custom-call(bf16[16,4,100,128]{3,2,1,0:T(8,128)(2,1)} %bitcast.30, f32[16,1,128]{2,1,0:T(1,128)} %bitcast.45, bf16[832,896]{1,0:T(8,128)(2,1)} %constant.51.clone.table_ref, f32[832,128]{1,0:T(8,128)} %constant.52.clone.sums_ref, bf16[2,208,512]{2,1,0:T(8,128)(2,1)} %constant.53.clone.band_ref, ...), custom_call_target="tpu_custom_call" | custom-call | flops 3053453312 | bytes 5505024 | tf_op jit(solution)/shard_map/pallas_call | solution.py:249
  64.9 12.8 %all-to-all-done = bf16[128,100,128]{2,1,0:T(8,128)(2,1)} async-done(((bf16[128,100,128]{2,1,0:T(8,128)(2,1)}), bf16[128,100,128]{2,1,0:T(8,128)(2,1)}, u32[]{:S(2)}, u32[]{:S(2)}) %all-to-all-start) | async-done | bytes 3276832 | tf_op jit(solution)/shard_map/all_to_all | solution.py:542
  77.7 33.0 %shard_map.138 = (bf16[401,32,128]{2,1,0:T(8,128)(2,1)}, bf16[401,32,128]{2,1,0:T(8,128)(2,1)}) custom-call(s32[2]{0:T(128)} %pad_add_fusion.place_ref, bf16[4,4,2,4,100,128]{5,4,3,2,1,0:T(8,128)(2,1)} %bitcast.11.x_ref, f32[16,2,1,128]{3,2,1,0:T(1,128)} %bitcast.44, bf16[2,416,512]{2,1,0:T(8,128)(2,1)} %constant.55.clone.table_ref, ...), custom_call_target="tpu_custom_call" | custom-call | flops 30000001024 | bytes 25165824 | tf_op jit(solution)/shard_map/pallas_call | solution.py:395
  110.7 0.1 collective-permute-start.10
  110.7 5.7 %shard_map.139.stacks_ref = f32[401,32,256]{2,1,0:T(8,128)} custom-call(s32[2]{0:T(128)} %pad_add_fusion.place_ref, bf16[401,32,128]{2,1,0:T(8,128)(2,1)} %get-tuple-element.15.added_ref, bf16[401,32,256]{2,1,0:T(8,128)(2,1)} %old_ref.3), custom_call_target="tpu_custom_call" | custom-call | flops 1642496 | bytes 13631488 | tf_op jit(solution)/shard_map/pallas_call | solution.py:442
  116.5 0.5 collective-permute-done.10.added_ref
  116.9 5.7 %shard_map.140 = f32[401,32,256]{2,1,0:T(8,128)} custom-call(s32[2]{0:T(128)} %pad_add_fusion.place_ref, f32[401,32,256]{2,1,0:T(8,128)} %shard_map.139.stacks_ref, bf16[401,32,128]{2,1,0:T(8,128)(2,1)} %collective-permute-done.10.added_ref, bf16[401,32,256]{2,1,0:T(8,128)(2,1)} %old_ref.3), custom_call_target="tpu_custom_call", output_to_operand_aliasing={{}: (1, {})} | custom-call | flops 1642496 | bytes 13631488 | tf_op jit(solution)/shard_map/pallas_call | solution.py:442
  (7 shorter events, 0.1 us)
Async XLA Ops:
  0.9 10.3 %collective-permute-start = (bf16[100,64]{1,0:T(8,128)(2,1)S(1)}, bf16[100,64]{1,0:T(8,128)(2,1)S(1)}, u32[]{:S(2)}, u32[]{:S(2)}) collective-permute-start(bf16[100,64]{1,0:T(8,128)(2,1)S(1)} %get-tuple-element.17), channel_id=1, source_target_pairs={{0,4},{1,5},{2,6},{3,7},{4,0},{5,1},{6,2},{7,3},{8,12},{9,13},{10,... | collective-permute-start | bytes 38408 | tf_op jit(solution)/shard_map/ppermute | solution.py:489
  3.0 8.3 %collective-permute-start.2 = (bf16[100,64]{1,0:T(8,128)(2,1)S(1)}, bf16[100,64]{1,0:T(8,128)(2,1)S(1)}, u32[]{:S(2)}, u32[]{:S(2)}) collective-permute-start(bf16[100,64]{1,0:T(8,128)(2,1)S(1)} %get-tuple-element.18), channel_id=1, source_target_pairs={{0,6},{1,7},{2,4},{3,5},{4,2},{5,3},{6,0},{7,1},{8,14},{9,15},{10,... | collective-permute-start | bytes 38408 | tf_op jit(solution)/shard_map/ppermute | solution.py:489
  5.5 5.8 %collective-permute-start.1 = (bf16[100,64]{1,0:T(8,128)(2,1)S(1)}, bf16[100,64]{1,0:T(8,128)(2,1)S(1)}, u32[]{:S(2)}, u32[]{:S(2)}) collective-permute-start(bf16[100,64]{1,0:T(8,128)(2,1)S(1)} %get-tuple-element.18), channel_id=1, source_target_pairs={{0,2},{1,3},{2,0},{3,1},{4,6},{5,7},{6,4},{7,5},{8,10},{9,11},{10,... | collective-permute-start | bytes 38408 | tf_op jit(solution)/shard_map/ppermute | solution.py:489
  6.6 17.8 %copy-start.1 = (s32[8192]{0:T(1024)S(1)}, s32[8192]{0:T(1024)}, u32[]{:S(2)}) copy-start(s32[8192]{0:T(1024)} %param.15) | copy-start | bytes 98308
  11.5 5.4 %collective-permute-start.5 = (bf16[2,100,128]{2,1,0:T(8,128)(2,1)S(1)}, bf16[2,100,128]{2,1,0:T(8,128)(2,1)S(1)}, u32[]{:S(2)}, u32[]{:S(2)}) collective-permute-start(bf16[2,100,128]{2,1,0:T(8,128)(2,1)S(1)} %maximum_select_fusion.1), channel_id=1, source_target_pairs={{0,24},{1,97},{2,26},{3,99},{4,28},{5,101},{6,30},{7,103},{8,16},{... | collective-permute-start | bytes 153608 | tf_op jit(solution)/shard_map/ppermute | solution.py:489
  14.5 5.6 %collective-permute-start.4 = (bf16[2,100,128]{2,1,0:T(8,128)(2,1)S(1)}, bf16[2,100,128]{2,1,0:T(8,128)(2,1)S(1)}, u32[]{:S(2)}, u32[]{:S(2)}) collective-permute-start(bf16[2,100,128]{2,1,0:T(8,128)(2,1)S(1)} %maximum_select_fusion.1), channel_id=1, source_target_pairs={{0,16},{1,65},{2,18},{3,67},{4,20},{5,69},{6,22},{7,71},{8,24},{9,... | collective-permute-start | bytes 153608 | tf_op jit(solution)/shard_map/ppermute | solution.py:489
  15.2 5.0 %collective-permute-start.3 = (bf16[2,100,128]{2,1,0:T(8,128)(2,1)S(1)}, bf16[2,100,128]{2,1,0:T(8,128)(2,1)S(1)}, u32[]{:S(2)}, u32[]{:S(2)}) collective-permute-start(bf16[2,100,128]{2,1,0:T(8,128)(2,1)S(1)} %maximum_select_fusion.1), channel_id=1, source_target_pairs={{0,8},{1,33},{2,10},{3,35},{4,12},{5,37},{6,14},{7,39},{8,0},{9,41... | collective-permute-start | bytes 153608 | tf_op jit(solution)/shard_map/ppermute | solution.py:489
  20.2 13.1 %collective-permute-start.8 = (bf16[4,2,100,128]{3,2,1,0:T(8,128)(2,1)S(1)}, bf16[4,2,100,128]{3,2,1,0:T(8,128)(2,1)S(1)}, u32[]{:S(2)}, u32[]{:S(2)}) collective-permute-start(bf16[4,2,100,128]{3,2,1,0:T(8,128)(2,1)S(1)} %pad_maximum_fusion.1), channel_id=1, source_target_pairs={{0,96},{1,25},{2,98},{3,27},{4,100},{5,29},{6,102},{7,31},{8,104},... | collective-permute-start | bytes 614408 | tf_op jit(solution)/shard_map/ppermute | solution.py:489
  23.1 10.3 %collective-permute-start.7 = (bf16[4,2,100,128]{3,2,1,0:T(8,128)(2,1)S(1)}, bf16[4,2,100,128]{3,2,1,0:T(8,128)(2,1)S(1)}, u32[]{:S(2)}, u32[]{:S(2)}) collective-permute-start(bf16[4,2,100,128]{3,2,1,0:T(8,128)(2,1)S(1)} %pad_maximum_fusion.1), channel_id=1, source_target_pairs={{0,64},{1,17},{2,66},{3,19},{4,68},{5,21},{6,70},{7,23},{8,72},{9,... | collective-permute-start | bytes 614408 | tf_op jit(solution)/shard_map/ppermute | solution.py:489
  23.9 9.5 %collective-permute-start.6 = (bf16[4,2,100,128]{3,2,1,0:T(8,128)(2,1)S(1)}, bf16[4,2,100,128]{3,2,1,0:T(8,128)(2,1)S(1)}, u32[]{:S(2)}, u32[]{:S(2)}) collective-permute-start(bf16[4,2,100,128]{3,2,1,0:T(8,128)(2,1)S(1)} %pad_maximum_fusion.1), channel_id=1, source_target_pairs={{0,32},{1,9},{2,34},{3,11},{4,36},{5,13},{6,38},{7,15},{8,40},{9,1... | collective-permute-start | bytes 614408 | tf_op jit(solution)/shard_map/ppermute | solution.py:489
  24.4 53.2 %all-to-all-start = ((bf16[128,100,128]{2,1,0:T(8,128)(2,1)}), bf16[128,100,128]{2,1,0:T(8,128)(2,1)}, u32[]{:S(2)}, u32[]{:S(2)}) async-start(bf16[128,100,128]{2,1,0:T(8,128)(2,1)} %bitcast.27), calls=%async_computation | async-start | bytes 6815744 | tf_op jit(solution)/shard_map/all_to_all | solution.py:542
  33.5 1.2 %copy-start = (s32[32,8192]{1,0:T(8,128)S(1)}, s32[32,8192]{1,0:T(8,128)}, u32[]{:S(2)}) copy-start(s32[32,8192]{1,0:T(8,128)} %param.16) | copy-start | bytes 3145732
  33.9 4.9 %collective-permute-start.9 = (bf16[16,2,100,128]{3,0,2,1:T(8,128)(2,1)S(1)}, bf16[16,2,100,128]{3,0,2,1:T(8,128)(2,1)}, u32[]{:S(2)}, u32[]{:S(2)}) collective-permute-start(bf16[16,2,100,128]{3,0,2,1:T(8,128)(2,1)S(1)} %bitcast.28), channel_id=1, source_target_pairs={{0,1},{1,0},{2,3},{3,2},{4,5},{5,4},{6,7},{7,6},{8,9},{9,8},{10,11... | collective-permute-start | bytes 2457608 | tf_op jit(solution)/shard_map/ppermute | solution.py:489
  110.7 6.3 %collective-permute-start.10 = (bf16[401,32,128]{2,1,0:T(8,128)(2,1)}, bf16[401,32,128]{2,1,0:T(8,128)(2,1)}, u32[]{:S(2)}, u32[]{:S(2)}) collective-permute-start(bf16[401,32,128]{2,1,0:T(8,128)(2,1)} %get-tuple-element.16), channel_id=1, source_target_pairs={{0,1},{1,0},{2,3},{3,2},{4,5},{5,4},{6,7},{7,6},{8,9},{9,8},{10,11... | collective-permute-start | bytes 9854984 | tf_op jit(solution)/shard_map/ppermute | solution.py:559
